TPU v7x, 256 devices: a whole 4x4x8 slice. The times are simulated.
256 devices in a mesh: dp: 32 (over x_lo, z, core), mp: 8 (over y, x_hi).
Axes of the slice: x: 4 (x_hi: 2, x_lo: 2; x = x_hi * 2 + x_lo), y: 4, z: 8, core: 2. Of those that a mesh axis runs over, the one named last changes fastest.
Arguments:
- video_feats: bfloat16 [8192, 3200], P('dp'), may hold values from -18 to 18
- text_feats: bfloat16 [8192, 512], P('dp'), may hold values from -11 to 11
- weight_in: bfloat16 [3200, 6400], P(None, 'mp'), may hold values from -0.109375 to 0.109375
- weight_out: bfloat16 [6400, 512], P('mp'), may hold values from -0.07625 to 0.07625
- logit_scale: float32 [1], replicated, may hold values from 20 to 50
Outputs:
- loss: float32 [1], replicated
- grad_in: float32 [3200, 6400], P('dp', 'mp')
- grad_out: float32 [6400, 512], P('mp', 'dp')
All inputs are finite; a program needn't handle non-finite values.
Results may differ from a plain program's by a relative error of at most 0.015.
Values may be sent and summed in bfloat16 or wider, within the bound.
No kernel may reach another device: no remote copies, remote signals or barrier semaphores. Data moves between devices by JAX's collectives and lax.ppermute only.
A program may use at most 128 MiB of HBM per device.

v0:
```python
import jax
import jax.numpy as jnp
from jax import lax
from jax.sharding import PartitionSpec as P

EPS = 1e-06
GELU_C = 0.7978845608
GELU_K = 0.044715


def gelu_parts(values):
    inner = GELU_C * (values + GELU_K * values * values * values)
    tanh_val = jnp.tanh(inner)
    gelu_val = 0.5 * values * (1.0 + tanh_val)
    gelu_der = 0.5 * (1.0 + tanh_val) + 0.5 * values * (1.0 - tanh_val * tanh_val) * GELU_C * (
        1.0 + 3.0 * GELU_K * values * values
    )
    return (gelu_val, gelu_der)


def on_device(video_feats, text_feats, weight_in, weight_out, logit_scale):
    tok_rows = video_feats.shape[0]
    dp_count = lax.axis_size("dp")
    mp_count = lax.axis_size("mp")
    mp_index = lax.axis_index("mp")
    batch_total = tok_rows * dp_count
    preact = jnp.dot(video_feats, weight_in, preferred_element_type=jnp.float32)
    gelu_val, gelu_der = gelu_parts(preact)
    hidden = gelu_val.astype(jnp.bfloat16)
    partial_value = jnp.dot(hidden, weight_out, preferred_element_type=jnp.float32)
    projected = lax.psum(partial_value, "mp")
    inv_norm = lax.rsqrt(jnp.sum(projected * projected, axis=-1, keepdims=True) + EPS)
    unit_emb = projected * inv_norm
    video_emb = unit_emb.astype(jnp.bfloat16)
    text_float = text_feats.astype(jnp.float32)
    text_emb = (
        text_float * lax.rsqrt(jnp.sum(text_float * text_float, axis=-1, keepdims=True) + EPS)
    ).astype(jnp.bfloat16)
    text_every = lax.all_gather(text_emb, "dp", axis=0, tiled=True)
    col_width = batch_total // mp_count
    text_cols = lax.dynamic_slice_in_dim(text_every, mp_index * col_width, col_width, 0)
    scale_val = logit_scale[0]
    logits = scale_val * lax.dot_general(
        video_emb, text_cols, (((1,), (1,)), ((), ())), preferred_element_type=jnp.float32
    )
    expo_vals = jnp.exp(logits)
    row_sum = lax.psum(jnp.sum(expo_vals, axis=1), "mp")
    col_sum = lax.psum(jnp.sum(expo_vals, axis=0), "dp")
    positive = scale_val * jnp.sum(
        video_emb.astype(jnp.float32) * text_emb.astype(jnp.float32), axis=-1
    )
    loss_piece = (jnp.sum(jnp.log(row_sum)) - 2.0 * jnp.sum(positive)) / mp_count + jnp.sum(
        jnp.log(col_sum)
    ) / dp_count
    loss = lax.psum(loss_piece, ("dp", "mp")) / (2.0 * batch_total)
    pair_weight = (expo_vals / row_sum[:, None] + expo_vals / col_sum[None, :]).astype(jnp.bfloat16)
    weighted_part = jnp.dot(pair_weight, text_cols, preferred_element_type=jnp.float32)
    weighted = lax.psum(weighted_part, "mp")
    grad_emb = 0.5 * scale_val * weighted - scale_val * text_emb.astype(jnp.float32)
    grad_proj = (
        inv_norm * (grad_emb - unit_emb * jnp.sum(unit_emb * grad_emb, axis=-1, keepdims=True))
    ).astype(jnp.bfloat16)
    grad_hidden = lax.dot_general(
        grad_proj, weight_out, (((1,), (1,)), ((), ())), preferred_element_type=jnp.float32
    )
    grad_pre = (grad_hidden * gelu_der).astype(jnp.bfloat16)
    out_term = lax.dot_general(
        hidden, grad_proj, (((0,), (0,)), ((), ())), preferred_element_type=jnp.float32
    )
    grad_out = lax.psum_scatter(out_term, "dp", scatter_dimension=1, tiled=True)
    whole_term = lax.dot_general(
        video_feats, grad_pre, (((0,), (0,)), ((), ())), preferred_element_type=jnp.float32
    )
    grad_in = lax.psum_scatter(whole_term, "dp", scatter_dimension=0, tiled=True)
    return (loss.reshape(1), grad_in, grad_out)


def solution(mesh):
    in_specs = (P("dp", None), P("dp", None), P(None, "mp"), P("mp", None), P())
    out_specs = (P(), P("dp", "mp"), P("mp", "dp"))
    return jax.shard_map(
        on_device, mesh=mesh, in_specs=in_specs, out_specs=out_specs, check_vma=False
    )
```

profile of v0, /device:TPU:1, one launch (start us, length us, event | category | flops | bytes accessed | tf_op | source)
XLA Modules:
  0.0 666.1 jit_solution(15935863508863412178)
XLA Ops:
  8.0 0.0 copy-start
  8.0 0.0 copy-start.3
  8.0 0.0 copy-start.2
  8.0 0.0 all-reduce.5.cloned.1.call-start
  8.1 1.4 copy-done
  9.4 4.0 fusion.39
  13.5 0.0 copy-done.3
  13.5 1.4 fusion.37
  14.9 0.0 all-reduce.5.cloned.1.call-update
  14.9 0.0 all-gather.2.cloned.1.call-start
  14.9 0.0 copy-done.2
  15.0 0.1 fusion.19
  15.1 0.8 fusion.20
  15.9 0.0 all-gather.2.cloned.1.call-update
  15.9 0.0 all-reduce.7.cloned.1.call-start
  16.6 93.6 %all-reduce.5.cloned.1.call-done = f32[256,512]{1,0:T(8,128)} async-done(((f32[256,512]{1,0:T(8,128)}), f32[256,512]{1,0:T(8,128)}) %all-reduce.5.cloned.1.call-update) | async-done | bytes 524304 | tf_op jit(solution)/shard_map/psum | solution.py:31
  110.2 1.2 multiply_reduce_fusion.1
  111.4 0.0 all-gather.2.cloned.1.call-done
  111.4 3.0 fusion.38
  114.4 0.0 copy-start.1
  114.4 59.1 %psum.37 = f32[1024]{0:T(1024)S(1)} all-reduce(f32[1024]{0:T(1024)S(1)} %get-tuple-element.9), channel_id=1, replica_groups=mesh['dp'=32,'mp'=8] {'dp'}, use_global_device_ids=true, to_apply=%region_9.0 | all-reduce | flops 1024 | bytes 8192 | tf_op jit(solution)/shard_map/psum | solution.py:48
  173.5 17.7 %psum.36 = f32[256]{0:T(256)S(1)} all-reduce(f32[256]{0:T(256)S(1)} %get-tuple-element.10), channel_id=1, replica_groups=mesh['dp'=32,'mp'=8] {'mp'}, use_global_device_ids=true, to_apply=%region_4.0 | all-reduce | flops 256 | bytes 2048 | tf_op jit(solution)/shard_map/psum | solution.py:47
  191.1 2.8 fusion.2
  194.0 0.0 all-reduce.7.cloned.1.call-update
  194.0 0.0 all-reduce.9.cloned.1.call-start
  194.0 81.8 %all-reduce.7.cloned.1.call-done = f32[256,512]{1,0:T(8,128)} async-done(((f32[256,512]{1,0:T(8,128)}), f32[256,512]{1,0:T(8,128)}) %all-reduce.7.cloned.1.call-update) | async-done | bytes 524304 | tf_op jit(solution)/shard_map/psum | solution.py:58
  275.8 0.0 copy-done.1
  275.8 1.4 multiply_reduce_fusion
  277.2 1.3 multiply_convert_fusion.1
  278.5 7.4 %convolution_bitcast_fusion = f32[3200,800]{0,1:T(8,128)} fusion(bf16[256,3200]{1,0:T(8,128)(2,1)S(1)} %copy-done, bf16[256,512]{1,0:T(8,128)(2,1)S(1)} %multiply_convert_fusion.1, bf16[800,512]{1,0:T(8,128)(2,1)} %param.8, f32[256,800]{0,1:T(8,128)S(1)} %fusion.39), kind=kOutput, calls=%fused_computation | convolution fusion | flops 1524326400 | bytes 13778944 | tf_op jit(solution)/shard_map/dot_general | solution.py:71
  285.9 0.0 copy-start.4
  285.9 0.0 all-reduce.9.cloned.1.call-update
  285.9 0.0 reduce-scatter.3.cloned.1.call-start
  286.0 1.8 fusion.36
  287.8 0.0 reduce-scatter.3.cloned.1.call-update
  287.8 0.0 copy-done.4
  287.8 0.6 dynamic-slice
  288.4 0.6 log_reduce_fusion
  289.7 0.6 log_reduce_fusion.1
  290.3 0.6 multiply_reduce_fusion.2
  292.8 80.4 %psum.38 = f32[]{:T(128)} all-reduce(f32[]{:T(128)S(6)} %add.57), channel_id=1, replica_groups=mesh['dp'=32,'mp'=8] {'dp','mp'}, use_global_device_ids=true, to_apply=%region_11.0 | all-reduce | flops 1 | bytes 8 | tf_op jit(solution)/shard_map/psum | solution.py:55
  373.9 167.2 %all-reduce.9.cloned.1.call-done = f32[3200,800]{0,1:T(8,128)} async-done(((f32[3200,800]{0,1:T(8,128)}), f32[3200,800]{0,1:T(8,128)}) %all-reduce.9.cloned.1.call-update) | async-done | bytes 10240016
  541.0 1.3 constant_dynamic-slice_fusion
  542.4 1.0 copy.9
  543.3 114.0 %reduce-scatter.3.cloned.1.call-done = f32[800,16]{0,1:T(8,128)} async-done(((f32[800,512]{0,1:T(8,128)}), f32[800,16]{0,1:T(8,128)}) %reduce-scatter.3.cloned.1.call-update) | async-done | bytes 51216 | tf_op jit(solution)/shard_map/reduce_scatter | solution.py:70
  (2 shorter events, 0.0 us)
Async XLA Ops:
  8.0 1.4 copy-start
  8.0 5.5 copy-start.3
  8.0 6.9 %copy-start.2 = (bf16[256,512]{1,0:T(8,128)(2,1)S(1)}, bf16[256,512]{1,0:T(8,128)(2,1)}, u32[]{:S(2)}) copy-start(bf16[256,512]{1,0:T(8,128)(2,1)} %param.6) | copy-start | bytes 786436
  8.0 102.2 %all-reduce.5.cloned.1.call-start = ((), (), s32[]{:S(2)}) async-start(), calls=%async_computation.1 | async-start | bytes 1048576 | tf_op jit(solution)/shard_map/psum | solution.py:31
  14.9 96.5 %all-gather.2.cloned.1.call-start = ((), (), s32[]{:S(2)}) async-start(), calls=%async_computation.2 | async-start | bytes 8650752 | tf_op jit(solution)/shard_map/all_gather | solution.py:39
  15.9 259.9 %all-reduce.7.cloned.1.call-start = ((), (), s32[]{:S(2)}) async-start(), calls=%async_computation.3 | async-start | bytes 1048576 | tf_op jit(solution)/shard_map/psum | solution.py:58
  114.4 161.4 %copy-start.1 = (f32[256,512]{1,0:T(8,128)S(1)}, f32[256,512]{1,0:T(8,128)}, u32[]{:S(2)}) copy-start(f32[256,512]{1,0:T(8,128)} %all-reduce.5.cloned.1.call-done) | copy-start | bytes 1572868
  194.0 347.1 %all-reduce.9.cloned.1.call-start = ((), (), s32[]{:S(2)}) async-start(), calls=%async_computation.5 | async-start | bytes 20480000
  285.9 1.9 copy-start.4
  285.9 371.4 %reduce-scatter.3.cloned.1.call-start = ((), (), s32[]{:S(2)}) async-start(), calls=%async_computation.4 | async-start | bytes 1892352 | tf_op jit(solution)/shard_map/reduce_scatter | solution.py:70
Sparse Core Ops, SparseCore 0:
  15.0 95.1 all-reduce.4
  194.1 81.6 all-reduce.6
Sparse Core Ops, SparseCore 1:
  17.8 77.7 all-gather.1
  286.0 255.0 all-reduce.8
  544.0 113.3 reduce-scatter.2
where the time goes:
time: 670 us; the launch traced here: 666 us
  waiting for transfers between devices  457 us (68%)
  blocking collectives  157 us (23%)
  between operations  20.8 us (3%)
  matrix products  20.4 us (3%)
    unnamed x6, waiting for transfers between devices  167 us
    reduce_scatter x1, waiting for transfers between devices, on_device(): grad_out = lax.psum_scatter(out_term, 'dp', scatter_dimension=1, tiled=True)  114 us
    psum x1, waiting for transfers between devices, on_device(): projected = lax.psum(partial_value, 'mp')  93.6 us
    psum x1, waiting for transfers between devices, on_device(): weighted = lax.psum(weighted_part, 'mp')  81.8 us
    psum x1, blocking collectives, on_device(): loss = lax.psum(loss_piece, ('dp', 'mp')) / (2.0 * batch_total)  80.4 us
    psum x1, blocking collectives, on_device(): col_sum = lax.psum(jnp.sum(expo_vals, axis=0), 'dp')  59.1 us
    psum x1, blocking collectives, on_device(): row_sum = lax.psum(jnp.sum(expo_vals, axis=1), 'mp')  17.7 us
  transfers between devices with their start and end apart: 5, of which 4 were waited for; matrix products, arithmetic and copies ran while one was open for 1% of the time, Pallas kernels for 0%

commit v1 on v0

v1 whole, which is shorter than its diff:
```python
import jax
import jax.numpy as jnp
from jax import lax
from jax.sharding import Mesh, PartitionSpec as P

EPS = 1e-06
GELU_C = 0.7978845608
GELU_K = 0.044715
MP = ("y", "x_hi")
DP = ("x_lo", "z", "core")
PLANE = ("core", "x_lo", "y", "x_hi")
BF = jnp.bfloat16
F32 = jnp.float32


def gelu_val(values, tanh_val):
    return 0.5 * values * (1.0 + tanh_val)


def gelu_der(values, tanh_val):
    return 0.5 * (1.0 + tanh_val) + 0.5 * values * (1.0 - tanh_val * tanh_val) * GELU_C * (
        1.0 + 3.0 * GELU_K * values * values
    )


def gelu_tanh(values):
    return jnp.tanh(GELU_C * (values + GELU_K * values * values * values))


def swap(value, axis):
    return lax.ppermute(value, axis, [(0, 1), (1, 0)])


def ordered(own, other, index):
    return jnp.where(index == 0, jnp.stack([own, other]), jnp.stack([other, own]))


def exchange(value, axis):
    return lax.all_to_all(value, axis, 0, 0)


def spread(value, axis):
    count = lax.axis_size(axis)
    return exchange(jnp.broadcast_to(value[None], (count,) + value.shape), axis)


def split3(value):
    first = value.astype(BF).astype(F32)
    second = (value - first).astype(BF).astype(F32)
    third = value - first - second
    return first, second, third


def on_device(video_feats, text_feats, weight_in, weight_out, logit_scale):
    rows = video_feats.shape[0]
    d_in = video_feats.shape[1]
    hid = weight_in.shape[1]
    emb = text_feats.shape[1]
    mp_count = lax.axis_size(MP)
    z_count = lax.axis_size("z")
    own_rows = rows // mp_count
    mp_index = lax.axis_index(MP)
    x_index = lax.axis_index("x_lo")
    c_index = lax.axis_index("core")
    batch_total = rows * lax.axis_size(DP)
    scale_val = logit_scale[0]

    text_float = text_feats.astype(F32)
    text_emb = (
        text_float * lax.rsqrt(jnp.sum(text_float * text_float, axis=-1, keepdims=True) + EPS)
    ).astype(BF)
    pair = ordered(text_emb, swap(text_emb, "x_lo"), x_index)
    text_cols = ordered(pair, swap(pair, "core"), c_index).reshape(4 * rows, emb)

    in_rows = d_in // lax.axis_size(DP)
    feats_t = video_feats.T.reshape(2, z_count, 2, in_rows, rows).transpose(2, 0, 1, 3, 4)
    keep = lax.dynamic_index_in_dim(feats_t, c_index, 0, False)
    give = lax.dynamic_index_in_dim(feats_t, 1 - c_index, 0, False)
    feats_c = ordered(keep, swap(give, "core"), c_index)
    keep = lax.dynamic_index_in_dim(feats_c, x_index, 1, False)
    give = lax.dynamic_index_in_dim(feats_c, 1 - x_index, 1, False)
    feats_q = ordered(keep, swap(give, "x_lo"), x_index)

    preact = jnp.dot(video_feats, weight_in, preferred_element_type=F32)
    hidden = gelu_val(preact, gelu_tanh(preact)).astype(BF)
    partial_value = jnp.dot(hidden, weight_out, preferred_element_type=F32).astype(BF)
    pre_bf = preact.astype(BF)
    pre_pair = ordered(pre_bf, swap(pre_bf, "x_lo"), x_index)
    pre_all = ordered(pre_pair, swap(pre_pair, "core"), c_index).reshape(4 * rows, hid)

    got = exchange(partial_value.reshape(mp_count, own_rows, emb), MP)
    projected = jnp.sum(got.astype(F32), axis=0)
    inv_norm = lax.rsqrt(jnp.sum(projected * projected, axis=-1, keepdims=True) + EPS)
    unit_emb = projected * inv_norm
    video_emb = unit_emb.astype(BF)
    video_rows = spread(video_emb, "z").reshape(z_count * own_rows, emb)

    logits = scale_val * lax.dot_general(
        video_rows, text_cols, (((1,), (1,)), ((), ())), preferred_element_type=F32
    )
    expo = jnp.exp(logits)
    row_part = jnp.sum(expo, axis=1)
    col_part = jnp.sum(expo, axis=0)
    col_sum = jnp.sum(spread(col_part.reshape(-1, 128), PLANE), axis=0).reshape(-1)
    first = jnp.dot(expo.astype(BF), text_cols, preferred_element_type=F32)
    second = jnp.dot(
        (expo / col_sum[None, :]).astype(BF), text_cols, preferred_element_type=F32
    )
    row_hi = row_part.astype(BF).astype(F32)
    row_lo = row_part - row_hi
    lane = lax.broadcasted_iota(jnp.int32, (1, 128), 1)
    row_lanes = jnp.where(lane < 64, row_hi[:, None], row_lo[:, None])
    packed = jnp.concatenate([first, second, row_lanes], axis=1).astype(BF)
    back = exchange(packed.reshape(z_count, own_rows, 2 * emb + 128), "z")
    back = jnp.sum(back.astype(F32), axis=0)
    row_sum = back[:, 2 * emb : 2 * emb + 1] + back[:, 2 * emb + 64 : 2 * emb + 65]
    weighted = back[:, :emb] / row_sum + back[:, emb : 2 * emb]

    text_own = lax.dynamic_slice_in_dim(text_emb, mp_index * own_rows, own_rows, 0).astype(F32)
    positive = scale_val * jnp.sum(video_emb.astype(F32) * text_own, axis=-1)
    loss_piece = (
        jnp.sum(jnp.log(row_sum))
        - 2.0 * jnp.sum(positive)
        + jnp.sum(jnp.log(col_sum)) / lax.axis_size(PLANE)
    )

    grad_emb = 0.5 * scale_val * weighted - scale_val * text_own
    grad_proj = inv_norm * (
        grad_emb - unit_emb * jnp.sum(unit_emb * grad_emb, axis=-1, keepdims=True)
    )
    a, b, c = split3(loss_piece)
    lane = lax.broadcasted_iota(jnp.int32, (1, emb), 1)
    loss_row = jnp.where(lane == 0, a, jnp.where(lane == 1, b, jnp.where(lane == 2, c, 0.0)))
    sent = jnp.concatenate([grad_proj, loss_row], axis=0).astype(BF)
    grads = spread(sent, PLANE)
    loss_piece = jnp.sum(grads[:, own_rows, :].astype(F32))
    gproj = grads[:, :own_rows, :].reshape(4 * rows, emb)

    pre_f = pre_all.astype(F32)
    tanh_all = gelu_tanh(pre_f)
    hidden_all = gelu_val(pre_f, tanh_all).astype(BF)
    grad_hidden = lax.dot_general(
        gproj, weight_out, (((1,), (1,)), ((), ())), preferred_element_type=F32
    )
    grad_pre = (grad_hidden * gelu_der(pre_f, tanh_all)).astype(BF)
    out_term = lax.dot_general(gproj, hidden_all, (((0,), (0,)), ((), ())), preferred_element_type=F32)
    out_cols = emb // lax.axis_size(DP)
    out_term = out_term.reshape(2, z_count, 2, out_cols, hid)
    out_term = lax.dynamic_index_in_dim(out_term, x_index, 0, False)
    out_term = lax.dynamic_index_in_dim(out_term, c_index, 1, False)
    grad_pre4 = grad_pre.reshape(2, 2, rows, hid)
    in_term = 0.0
    for core in range(2):
        for x in range(2):
            in_term = in_term + jnp.dot(
                feats_q[x, core].reshape(z_count * in_rows, rows),
                grad_pre4[core, x],
                preferred_element_type=F32,
            )
    a, b, c = split3(loss_piece)
    lane = lax.broadcasted_iota(jnp.int32, (1, 1, hid), 2)
    loss_row = jnp.where(lane == 0, a, jnp.where(lane == 1, b, jnp.where(lane == 2, c, 0.0)))
    loss_row = jnp.broadcast_to(loss_row, (z_count, 1, hid))
    packed = jnp.concatenate(
        [out_term.astype(BF), in_term.reshape(z_count, in_rows, hid).astype(BF), loss_row.astype(BF)],
        axis=1,
    )
    final = jnp.sum(exchange(packed, "z").astype(F32), axis=0)
    grad_out = final[:out_cols].T
    grad_in = final[out_cols : out_cols + in_rows]
    loss = jnp.sum(final[out_cols + in_rows, :3]) / (2.0 * batch_total)
    return (loss.reshape(1), grad_in, grad_out)


def solution(mesh):
    fine = Mesh(mesh.devices.reshape(2, -1, 2, mesh.devices.shape[1] // 2, 2), DP + MP)
    in_specs = (P(DP, None), P(DP, None), P(None, MP), P(MP, None), P())
    out_specs = (P(), P(DP, MP), P(MP, DP))
    return jax.shard_map(
        on_device, mesh=fine, in_specs=in_specs, out_specs=out_specs, check_vma=False
    )
```

time: 670 us -> 206 us (0.31)
  waiting for transfers between devices: 457 us -> 29.6 us
  blocking collectives: 157 us -> 46.9 us
  local copies, waits for them, and re-layouts: 4.26 us -> 43.5 us
  starting transfers between devices: 0.21 us -> 35.5 us
  other arithmetic: 6.59 us -> 23.9 us
  between operations: 20.8 us -> 6.79 us
    psum x2 -> x0, waiting for transfers between devices: 175 us -> none  [the longest x1 93.6 us: on_device(): projected = lax.psum(partial_value, 'mp')]
    unnamed x6 -> x0, waiting for transfers between devices: 167 us -> none
    psum x3 -> x0, blocking collectives: 157 us -> none  [the longest x1 80.4 us: on_device(): loss = lax.psum(loss_piece, ('dp', 'mp')) / (2.0 * batch_total)]
    reduce_scatter x1 -> x0, waiting for transfers between devices: 114 us -> none  [on_device(): grad_out = lax.psum_scatter(out_term, 'dp', scatter_dimension=1, tiled=True)]
    all_to_all x0 -> x1, blocking collectives: none -> 46.9 us  [exchange(): return lax.all_to_all(value, axis, 0, 0)]
    all_to_all x0 -> x5, starting transfers between devices: none -> 29.5 us  [exchange(): return lax.all_to_all(value, axis, 0, 0)]
    all_to_all x0 -> x5, waiting for transfers between devices: none -> 18.8 us  [exchange(): return lax.all_to_all(value, axis, 0, 0)]
    convert_element_type x0 -> x6, local copies, waits for them, and re-layouts: none -> 15 us  [the longest x2 9.89 us: on_device(): pre_f = pre_all.astype(F32)]
  transfers between devices with their start and end apart: 5 -> 11, of which waited for: 4 -> 4; matrix products, arithmetic and copies ran while one was open for 1% -> 26% of each run, Pallas kernels for 0% -> 0%
where the time goes in v1:
time: 206 us; the launch traced here: 205 us
  blocking collectives  46.9 us (23%)
  local copies, waits for them, and re-layouts  43.5 us (21%)
  starting transfers between devices  35.5 us (17%)
  waiting for transfers between devices  29.6 us (14%)
  other arithmetic  23.9 us (12%)
  matrix products  18.4 us (9%)
  between operations  6.79 us (3%)
    all_to_all x1, blocking collectives, exchange(): return lax.all_to_all(value, axis, 0, 0)  46.9 us
    all_to_all x5, starting transfers between devices, exchange(): return lax.all_to_all(value, axis, 0, 0)  29.5 us
    all_to_all x5, waiting for transfers between devices, exchange(): return lax.all_to_all(value, axis, 0, 0)  18.8 us
    ppermute x6, waiting for transfers between devices, swap(): return lax.ppermute(value, axis, [(0, 1), (1, 0)])  10.8 us
    convert_element_type x2, local copies, waits for them, and re-layouts, on_device(): pre_f = pre_all.astype(F32)  9.89 us
    select_n x7, other arithmetic, ordered(): jnp.where(index == 0, jnp.stack([own, other]), jnp.stack([other, own]))  9.71 us
    ppermute x6, starting transfers between devices, swap(): return lax.ppermute(value, axis, [(0, 1), (1, 0)])  6.04 us
    dot_general x1, matrix products, on_device(): preact = jnp.dot(video_feats, weight_in, preferred_element_type=F32)  5.29 us
  transfers between devices with their start and end apart: 11, of which 4 were waited for; matrix products, arithmetic and copies ran while one was open for 26% of the time, Pallas kernels for 0%

profile of v1, /device:TPU:1, one launch (start us, length us, event | category | flops | bytes accessed | tf_op | source)
XLA Modules:
  0.0 204.7 jit_solution(16546070864769867615)
XLA Ops:
  0.6 1.2 fusion.21
  1.8 1.8 fusion.22
  3.6 2.0 collective-permute-start
  5.6 5.3 %fusion.47 = (bf16[256,800]{0,1:T(8,128)(2,1)}, f32[256,800]{0,1:T(8,128)S(1)}) fusion(bf16[256,3200]{1,0:T(8,128)(2,1)} %param.5, bf16[3200,800]{0,1:T(8,128)(2,1)} %param.7), kind=kOutput, calls=%fused_computation.110 | convolution fusion | flops 1310924800 | bytes 7987200 | tf_op jit(solution)/shard_map/dot_general | solution.py:84
  10.9 1.3 convolution_convert_fusion.2
  12.2 6.3 %all-to-all-start = ((bf16[8,32,512]{2,1,0:T(8,128)(2,1)}), bf16[8,32,512]{2,1,0:T(8,128)(2,1)S(1)}, u32[]{:S(2)}, u32[]{:S(2)}) async-start(bf16[8,32,512]{2,1,0:T(8,128)(2,1)} %bitcast), calls=%async_computation | async-start | bytes 524288 | tf_op jit(solution)/shard_map/all_to_all | solution.py:39
  18.5 2.3 %copy.67 = bf16[3200,256]{1,0:T(8,128)(2,1)} copy(bf16[3200,256]{0,1:T(8,128)(2,1)S(1)} %bitcast.96) | data formatting | bytes 3276800 | tf_op jit(solution)/shard_map/transpose | solution.py:76
  20.8 2.3 %reshape.334 = bf16[2,8,2,100,256]{4,3,2,1,0:T(8,128)(2,1)S(1)} reshape(bf16[3200,256]{1,0:T(8,128)(2,1)} %copy.67) | data formatting | bytes 3276800 | tf_op jit(solution)/shard_map/reshape | solution.py:76
  23.1 1.0 constant_dynamic-slice_fusion.1
  24.1 1.1 copy.97
  25.2 1.2 collective-permute-start.4
  27.4 1.1 maximum_select_fusion.7
  28.5 1.4 collective-permute-start.1
  30.0 0.7 broadcast_in_dim.83
  30.7 8.2 %all-to-all-start.1 = ((bf16[8,32,512]{2,1,0:T(8,128)(2,1)}), bf16[8,32,512]{2,1,0:T(8,128)(2,1)S(1)}, u32[]{:S(2)}, u32[]{:S(2)}) async-start(bf16[8,32,512]{2,1,0:T(8,128)(2,1)} %broadcast_in_dim.83), calls=%async_computation.1 | async-start | bytes 524288 | tf_op jit(solution)/shard_map/all_to_all | solution.py:39
  39.0 1.1 maximum_select_fusion.6
  40.3 10.9 %all-to-all-done.1 = bf16[8,32,512]{2,1,0:T(8,128)(2,1)S(1)} async-done(((bf16[8,32,512]{2,1,0:T(8,128)(2,1)}), bf16[8,32,512]{2,1,0:T(8,128)(2,1)S(1)}, u32[]{:S(2)}, u32[]{:S(2)}) %all-to-all-start.1) | async-done | bytes 262176 | tf_op jit(solution)/shard_map/all_to_all | solution.py:39
  51.3 0.6 fusion.43
  52.0 0.7 broadcast_in_dim.85
  52.6 6.5 %all-to-all-start.2 = ((f32[32,8,128]{2,1,0:T(8,128)}), f32[32,8,128]{2,1,0:T(8,128)S(1)}, u32[]{:S(2)}, u32[]{:S(2)}) async-start(f32[32,8,128]{2,1,0:T(8,128)} %broadcast_in_dim.85), calls=%async_computation.2 | async-start | bytes 262144 | tf_op jit(solution)/shard_map/all_to_all | solution.py:39
  59.3 7.5 %all-to-all-done.2 = f32[32,8,128]{2,1,0:T(8,128)S(1)} async-done(((f32[32,8,128]{2,1,0:T(8,128)}), f32[32,8,128]{2,1,0:T(8,128)S(1)}, u32[]{:S(2)}, u32[]{:S(2)}) %all-to-all-start.2) | async-done | bytes 131104 | tf_op jit(solution)/shard_map/all_to_all | solution.py:39
  67.0 0.4 convolution_convert_fusion.1
  67.8 0.9 pad_maximum_fusion.1
  68.7 3.5 %all-to-all-start.3 = ((bf16[8,32,1152]{2,1,0:T(8,128)(2,1)}), bf16[8,32,1152]{2,1,0:T(8,128)(2,1)S(1)}, u32[]{:S(2)}, u32[]{:S(2)}) async-start(bf16[8,32,1152]{2,1,0:T(8,128)(2,1)} %pad_maximum_fusion.1), calls=%async_computation.3 | async-start | bytes 1179648 | tf_op jit(solution)/shard_map/all_to_all | solution.py:39
  72.6 10.8 %collective-permute-done.2 = bf16[256,800]{0,1:T(8,128)(2,1)} collective-permute-done((bf16[256,800]{0,1:T(8,128)(2,1)}, bf16[256,800]{0,1:T(8,128)(2,1)}, u32[]{:S(2)}, u32[]{:S(2)}) %collective-permute-start.2) | collective-permute-done | bytes 409632 | tf_op jit(solution)/shard_map/ppermute | solution.py:31
  83.3 2.4 %maximum_select_fusion.5 = bf16[2,256,800]{1,2,0:T(8,128)(2,1)} fusion(bf16[1,256,800]{1,2,0:T(8,128)(2,1)} %bitcast.21, bf16[1,256,800]{1,2,0:T(8,128)(2,1)} %bitcast.20, pred[]{:T(512)S(6)} %eq.98), kind=kLoop, calls=%fused_computation.39 | loop fusion | flops 1228800 | bytes 1638401 | tf_op jit(solution)/shard_map/jit(_where)/select_n | solution.py:35
  85.8 1.2 collective-permute-start.3
  87.0 1.6 maximum_select_fusion.1
  88.6 1.3 dynamic-slice_bitcast_fusion.1
  89.9 0.6 log_reduce_fusion.1
  91.7 0.7 fusion.36
  92.4 1.0 multiply_reduce_fusion
  93.3 0.6 multiply_reduce_fusion.2
  95.2 0.9 multiply_convert_fusion
  96.1 1.1 broadcast_in_dim.93
  97.3 4.9 %all-to-all-start.4 = ((bf16[32,33,512]{2,1,0:T(8,128)(2,1)}), bf16[32,33,512]{2,1,0:T(8,128)(2,1)}, u32[]{:S(2)}, u32[]{:S(2)}) async-start(bf16[32,33,512]{2,1,0:T(8,128)(2,1)} %broadcast_in_dim.93), calls=%async_computation.4 | async-start | bytes 2621440 | tf_op jit(solution)/shard_map/all_to_all | solution.py:39
  102.2 1.6 maximum_select_fusion.4
  103.7 0.9 copy-done.4
  104.6 1.3 fusion.4
  105.9 1.7 copy.66
  107.6 2.1 %reshape.339 = bf16[1024,800,1,1,1]{0,1,2,3,4:T(8,128)(2,1)} reshape(bf16[2,2,256,800]{2,1,0,3:T(2,128)(2,1)S(1)} %copy.66) | data formatting | bytes 3276800 | tf_op jit(solution)/shard_map/convert_element_type | solution.py:141
  109.7 1.7 fusion.12
  111.3 4.2 %copy.71 = f32[2,2,256,800]{2,1,0,3:T(2,128)} copy(f32[2,2,256,800]{2,3,1,0:T(8,128)S(1)} %fusion.12) | data formatting | bytes 6553600 | tf_op jit(solution)/shard_map/convert_element_type | solution.py:139
  115.6 5.7 %reshape.337 = f32[1024,800]{0,1:T(8,128)} reshape(f32[2,2,256,800]{2,1,0,3:T(2,128)} %copy.71) | data formatting | bytes 6553600 | tf_op jit(solution)/shard_map/convert_element_type | solution.py:139
  121.3 1.7 maximum_select_fusion.2
  123.1 0.8 reshape_squeeze.15
  124.4 0.8 reshape_squeeze.12
  125.2 1.7 fusion.34
  128.2 1.3 slice.72
  129.6 1.4 copy.65
  130.9 5.1 %fusion.11 = bf16[1024,800]{0,1:T(8,128)(2,1)} fusion(f32[1024,800]{0,1:T(8,128)} %reshape.337, bf16[1024,512]{1,0:T(8,128)(2,1)S(1)} %bitcast.90, bf16[800,512]{1,0:T(8,128)(2,1)S(1)} %copy-done), kind=kOutput, calls=%fused_computation.14 | convolution fusion | flops 854425600 | bytes 6782976 | tf_op jit(solution)/shard_map/dot_general | solution.py:142
  136.0 4.2 %reshape.335 = bf16[2,2,256,800]{2,1,0,3:T(2,128)(2,1)S(1)} reshape(bf16[1024,800]{0,1:T(8,128)(2,1)} %fusion.11) | data formatting | bytes 3276800 | tf_op jit(solution)/shard_map/reshape | solution.py:151
  140.2 2.5 %fusion.44 = (bf16[1,1,256,800]{2,1,0,3:T(2,128)(2,1)S(1)}, bf16[1,1,256,800]{2,1,0,3:T(2,128)(2,1)S(1)}, bf16[1,1,256,800]{2,1,0,3:T(2,128)(2,1)S(1)}, bf16[1,1,256,800]{2,1,0,3:T(2,128)(2,1)S(1)}) fusion(bf16[2,2,256,800]{2,1,0,3:T(2,128)(2,1)S(1)} %reshape.335), kind=kLoop, calls=%fused_computation.107 | loop fusion | bytes 3276800 | tf_op jit(solution)/shard_map/slice | solution.py:157
  142.8 0.6 fusion.24
  143.4 0.6 fusion.25
  144.4 0.6 fusion.26
  145.4 0.6 add_convert_fusion
  146.1 1.3 convert_element_type.180
  147.6 2.8 %fusion.13 = bf16[2,8,2,16,800]{4,3,2,1,0:T(8,128)(2,1)S(1)} fusion(bf16[2,8,2,16,1024]{4,3,2,1,0:T(8,128)(2,1)S(1)} %bitcast.97, bf16[1024,800,1,1,1]{0,1,2,3,4:T(8,128)(2,1)} %reshape.339), kind=kOutput, calls=%fused_computation.22 | convolution fusion | flops 838860800 | bytes 3506176 | tf_op jit(solution)/shard_map/dot_general | solution.py:146
  150.7 2.4 %copy.79 = bf16[8,117,800]{1,2,0:T(8,128)(2,1)} copy(bf16[8,117,800]{2,1,0:T(8,128)(2,1)S(1)} %pad_maximum_fusion) | data formatting | bytes 2995200 | tf_op jit(solution)/shard_map/concatenate | solution.py:164
  153.1 46.9 %all_to_all.30 = bf16[8,117,800]{1,2,0:T(8,128)(2,1)S(1)} all-to-all(bf16[8,117,800]{1,2,0:T(8,128)(2,1)} %copy.79), channel_id=1, replica_groups=mesh['x_lo'=2,'z'=8,'core'=2,'y'=4,'x_hi'=2] {'z'}, dimensions={0} | all-to-all | bytes 2995200 | tf_op jit(solution)/shard_map/all_to_all | solution.py:39
  200.3 0.7 slice_reduce_fusion
  201.2 0.8 copy.81
  202.0 0.9 copy.80
  (63 shorter events, 4.6 us)
Async XLA Ops:
  0.6 10.3 %copy-start = (bf16[800,512]{1,0:T(8,128)(2,1)S(1)}, bf16[800,512]{1,0:T(8,128)(2,1)}, u32[]{:S(2)}) copy-start(bf16[800,512]{1,0:T(8,128)(2,1)} %param.8) | copy-start | bytes 2457604
  3.6 23.8 %collective-permute-start = (bf16[256,512]{1,0:T(8,128)(2,1)}, bf16[256,512]{1,0:T(8,128)(2,1)}, u32[]{:S(2)}, u32[]{:S(2)}) collective-permute-start(bf16[256,512]{1,0:T(8,128)(2,1)} %fusion.22), channel_id=1, source_target_pairs={{0,128},{128,0},{1,129},{129,1},{2,130},{130,2},{3,131},{131,3},{4... | collective-permute-start | bytes 786440 | tf_op jit(solution)/shard_map/ppermute | solution.py:31
  10.9 7.6 %copy-start.7 = (bf16[256,3200]{1,0:T(8,128)(2,1)S(1)}, bf16[256,3200]{1,0:T(8,128)(2,1)}, u32[]{:S(2)}) copy-start(bf16[256,3200]{1,0:T(8,128)(2,1)} %param.5) | copy-start | bytes 4915204
  12.2 15.1 %all-to-all-start = ((bf16[8,32,512]{2,1,0:T(8,128)(2,1)}), bf16[8,32,512]{2,1,0:T(8,128)(2,1)S(1)}, u32[]{:S(2)}, u32[]{:S(2)}) async-start(bf16[8,32,512]{2,1,0:T(8,128)(2,1)} %bitcast), calls=%async_computation | async-start | bytes 524288 | tf_op jit(solution)/shard_map/all_to_all | solution.py:39
  23.1 4.0 %copy-start.2 = (bf16[256,512]{1,0:T(8,128)(2,1)S(1)}, bf16[256,512]{1,0:T(8,128)(2,1)}, u32[]{:S(2)}) copy-start(bf16[256,512]{1,0:T(8,128)(2,1)} %param.6) | copy-start | bytes 786436
  25.2 61.8 %collective-permute-start.4 = (bf16[2,8,100,256]{3,1,2,0:T(8,128)(2,1)}, bf16[2,8,100,256]{3,1,2,0:T(8,128)(2,1)}, u32[]{:S(2)}, u32[]{:S(2)}) collective-permute-start(bf16[2,8,100,256]{3,1,2,0:T(8,128)(2,1)} %bitcast.79), channel_id=1, source_target_pairs={{0,8},{8,0},{1,9},{9,1},{2,10},{10,2},{3,11},{11,3},{4,12},{12,4},... | collective-permute-start | bytes 2457608 | tf_op jit(solution)/shard_map/ppermute | solution.py:31
  28.5 11.6 %collective-permute-start.1 = (bf16[2,256,512]{2,1,0:T(8,128)(2,1)S(1)}, bf16[2,256,512]{2,1,0:T(8,128)(2,1)S(1)}, u32[]{:S(2)}, u32[]{:S(2)}) collective-permute-start(bf16[2,256,512]{2,1,0:T(8,128)(2,1)S(1)} %maximum_select_fusion.7), channel_id=1, source_target_pairs={{0,8},{8,0},{1,9},{9,1},{2,10},{10,2},{3,11},{11,3},{4,12},{12,4},... | collective-permute-start | bytes 1572872 | tf_op jit(solution)/shard_map/ppermute | solution.py:31
  30.7 20.6 %all-to-all-start.1 = ((bf16[8,32,512]{2,1,0:T(8,128)(2,1)}), bf16[8,32,512]{2,1,0:T(8,128)(2,1)S(1)}, u32[]{:S(2)}, u32[]{:S(2)}) async-start(bf16[8,32,512]{2,1,0:T(8,128)(2,1)} %broadcast_in_dim.83), calls=%async_computation.1 | async-start | bytes 524288 | tf_op jit(solution)/shard_map/all_to_all | solution.py:39
  52.6 14.1 %all-to-all-start.2 = ((f32[32,8,128]{2,1,0:T(8,128)}), f32[32,8,128]{2,1,0:T(8,128)S(1)}, u32[]{:S(2)}, u32[]{:S(2)}) async-start(f32[32,8,128]{2,1,0:T(8,128)} %broadcast_in_dim.85), calls=%async_computation.2 | async-start | bytes 262144 | tf_op jit(solution)/shard_map/all_to_all | solution.py:39
  67.4 5.0 %copy-start.3 = (bf16[2,8,1,100,256]{4,3,2,1,0:T(8,128)(2,1)S(1)}, bf16[2,8,1,100,256]{4,3,2,1,0:T(8,128)(2,1)}, u32[]{:S(2)}) copy-start(bf16[2,8,1,100,256]{4,3,2,1,0:T(8,128)(2,1)} %get-tuple-element.15) | copy-start | bytes 2457604
  68.7 22.9 %all-to-all-start.3 = ((bf16[8,32,1152]{2,1,0:T(8,128)(2,1)}), bf16[8,32,1152]{2,1,0:T(8,128)(2,1)S(1)}, u32[]{:S(2)}, u32[]{:S(2)}) async-start(bf16[8,32,1152]{2,1,0:T(8,128)(2,1)} %pad_maximum_fusion.1), calls=%async_computation.3 | async-start | bytes 1179648 | tf_op jit(solution)/shard_map/all_to_all | solution.py:39
  72.3 11.0 %collective-permute-start.2 = (bf16[256,800]{0,1:T(8,128)(2,1)}, bf16[256,800]{0,1:T(8,128)(2,1)}, u32[]{:S(2)}, u32[]{:S(2)}) collective-permute-start(bf16[256,800]{0,1:T(8,128)(2,1)} %get-tuple-element.30), channel_id=1, source_target_pairs={{0,128},{128,0},{1,129},{129,1},{2,130},{130,2},{3,131},{131,3},{4... | collective-permute-start | bytes 1228808 | tf_op jit(solution)/shard_map/ppermute | solution.py:31
  85.8 18.0 %collective-permute-start.3 = (bf16[2,256,800]{1,2,0:T(8,128)(2,1)}, bf16[2,256,800]{1,2,0:T(8,128)(2,1)S(1)}, u32[]{:S(2)}, u32[]{:S(2)}) collective-permute-start(bf16[2,256,800]{1,2,0:T(8,128)(2,1)} %maximum_select_fusion.5), channel_id=1, source_target_pairs={{0,8},{8,0},{1,9},{9,1},{2,10},{10,2},{3,11},{11,3},{4,12},{12,4},... | collective-permute-start | bytes 2457608 | tf_op jit(solution)/shard_map/ppermute | solution.py:31
  89.9 31.4 %collective-permute-start.5 = (bf16[2,8,100,256]{3,1,2,0:T(8,128)(2,1)}, bf16[2,8,100,256]{3,1,2,0:T(8,128)(2,1)}, u32[]{:S(2)}, u32[]{:S(2)}) collective-permute-start(bf16[2,8,100,256]{3,1,2,0:T(8,128)(2,1)} %get-tuple-element.26), channel_id=1, source_target_pairs={{0,128},{128,0},{1,129},{129,1},{2,130},{130,2},{3,131},{131,3},{4... | collective-permute-start | bytes 2457608 | tf_op jit(solution)/shard_map/ppermute | solution.py:31
  97.3 27.9 %all-to-all-start.4 = ((bf16[32,33,512]{2,1,0:T(8,128)(2,1)}), bf16[32,33,512]{2,1,0:T(8,128)(2,1)}, u32[]{:S(2)}, u32[]{:S(2)}) async-start(bf16[32,33,512]{2,1,0:T(8,128)(2,1)} %broadcast_in_dim.93), calls=%async_computation.4 | async-start | bytes 2621440 | tf_op jit(solution)/shard_map/all_to_all | solution.py:39
  103.7 0.9 copy-start.4
  115.6 5.7 %copy-start.5 = (bf16[1,2,8,100,256]{4,2,3,1,0:T(8,128)(2,1)S(1)}, bf16[1,2,8,100,256]{4,2,3,1,0:T(8,128)(2,1)}, u32[]{:S(2)}) copy-start(bf16[1,2,8,100,256]{4,2,3,1,0:T(8,128)(2,1)} %get-tuple-element.25) | copy-start | bytes 2457604
  143.4 1.0 copy-start.6
  144.4 1.0 copy-start.8
  146.1 1.5 copy-start.9
  147.6 2.9 %copy-start.1 = (bf16[8,100,800]{2,1,0:T(8,128)(2,1)S(1)}, bf16[8,100,800]{2,1,0:T(8,128)(2,1)}, u32[]{:S(2)}) copy-start(bf16[8,100,800]{2,1,0:T(8,128)(2,1)} %convert_element_type.180) | copy-start | bytes 3840004

commit v2 on v0

v2 whole, which is shorter than its diff:
```python
import functools

import jax
import jax.numpy as jnp
from jax import lax
from jax.experimental import pallas as pl
from jax.experimental.pallas import tpu as pltpu
from jax.sharding import Mesh, PartitionSpec as P

EPS = 1e-06
GELU_C = 0.7978845608
GELU_K = 0.044715
MP = ("y", "x_hi")
DP = ("x_lo", "z", "core")
PLANE = ("core", "x_lo", "y", "x_hi")
BF = jnp.bfloat16
F32 = jnp.float32
LANES = 128
OUT_COLS = 16
MIB = 1 << 20
NT = (((1,), (1,)), ((), ()))


def gelu_val(values, tanh_val):
    return 0.5 * values * (1.0 + tanh_val)


def gelu_der(values, tanh_val):
    return 0.5 * (1.0 + tanh_val) + 0.5 * values * (1.0 - tanh_val * tanh_val) * GELU_C * (
        1.0 + 3.0 * GELU_K * values * values
    )


def gelu_tanh(values):
    return jnp.tanh(GELU_C * (values + GELU_K * values * values * values))


def swap(value, axis):
    return lax.ppermute(value, axis, [(0, 1), (1, 0)])


def exchange(value, axis):
    return lax.all_to_all(value, axis, 0, 0)


def split3(value):
    first = value.astype(BF).astype(F32)
    second = (value - first).astype(BF).astype(F32)
    return first, second, value - first - second


def call(kernel, outs, vmem, cost, *args, scalars=0, scratch=()):
    specs = [pl.BlockSpec(memory_space=pltpu.SMEM)] * scalars
    specs += [pl.BlockSpec(memory_space=pltpu.VMEM)] * (len(args) - scalars)
    moved = sum(a.size * a.dtype.itemsize for a in args)
    return pl.pallas_call(
        kernel,
        out_shape=[jax.ShapeDtypeStruct(s, d) for s, d in outs],
        in_specs=specs,
        out_specs=[pl.BlockSpec(memory_space=pltpu.VMEM)] * len(outs),
        scratch_shapes=list(scratch),
        compiler_params=pltpu.CompilerParams(vmem_limit_bytes=vmem * MIB),
        cost_estimate=pl.CostEstimate(flops=cost, bytes_accessed=moved, transcendentals=0),
    )(*args)


def text_kernel(text_ref, out_ref):
    text = text_ref[...].astype(F32)
    out_ref[...] = (text * lax.rsqrt(jnp.sum(text * text, axis=-1, keepdims=True) + EPS)).astype(BF)


def feats_kernel(where_ref, feats_ref, out_ref):
    x_index, c_index = where_ref[0], where_ref[1]
    width = feats_ref.shape[1]
    z_count = out_ref.shape[3] // LANES
    chunk = width // (4 * z_count)
    source = lax.broadcasted_iota(jnp.int32, (2 * LANES, LANES), 0)
    target = lax.broadcasted_iota(jnp.int32, (2 * LANES, LANES), 1)
    inside = (target >= OUT_COLS) & (target < OUT_COLS + chunk)
    for x in range(2):
        for c in range(2):
            for z in range(z_count):
                begin = (x * 2 * z_count + z * 2 + c) * chunk
                window = min(begin // LANES * LANES, width - 2 * LANES)
                shift = begin - window - OUT_COLS
                move = jnp.where(inside & (source == target + shift), 1.0, 0.0).astype(BF)
                piece = jnp.dot(
                    feats_ref[:, window : window + 2 * LANES], move, preferred_element_type=F32
                )
                out_ref[x ^ x_index, c ^ c_index, :, z * LANES : (z + 1) * LANES] = piece.astype(BF)


def unit_kernel(got_ref, unit_ref, inv_ref, spread_ref):
    projected = jnp.sum(got_ref[...].astype(F32), axis=0)
    inv_norm = lax.rsqrt(jnp.sum(projected * projected, axis=-1, keepdims=True) + EPS)
    unit = projected * inv_norm
    unit_ref[...] = unit
    inv_ref[...] = jnp.broadcast_to(inv_norm, inv_ref.shape)
    spread_ref[...] = jnp.broadcast_to(unit.astype(BF)[None], spread_ref.shape)


def logits_kernel(where_ref, scale_ref, video_ref, *refs):
    text_refs, (expo_ref, first_ref, lanes_ref, spread_ref, col_ref) = refs[:4], refs[4:]
    x_index, c_index = where_ref[0], where_ref[1]
    scale_val = scale_ref[0]
    z_count, own_rows, emb = video_ref.shape
    video = video_ref[...].reshape(z_count * own_rows, emb)
    first = jnp.zeros((z_count * own_rows, emb), F32)
    row_part = jnp.zeros((z_count * own_rows, 1), F32)
    for block in range(4):
        rx, rc = block // 2, block % 2
        text = text_refs[block][...]
        expo = jnp.exp(scale_val * lax.dot_general(video, text, NT, preferred_element_type=F32))
        expo_ref[block] = expo
        row_part += jnp.sum(expo, axis=1, keepdims=True)
        col_part = jnp.sum(expo, axis=0, keepdims=True)
        place = ((rc ^ c_index) * 2 + (rx ^ x_index)) * 2
        for half in range(2):
            col_ref[pl.ds(place + half, 1), :] = col_part[:, half * LANES : (half + 1) * LANES]
        first += jnp.dot(expo.astype(BF), text, preferred_element_type=F32)
    first_ref[...] = first.astype(BF).reshape(first_ref.shape)
    row_hi = row_part.astype(BF).astype(F32)
    lane = lax.broadcasted_iota(jnp.int32, (z_count * own_rows, LANES), 1)
    both = jnp.where(lane < LANES // 2, row_hi, row_part - row_hi)
    lanes_ref[...] = both.astype(BF).reshape(lanes_ref.shape)
    spread_ref[...] = jnp.broadcast_to(col_ref[...][None], spread_ref.shape)


def weights_kernel(where_ref, got_ref, expo_ref, first_ref, lanes_ref, *refs):
    text_refs, (packed_ref, log_ref, inv_ref) = refs[:4], refs[4:]
    x_index, c_index = where_ref[0], where_ref[1]
    z_count, own_rows, emb = first_ref.shape
    col_sum = jnp.sum(got_ref[...], axis=0)
    log_ref[...] = jnp.log(col_sum)
    inv_ref[...] = 1.0 / col_sum
    second = jnp.zeros((z_count * own_rows, emb), F32)
    for block in range(4):
        rx, rc = block // 2, block % 2
        place = ((rc ^ c_index) * 2 + (rx ^ x_index)) * 2
        for half in range(2):
            lanes = slice(half * LANES, (half + 1) * LANES)
            weight = expo_ref[block, :, lanes] * inv_ref[pl.ds(place + half, 1), :]
            second += jnp.dot(
                weight.astype(BF), text_refs[block][lanes, :], preferred_element_type=F32
            )
    packed_ref[:, :, :emb] = first_ref[...]
    packed_ref[:, :, emb : 2 * emb] = second.astype(BF).reshape(first_ref.shape)
    packed_ref[:, :, 2 * emb :] = lanes_ref[...]


def proj_kernel(where_ref, scale_ref, back_ref, unit_ref, inv_ref, text_ref, log_ref, out_ref):
    scale_val = scale_ref[0]
    own_rows, emb = unit_ref.shape
    back = jnp.sum(back_ref[...].astype(F32), axis=0)
    half = 2 * emb + LANES // 2
    row_sum = back[:, 2 * emb : 2 * emb + 1] + back[:, half : half + 1]
    weighted = back[:, :emb] / row_sum + back[:, emb : 2 * emb]
    text = text_ref[where_ref[2]].astype(F32)
    unit = unit_ref[...]
    positive = scale_val * jnp.sum(unit.astype(BF).astype(F32) * text, axis=-1, keepdims=True)
    rows_piece = jnp.sum(jnp.log(row_sum) - 2.0 * positive, axis=0, keepdims=True)
    cols_piece = jnp.sum(jnp.sum(log_ref[...], axis=0, keepdims=True), axis=1, keepdims=True)
    a, b, c = split3(rows_piece + cols_piece / out_ref.shape[0])
    grad_emb = 0.5 * scale_val * weighted - scale_val * text
    grad_proj = inv_ref[:, :1] * (
        grad_emb - unit * jnp.sum(unit * grad_emb, axis=-1, keepdims=True)
    )
    lane = lax.broadcasted_iota(jnp.int32, (own_rows, LANES), 1)
    row = lax.broadcasted_iota(jnp.int32, (own_rows, LANES), 0)
    loss = jnp.where(lane == 0, a, jnp.where(lane == 1, b, jnp.where(lane == 2, c, 0.0)))
    loss = jnp.where(row == 0, loss, 0.0)
    sent = jnp.concatenate([grad_proj, loss], axis=1).astype(BF)
    out_ref[...] = jnp.broadcast_to(sent[None], out_ref.shape)


def gelu_kernel(*refs):
    pre_refs, (hidden_ref, der_ref) = refs[:4], refs[4:]
    for block in range(4):
        pre = pre_refs[block][...].astype(F32)
        tanh_val = gelu_tanh(pre)
        hidden_ref[block] = gelu_val(pre, tanh_val).astype(BF)
        der_ref[block] = gelu_der(pre, tanh_val).astype(BF)


def grads_kernel(where_ref, grads_ref, hidden_ref, der_ref, weight_ref, *refs):
    feats_refs, (out_ref,) = refs[:4], refs[4:]
    x_index, c_index = where_ref[0], where_ref[1]
    _, mp_count, own_rows, wide = grads_ref.shape
    emb = wide - LANES
    hid = weight_ref.shape[0]
    z_count = out_ref.shape[0]
    rows = mp_count * own_rows
    source = lax.broadcasted_iota(jnp.int32, (emb, LANES), 0)
    target = lax.broadcasted_iota(jnp.int32, (emb, LANES), 1)
    column = x_index * (emb // 2) + (target // OUT_COLS) * (2 * OUT_COLS) + c_index * OUT_COLS
    pick = jnp.where(source == column + target % OUT_COLS, 1.0, 0.0).astype(BF)
    grads, picked = [], []
    for block in range(4):
        rx, rc = block // 2, block % 2
        part = grads_ref[(rc ^ c_index) * 2 + (rx ^ x_index), :, :, :emb].reshape(rows, emb)
        grads.append(part)
        picked.append(jnp.dot(part, pick, preferred_element_type=F32).astype(BF))
    loss = jnp.sum(grads_ref[:, :, 0, emb:].astype(F32).reshape(4 * mp_count, LANES), axis=0, keepdims=True)
    loss = jnp.sum(loss, axis=1, keepdims=True)
    parts = 2
    step = hid // parts
    lane = lax.broadcasted_iota(jnp.int32, (step, LANES), 1)
    row = lax.broadcasted_iota(jnp.int32, (step, LANES), 0)
    a, b, c = split3(loss)
    extra = jnp.where(row == 0, a, jnp.where(row == 1, b, jnp.where(row == 2, c, 0.0)))
    extra = jnp.where(lane == LANES - 1, extra, 0.0)
    for part in range(parts):
        span = slice(part * step, (part + 1) * step)
        total = jnp.zeros((step, z_count * LANES), F32)
        outer = jnp.zeros((step, LANES), F32)
        for block in range(4):
            grad_hidden = lax.dot_general(
                weight_ref[span, :], grads[block], NT, preferred_element_type=F32
            )
            grad_pre = (grad_hidden * der_ref[block, span, :].astype(F32)).astype(BF)
            total += jnp.dot(grad_pre, feats_refs[block][...], preferred_element_type=F32)
            outer += jnp.dot(hidden_ref[block, span, :], picked[block], preferred_element_type=F32)
        for z in range(z_count):
            moved = outer if z == 0 else pltpu.roll(outer, LANES - z * OUT_COLS, 1)
            value = jnp.where(lane < OUT_COLS, moved, total[:, z * LANES : (z + 1) * LANES])
            if part == 0:
                value = jnp.where(lane == LANES - 1, extra, value)
            out_ref[z, span, :] = value.astype(BF)


def final_kernel(got_ref, in_ref, out_ref, loss_ref, *, batch_total):
    total = jnp.sum(got_ref[...].astype(F32), axis=0)
    turned = total.T
    in_rows = in_ref.shape[0]
    out_ref[...] = turned[:OUT_COLS]
    in_ref[...] = turned[OUT_COLS : OUT_COLS + in_rows]
    loss = jnp.sum(total[:3, LANES - 1 :], axis=0, keepdims=True) / (2.0 * batch_total)
    loss_ref[...] = loss


def on_device(video_feats, text_feats, weight_in, weight_out, logit_scale):
    rows, d_in = video_feats.shape
    hid, emb = weight_out.shape
    mp_count = lax.axis_size(MP)
    z_count = lax.axis_size("z")
    plane = lax.axis_size(PLANE)
    own_rows = rows // mp_count
    batch_total = rows * lax.axis_size(DP)
    where = jnp.stack([lax.axis_index("x_lo"), lax.axis_index("core"), lax.axis_index(MP)])
    where = where.astype(jnp.int32)

    pre_t = lax.dot_general(weight_in, video_feats, (((0,), (1,)), ((), ())), preferred_element_type=F32)
    hidden_t = gelu_val(pre_t, gelu_tanh(pre_t)).astype(BF)
    partial_value = lax.dot_general(
        hidden_t, weight_out, (((0,), (0,)), ((), ())), preferred_element_type=F32
    ).astype(BF)
    got = exchange(partial_value.reshape(mp_count, own_rows, emb), MP)

    (text_emb,) = call(text_kernel, [((rows, emb), BF)], 8, 10**6, text_feats)
    text_x = swap(text_emb, "x_lo")
    text = (text_emb, swap(text_emb, "core"), text_x, swap(text_x, "core"))

    (feats,) = call(
        feats_kernel, [((2, 2, rows, z_count * LANES), BF)], 16, 10**9, where, video_feats, scalars=1
    )
    feats_x = swap(feats[1], "x_lo")
    feats_q = (feats[0, 0], swap(feats[0, 1], "core"), feats_x[0], swap(feats_x[1], "core"))

    pre_bf = pre_t.astype(BF)
    pre_x = swap(pre_bf, "x_lo")
    pre = (pre_bf, swap(pre_bf, "core"), pre_x, swap(pre_x, "core"))

    unit, inv_norm, video = call(
        unit_kernel,
        [((own_rows, emb), F32), ((own_rows, LANES), F32), ((z_count, own_rows, emb), BF)],
        8, 10**6, got,
    )
    video_rows = exchange(video, "z")
    expo, first, lanes, cols = call(
        logits_kernel,
        [
            ((4, rows, rows), F32),
            ((z_count, own_rows, emb), BF),
            ((z_count, own_rows, LANES), BF),
            ((plane, 8, LANES), F32),
        ],
        16, 10**9, where, logit_scale, video_rows, *text, scalars=2,
        scratch=[pltpu.VMEM((8, LANES), F32)],
    )
    cols = exchange(cols, PLANE)
    packed, logs = call(
        weights_kernel,
        [((z_count, own_rows, 2 * emb + LANES), BF), ((8, LANES), F32)],
        16, 10**9, where, cols, expo, first, lanes, *text, scalars=1,
        scratch=[pltpu.VMEM((8, LANES), F32)],
    )
    back = exchange(packed, "z")
    (sent,) = call(
        proj_kernel, [((plane, own_rows, emb + LANES), BF)], 8, 10**6,
        where, logit_scale, back, unit, inv_norm, text_emb.reshape(mp_count, own_rows, emb), logs,
        scalars=2,
    )
    grads = exchange(sent, PLANE)
    hidden_all, der_all = call(
        gelu_kernel, [((4, hid, rows), BF), ((4, hid, rows), BF)], 24, 3 * 10**9, *pre
    )
    (packed,) = call(
        grads_kernel, [((z_count, hid, LANES), BF)], 40, 6 * 10**9,
        where, grads.reshape(4, mp_count, own_rows, emb + LANES), hidden_all, der_all, weight_out,
        *feats_q, scalars=1,
    )
    final = exchange(packed, "z")
    in_rows = d_in // lax.axis_size(DP)
    grad_in, grad_out, loss = call(
        functools.partial(final_kernel, batch_total=batch_total),
        [((in_rows, hid), F32), ((OUT_COLS, hid), F32), ((1, 1), F32)],
        16, 10**7, final,
    )
    return (loss.reshape(1), grad_in, grad_out.T)


def solution(mesh):
    fine = Mesh(mesh.devices.reshape(2, -1, 2, mesh.devices.shape[1] // 2, 2), DP + MP)
    in_specs = (P(DP, None), P(DP, None), P(None, MP), P(MP, None), P())
    out_specs = (P(), P(DP, MP), P(MP, DP))
    return jax.shard_map(
        on_device, mesh=fine, in_specs=in_specs, out_specs=out_specs, check_vma=False
    )
```

time: 670 us -> 182 us (0.27)
  waiting for transfers between devices: 457 us -> 50.5 us
  blocking collectives: 157 us -> 61.9 us
  starting transfers between devices: 0.21 us -> 31.3 us
  between operations: 20.8 us -> 1.45 us
  Pallas kernels: 0 us -> 16.3 us
  matrix products: 20.4 us -> 6.61 us
  local copies, waits for them, and re-layouts: 4.26 us -> 13.6 us
    psum x2 -> x0, waiting for transfers between devices: 175 us -> none  [the longest x1 93.6 us: on_device(): projected = lax.psum(partial_value, 'mp')]
    unnamed x6 -> x0, waiting for transfers between devices: 167 us -> none
    psum x3 -> x0, blocking collectives: 157 us -> none  [the longest x1 80.4 us: on_device(): loss = lax.psum(loss_piece, ('dp', 'mp')) / (2.0 * batch_total)]
    reduce_scatter x1 -> x0, waiting for transfers between devices: 114 us -> none  [on_device(): grad_out = lax.psum_scatter(out_term, 'dp', scatter_dimension=1, tiled=True)]
    all_to_all x0 -> x2, blocking collectives: none -> 61.9 us  [exchange(): return lax.all_to_all(value, axis, 0, 0)]
    all_to_all x0 -> x4, waiting for transfers between devices: none -> 26.2 us  [exchange(): return lax.all_to_all(value, axis, 0, 0)]
    ppermute x0 -> x9, waiting for transfers between devices: none -> 24.2 us  [swap(): return lax.ppermute(value, axis, [(0, 1), (1, 0)])]
    all_to_all x0 -> x4, starting transfers between devices: none -> 23.4 us  [exchange(): return lax.all_to_all(value, axis, 0, 0)]
  transfers between devices with their start and end apart: 5 -> 13, of which waited for: 4 -> 6; matrix products, arithmetic and copies ran while one was open for 1% -> 2% of each run, Pallas kernels for 0% -> 4%
where the time goes in v2:
time: 182 us
  blocking collectives  61.9 us (34%)
  waiting for transfers between devices  50.5 us (28%)
  starting transfers between devices  31.3 us (17%)
  Pallas kernels  16.3 us (9%)
  local copies, waits for them, and re-layouts  13.6 us (7%)
  matrix products  6.61 us (4%)
    all_to_all x2, blocking collectives, exchange(): return lax.all_to_all(value, axis, 0, 0)  61.9 us
    all_to_all x4, waiting for transfers between devices, exchange(): return lax.all_to_all(value, axis, 0, 0)  26.2 us
    ppermute x9, waiting for transfers between devices, swap(): return lax.ppermute(value, axis, [(0, 1), (1, 0)])  24.2 us
    all_to_all x4, starting transfers between devices, exchange(): return lax.all_to_all(value, axis, 0, 0)  23.4 us
    pallas_call x9, Pallas kernels, call(): pl.pallas_call(kernel, out_shape=[jax.ShapeDtypeStruct(s, d) for s, d in...  16.3 us
    unnamed x28, local copies, waits for them, and re-layouts  10.4 us
    ppermute x9, starting transfers between devices, swap(): return lax.ppermute(value, axis, [(0, 1), (1, 0)])  7.96 us
    dot_general x1, matrix products, on_device(): lax.dot_general(weight_in, video_feats, (((0,), (1,)), ((), ())), preferr...  5.36 us
  transfers between devices with their start and end apart: 13, of which 6 were waited for; matrix products, arithmetic and copies ran while one was open for 2% of the time, Pallas kernels for 4%

profile of v2, /device:TPU:1, one launch (start us, length us, event | category | flops | bytes accessed | tf_op | source)
XLA Modules:
  0.0 181.7 jit_solution(6604738543983316776)
XLA Ops:
  0.6 0.0 copy-start.3
  0.6 5.4 %fusion.14 = (bf16[800,256]{1,0:T(8,128)(2,1)}, f32[800,256]{1,0:T(8,128)S(1)}) fusion(bf16[3200,800]{0,1:T(8,128)(2,1)} %param.7, bf16[256,3200]{1,0:T(8,128)(2,1)} %feats_ref.1), kind=kOutput, calls=%fused_computation.21 | convolution fusion | flops 1310924800 | bytes 7987200 | tf_op jit(solution)/shard_map/dot_general | solution.py:252
  6.0 0.0 copy-done.3
  6.0 1.2 convolution_convert_fusion
  7.3 7.5 %all-to-all-start = ((bf16[8,32,512]{2,1,0:T(8,128)(2,1)}), bf16[8,32,512]{2,1,0:T(8,128)(2,1)S(1)}, u32[]{:S(2)}, u32[]{:S(2)}) async-start(bf16[8,32,512]{2,1,0:T(8,128)(2,1)} %bitcast.3), calls=%async_computation | async-start | bytes 524288 | tf_op jit(solution)/shard_map/all_to_all | solution.py:43
  14.7 0.0 copy-done.2
  14.7 0.1 shard_map.77.refs_0_
  14.9 0.4 collective-permute-start.1
  15.3 7.1 %all-to-all-done.got_ref = bf16[8,32,512]{2,1,0:T(8,128)(2,1)S(1)} async-done(((bf16[8,32,512]{2,1,0:T(8,128)(2,1)}), bf16[8,32,512]{2,1,0:T(8,128)(2,1)S(1)}, u32[]{:S(2)}, u32[]{:S(2)}) %all-to-all-start) | async-done | bytes 262176 | tf_op jit(solution)/shard_map/all_to_all | solution.py:43
  22.4 0.8 shard_map.76
  23.2 8.2 %all-to-all-start.1 = ((bf16[8,32,512]{2,1,0:T(8,128)(2,1)}), bf16[8,32,512]{2,1,0:T(8,128)(2,1)S(1)}, u32[]{:S(2)}, u32[]{:S(2)}) async-start(bf16[8,32,512]{2,1,0:T(8,128)(2,1)} %get-tuple-element.17), calls=%async_computation.1 | async-start | bytes 524288 | tf_op jit(solution)/shard_map/all_to_all | solution.py:43
  31.4 3.8 %collective-permute-start = (bf16[256,512]{1,0:T(8,128)(2,1)S(1)}, bf16[256,512]{1,0:T(8,128)(2,1)S(1)}, u32[]{:S(2)}, u32[]{:S(2)}) collective-permute-start(bf16[256,512]{1,0:T(8,128)(2,1)S(1)} %shard_map.77.refs_0_), channel_id=1, source_target_pairs={{0,8},{8,0},{1,9},{9,1},{2,10},{10,2},{3,11},{11,3},{4,12},{12,4},... | collective-permute-start | bytes 786440 | tf_op jit(solution)/shard_map/ppermute | solution.py:39
  35.2 0.0 collective-permute-done.1.refs_2_
  35.2 0.1 collective-permute-start.2
  36.0 0.1 pad_add_fusion.where_ref
  36.1 0.3 collective-permute-done.refs_1_
  36.4 0.4 collective-permute-done.2.refs_3_
  36.8 4.1 %all-to-all-done.1.video_ref = bf16[8,32,512]{2,1,0:T(8,128)(2,1)S(1)} async-done(((bf16[8,32,512]{2,1,0:T(8,128)(2,1)}), bf16[8,32,512]{2,1,0:T(8,128)(2,1)S(1)}, u32[]{:S(2)}, u32[]{:S(2)}) %all-to-all-start.1) | async-done | bytes 262176 | tf_op jit(solution)/shard_map/all_to_all | solution.py:43
  40.9 1.7 shard_map.78
  42.6 15.1 %all_to_all.30.got_ref = f32[32,8,128]{2,1,0:T(8,128)S(1)} all-to-all(f32[32,8,128]{2,1,0:T(8,128)S(1)} %get-tuple-element.18), channel_id=1, replica_groups=mesh['x_lo'=2,'z'=8,'core'=2,'y'=4,'x_hi'=2] {'core','x_lo','y','x_hi'}, dimensions={0} | all-to-all | bytes 262144 | tf_op jit(solution)/shard_map/all_to_all | solution.py:43
  57.7 2.1 %shard_map.79 = (bf16[8,32,1152]{2,1,0:T(8,128)(2,1)}, f32[8,128]{1,0:T(8,128)S(1)}) custom-call(s32[3]{0:T(128)S(1)} %pad_add_fusion.where_ref, f32[32,8,128]{2,1,0:T(8,128)S(1)} %all_to_all.30.got_ref, f32[4,256,256]{2,1,0:T(8,128)S(1)} %get-tuple-element.19.expo_ref, bf16[8,32,512]{2,1,0:T(8,128)(2,1)S(1)} %get-tuple-element.20.first_ref, ...), custom_call_target="tpu_custom_call" | custom-call | flops 1000000000 | bytes 2555916 | tf_op jit(solution)/shard_map/pallas_call | solution.py:56
  59.8 3.5 %all-to-all-start.3 = ((bf16[8,32,1152]{2,1,0:T(8,128)(2,1)}), bf16[8,32,1152]{2,1,0:T(8,128)(2,1)S(1)}, u32[]{:S(2)}, u32[]{:S(2)}) async-start(bf16[8,32,1152]{2,1,0:T(8,128)(2,1)} %get-tuple-element.22), calls=%async_computation.3 | async-start | bytes 1179648 | tf_op jit(solution)/shard_map/all_to_all | solution.py:43
  63.3 0.0 copy-start
  63.3 1.4 copy-done
  64.8 1.8 shard_map.82
  66.6 1.0 slice_bitcast_fusion
  67.6 0.1 collective-permute-start.7
  67.6 15.0 %all-to-all-done.3.back_ref = bf16[8,32,1152]{2,1,0:T(8,128)(2,1)S(1)} async-done(((bf16[8,32,1152]{2,1,0:T(8,128)(2,1)}), bf16[8,32,1152]{2,1,0:T(8,128)(2,1)S(1)}, u32[]{:S(2)}, u32[]{:S(2)}) %all-to-all-start.3) | async-done | bytes 589856 | tf_op jit(solution)/shard_map/all_to_all | solution.py:43
  82.7 1.9 %shard_map.80 = bf16[32,32,640]{2,1,0:T(8,128)(2,1)} custom-call(s32[3]{0:T(128)S(1)} %pad_add_fusion.where_ref, f32[1]{0:T(128)S(6)} %copy.8.scale_ref, bf16[8,32,1152]{2,1,0:T(8,128)(2,1)S(1)} %all-to-all-done.3.back_ref, f32[32,512]{1,0:T(8,128)S(1)} %get-tuple-element.23.unit_ref, f32[32,128]{1,0:T(8,128)S(1)} %get-tuple-element.24.inv_ref, ...), custom_call_target="tpu_custom_call" | custom-call | flops 1000000 | bytes 938000 | tf_op jit(solution)/shard_map/pallas_call | solution.py:56
  84.6 4.2 %all-to-all-start.4 = ((bf16[32,32,640]{2,1,0:T(8,128)(2,1)}), bf16[32,32,640]{2,1,0:T(8,128)(2,1)S(1)}, u32[]{:S(2)}, u32[]{:S(2)}) async-start(bf16[32,32,640]{2,1,0:T(8,128)(2,1)} %shard_map.80), calls=%async_computation.4 | async-start | bytes 2621440 | tf_op jit(solution)/shard_map/all_to_all | solution.py:43
  88.8 0.0 copy-start.9
  88.8 1.5 collective-permute-start.4
  90.3 0.6 collective-permute-start.3
  90.9 0.9 slice_bitcast_fusion.3
  91.7 0.0 collective-permute-start.6
  91.7 23.5 %collective-permute-done.4.refs_2_ = bf16[800,256]{1,0:T(8,128)(2,1)S(1)} collective-permute-done((bf16[800,256]{1,0:T(8,128)(2,1)}, bf16[800,256]{1,0:T(8,128)(2,1)S(1)}, u32[]{:S(2)}, u32[]{:S(2)}) %collective-permute-start.4) | collective-permute-done | bytes 409632 | tf_op jit(solution)/shard_map/ppermute | solution.py:39
  115.3 1.2 collective-permute-start.5
  116.5 0.0 collective-permute-done.7
  116.5 1.3 slice_bitcast_fusion.1
  117.8 0.0 copy-start.1
  117.8 0.0 copy-start.4
  117.8 0.3 collective-permute-start.8
  118.1 0.0 collective-permute-done.3.refs_1_
  118.1 0.0 collective-permute-done.5.refs_3_
  118.1 0.0 copy-done.9
  118.1 2.4 %shard_map.81 = (bf16[4,800,256]{2,1,0:T(8,128)(2,1)S(1)}, bf16[4,800,256]{2,1,0:T(8,128)(2,1)S(1)}) custom-call(bf16[800,256]{1,0:T(8,128)(2,1)S(1)} %copy-done.9, bf16[800,256]{1,0:T(8,128)(2,1)S(1)} %collective-permute-done.3.refs_1_, bf16[800,256]{1,0:T(8,128)(2,1)S(1)} %collective-permute-done.4.refs_2_, bf16[800,256]{1,0:T(8,128)(2,1)S(1)} %collective-permute-done.5.refs_3_), custom_call_target="tpu_custom_call" | custom-call | flops 3000000000 | bytes 1638400 | tf_op jit(solution)/shard_map/pallas_call | solution.py:56
  120.5 0.0 copy-start.10
  120.6 1.2 copy-done.10
  121.7 1.2 copy-done.12
  122.9 0.0 collective-permute-done.6.refs_1_
  122.9 0.8 copy-done.5
  123.7 0.0 collective-permute-done.8.refs_3_
  123.7 0.8 copy-done.7
  124.5 0.0 all-to-all-done.4
  124.5 0.0 copy-done.1
  124.5 0.0 copy-done.4
  124.6 0.0 copy-start.6
  124.6 1.0 copy-done.6
  125.6 1.0 copy-done.8
  126.6 1.4 copy-done.11
  128.1 1.4 copy-done.13
  129.5 4.4 %shard_map.83 = bf16[8,800,128]{2,1,0:T(8,128)(2,1)S(1)} custom-call(s32[3]{0:T(128)S(1)} %pad_add_fusion.where_ref, bf16[4,8,32,640]{3,2,1,0:T(8,128)(2,1)S(1)} %bitcast.21, bf16[4,800,256]{2,1,0:T(8,128)(2,1)S(1)} %copy-done.11, bf16[4,800,256]{2,1,0:T(8,128)(2,1)S(1)} %copy-done.13, bf16[800,512]{1,0:T(8,128)(2,1)S(1)} %copy-done.4, ...), custom_call_target="tpu_custom_call" | custom-call | flops 6000000000 | bytes 7503884 | tf_op jit(solution)/shard_map/pallas_call | solution.py:56
  133.9 46.8 %all_to_all.31.got_ref = bf16[8,800,128]{2,1,0:T(8,128)(2,1)S(1)} all-to-all(bf16[8,800,128]{2,1,0:T(8,128)(2,1)S(1)} %shard_map.83), channel_id=1, replica_groups=mesh['x_lo'=2,'z'=8,'core'=2,'y'=4,'x_hi'=2] {'z'}, dimensions={0} | all-to-all | bytes 3276800 | tf_op jit(solution)/shard_map/all_to_all | solution.py:43
  180.7 1.0 shard_map.84
  (7 shorter events, 0.0 us)
Async XLA Ops:
  0.6 5.4 %copy-start.3 = (bf16[800,512]{1,0:T(8,128)(2,1)S(1)}, bf16[800,512]{1,0:T(8,128)(2,1)}, u32[]{:S(2)}) copy-start(bf16[800,512]{1,0:T(8,128)(2,1)} %weight_ref.1) | copy-start | bytes 2457604
  6.0 8.7 %copy-start.2 = (bf16[256,512]{1,0:T(8,128)(2,1)S(1)}, bf16[256,512]{1,0:T(8,128)(2,1)}, u32[]{:S(2)}) copy-start(bf16[256,512]{1,0:T(8,128)(2,1)} %text_ref.1) | copy-start | bytes 786436
  7.3 15.1 %all-to-all-start = ((bf16[8,32,512]{2,1,0:T(8,128)(2,1)}), bf16[8,32,512]{2,1,0:T(8,128)(2,1)S(1)}, u32[]{:S(2)}, u32[]{:S(2)}) async-start(bf16[8,32,512]{2,1,0:T(8,128)(2,1)} %bitcast.3), calls=%async_computation | async-start | bytes 524288 | tf_op jit(solution)/shard_map/all_to_all | solution.py:43
  14.9 20.4 %collective-permute-start.1 = (bf16[256,512]{1,0:T(8,128)(2,1)S(1)}, bf16[256,512]{1,0:T(8,128)(2,1)S(1)}, u32[]{:S(2)}, u32[]{:S(2)}) collective-permute-start(bf16[256,512]{1,0:T(8,128)(2,1)S(1)} %shard_map.77.refs_0_), channel_id=1, source_target_pairs={{0,128},{128,0},{1,129},{129,1},{2,130},{130,2},{3,131},{131,3},{4... | collective-permute-start | bytes 786440 | tf_op jit(solution)/shard_map/ppermute | solution.py:39
  23.2 17.7 %all-to-all-start.1 = ((bf16[8,32,512]{2,1,0:T(8,128)(2,1)}), bf16[8,32,512]{2,1,0:T(8,128)(2,1)S(1)}, u32[]{:S(2)}, u32[]{:S(2)}) async-start(bf16[8,32,512]{2,1,0:T(8,128)(2,1)} %get-tuple-element.17), calls=%async_computation.1 | async-start | bytes 524288 | tf_op jit(solution)/shard_map/all_to_all | solution.py:43
  31.4 5.0 %collective-permute-start = (bf16[256,512]{1,0:T(8,128)(2,1)S(1)}, bf16[256,512]{1,0:T(8,128)(2,1)S(1)}, u32[]{:S(2)}, u32[]{:S(2)}) collective-permute-start(bf16[256,512]{1,0:T(8,128)(2,1)S(1)} %shard_map.77.refs_0_), channel_id=1, source_target_pairs={{0,8},{8,0},{1,9},{9,1},{2,10},{10,2},{3,11},{11,3},{4,12},{12,4},... | collective-permute-start | bytes 786440 | tf_op jit(solution)/shard_map/ppermute | solution.py:39
  35.2 1.5 collective-permute-start.2
  59.8 22.9 %all-to-all-start.3 = ((bf16[8,32,1152]{2,1,0:T(8,128)(2,1)}), bf16[8,32,1152]{2,1,0:T(8,128)(2,1)S(1)}, u32[]{:S(2)}, u32[]{:S(2)}) async-start(bf16[8,32,1152]{2,1,0:T(8,128)(2,1)} %get-tuple-element.22), calls=%async_computation.3 | async-start | bytes 1179648 | tf_op jit(solution)/shard_map/all_to_all | solution.py:43
  63.3 1.4 copy-start
  67.6 48.9 %collective-permute-start.7 = (bf16[2,256,1024]{2,1,0:T(8,128)(2,1)}, bf16[2,256,1024]{2,1,0:T(8,128)(2,1)}, u32[]{:S(2)}, u32[]{:S(2)}) collective-permute-start(bf16[2,256,1024]{2,1,0:T(8,128)(2,1)} %slice_bitcast_fusion), channel_id=1, source_target_pairs={{0,128},{128,0},{1,129},{129,1},{2,130},{130,2},{3,131},{131,3},{4... | collective-permute-start | bytes 3145736 | tf_op jit(solution)/shard_map/ppermute | solution.py:39
  84.6 39.9 %all-to-all-start.4 = ((bf16[32,32,640]{2,1,0:T(8,128)(2,1)}), bf16[32,32,640]{2,1,0:T(8,128)(2,1)S(1)}, u32[]{:S(2)}, u32[]{:S(2)}) async-start(bf16[32,32,640]{2,1,0:T(8,128)(2,1)} %shard_map.80), calls=%async_computation.4 | async-start | bytes 2621440 | tf_op jit(solution)/shard_map/all_to_all | solution.py:43
  88.8 29.3 %copy-start.9 = (bf16[800,256]{1,0:T(8,128)(2,1)S(1)}, bf16[800,256]{1,0:T(8,128)(2,1)}, u32[]{:S(2)}) copy-start(bf16[800,256]{1,0:T(8,128)(2,1)} %get-tuple-element.35.refs_0_) | copy-start | bytes 1228804
  88.8 26.5 %collective-permute-start.4 = (bf16[800,256]{1,0:T(8,128)(2,1)}, bf16[800,256]{1,0:T(8,128)(2,1)S(1)}, u32[]{:S(2)}, u32[]{:S(2)}) collective-permute-start(bf16[800,256]{1,0:T(8,128)(2,1)} %get-tuple-element.35.refs_0_), channel_id=1, source_target_pairs={{0,128},{128,0},{1,129},{129,1},{2,130},{130,2},{3,131},{131,3},{4... | collective-permute-start | bytes 1228808 | tf_op jit(solution)/shard_map/ppermute | solution.py:39
  90.3 27.8 %collective-permute-start.3 = (bf16[800,256]{1,0:T(8,128)(2,1)}, bf16[800,256]{1,0:T(8,128)(2,1)S(1)}, u32[]{:S(2)}, u32[]{:S(2)}) collective-permute-start(bf16[800,256]{1,0:T(8,128)(2,1)} %get-tuple-element.35.refs_0_), channel_id=1, source_target_pairs={{0,8},{8,0},{1,9},{9,1},{2,10},{10,2},{3,11},{11,3},{4,12},{12,4},... | collective-permute-start | bytes 1228808 | tf_op jit(solution)/shard_map/ppermute | solution.py:39
  91.7 31.2 %collective-permute-start.6 = (bf16[256,1024]{1,0:T(8,128)(2,1)S(1)}, bf16[256,1024]{1,0:T(8,128)(2,1)S(1)}, u32[]{:S(2)}, u32[]{:S(2)}) collective-permute-start(bf16[256,1024]{1,0:T(8,128)(2,1)S(1)} %get-tuple-element.31), channel_id=1, source_target_pairs={{0,8},{8,0},{1,9},{9,1},{2,10},{10,2},{3,11},{11,3},{4,12},{12,4},... | collective-permute-start | bytes 1572872 | tf_op jit(solution)/shard_map/ppermute | solution.py:39
  115.3 2.8 %collective-permute-start.5 = (bf16[800,256]{1,0:T(8,128)(2,1)S(1)}, bf16[800,256]{1,0:T(8,128)(2,1)S(1)}, u32[]{:S(2)}, u32[]{:S(2)}) collective-permute-start(bf16[800,256]{1,0:T(8,128)(2,1)S(1)} %collective-permute-done.4.refs_2_), channel_id=1, source_target_pairs={{0,8},{8,0},{1,9},{9,1},{2,10},{10,2},{3,11},{11,3},{4,12},{12,4},... | collective-permute-start | bytes 1228808 | tf_op jit(solution)/shard_map/ppermute | solution.py:39
  117.8 6.8 %copy-start.1 = (bf16[256,1024]{1,0:T(8,128)(2,1)S(1)}, bf16[256,1024]{1,0:T(8,128)(2,1)}, u32[]{:S(2)}) copy-start(bf16[256,1024]{1,0:T(8,128)(2,1)} %get-tuple-element.32.refs_0_) | copy-start | bytes 1572868
  117.8 6.8 %copy-start.4 = (bf16[800,512]{1,0:T(8,128)(2,1)S(1)}, bf16[800,512]{1,0:T(8,128)(2,1)}, u32[]{:S(2)}) copy-start(bf16[800,512]{1,0:T(8,128)(2,1)} %weight_ref.1) | copy-start | bytes 2457604
  117.8 5.9 %collective-permute-start.8 = (bf16[256,1024]{1,0:T(8,128)(2,1)S(1)}, bf16[256,1024]{1,0:T(8,128)(2,1)S(1)}, u32[]{:S(2)}, u32[]{:S(2)}) collective-permute-start(bf16[256,1024]{1,0:T(8,128)(2,1)S(1)} %get-tuple-element.33), channel_id=1, source_target_pairs={{0,8},{8,0},{1,9},{9,1},{2,10},{10,2},{3,11},{11,3},{4,12},{12,4},... | collective-permute-start | bytes 1572872 | tf_op jit(solution)/shard_map/ppermute | solution.py:39
  120.5 1.2 copy-start.10
  121.7 1.2 copy-start.12
  122.9 0.8 copy-start.5
  123.7 0.8 copy-start.7
  124.6 1.0 copy-start.6
  125.6 1.0 copy-start.8
  126.6 1.4 copy-start.11
  128.1 1.4 copy-start.13

commit v3 on v2

v3 whole, which is shorter than its diff:
```python
import functools

import jax
import jax.numpy as jnp
from jax import lax
from jax.experimental import pallas as pl
from jax.experimental.pallas import tpu as pltpu
from jax.sharding import Mesh, PartitionSpec as P

EPS = 1e-06
GELU_C = 0.7978845608
GELU_K = 0.044715
MP = ("y", "x_hi")
DP = ("x_lo", "zh", "zl", "core")
CUBE = ("x_lo", "zl", "core")
COLS = ("zh", "y", "x_hi")
SPREAD = ("x_lo", "zl", "y", "x_hi")
BF = jnp.bfloat16
F32 = jnp.float32
LANES = 128
OUT_COLS = 16
MIB = 1 << 20
LIM = (60, 60, 8, 60, 60, 60, 60, 60, 16)
NT = (((1,), (1,)), ((), ()))


def gelu_val(values, tanh_val):
    return 0.5 * values * (1.0 + tanh_val)


def gelu_der(values, tanh_val):
    return 0.5 * (1.0 + tanh_val) + 0.5 * values * (1.0 - tanh_val * tanh_val) * GELU_C * (
        1.0 + 3.0 * GELU_K * values * values
    )


def gelu_tanh(values):
    return jnp.tanh(GELU_C * (values + GELU_K * values * values * values))


def swap(value, axis):
    return lax.ppermute(value, axis, [(0, 1), (1, 0)])


def exchange(value, axis):
    return lax.all_to_all(value, axis, 0, 0)


def split3(value):
    first = value.astype(BF).astype(F32)
    second = (value - first).astype(BF).astype(F32)
    return first, second, value - first - second


def call(kernel, outs, vmem, *args, scalars=0, scratch=(), after=(), raw=False):
    held = [] if raw else list(args[scalars:])
    total = len(args) + len(after)

    def body(*refs):
        outputs = refs[total : total + len(outs)]
        rest = refs[total + len(outs) :]
        if raw:
            kernel(*refs[: len(args)], *outputs, *rest)
            return
        places, sems, rest = rest[: len(held)], rest[len(held)], rest[len(held) + 1 :]
        copies = [
            pltpu.make_async_copy(refs[scalars + i], places[i], sems.at[i])
            for i in range(len(held))
        ]
        for copy in copies:
            copy.start()
        for copy in copies:
            copy.wait()
        kernel(*refs[:scalars], *places, *outputs, *rest)

    places = [pltpu.VMEM(a.shape, a.dtype) for a in held]
    if held:
        places.append(pltpu.SemaphoreType.DMA((len(held),)))
    anywhere = pl.BlockSpec(memory_space=pl.ANY)
    return pl.pallas_call(
        body,
        grid=(1,),
        out_shape=[jax.ShapeDtypeStruct(s, d) for s, d in outs],
        in_specs=[pl.BlockSpec(memory_space=pltpu.SMEM)] * scalars + [anywhere] * (total - scalars),
        out_specs=[whole(s) for s, _ in outs],
        scratch_shapes=[*places, *scratch],
        compiler_params=pltpu.CompilerParams(vmem_limit_bytes=vmem * MIB),
        cost_estimate=pl.CostEstimate(flops=1024, bytes_accessed=1024, transcendentals=0),
    )(*args, *after)


def whole(shape):
    return pl.BlockSpec(shape, lambda i: (0,) * len(shape), pipeline_mode=pl.Buffered(1))


def gate(after, *arrays):
    anywhere = pl.BlockSpec(memory_space=pl.ANY)
    return pl.pallas_call(
        lambda *refs: None,
        out_shape=[jax.ShapeDtypeStruct(a.shape, a.dtype) for a in arrays],
        in_specs=[anywhere] * (len(arrays) + 1),
        out_specs=[anywhere] * len(arrays),
        input_output_aliases={i + 1: i for i in range(len(arrays))},
        compiler_params=pltpu.CompilerParams(vmem_limit_bytes=60 * MIB),
    )(after, *arrays)


def parts_of(size, count):
    step = -(-size // (16 * count)) * 16
    return [slice(i, min(i + step, size)) for i in range(0, size, step)]


def head_kernel(
    text_hbm, feats_hbm, win_hbm, wout_hbm, partial_ref, pre_ref, emb_ref,
    text_ref, feats_ref, win_ref, wout_ref, hidden_ref, sems,
):
    spans = parts_of(win_ref.shape[0], 3)
    copies = [
        pltpu.make_async_copy(text_hbm, text_ref, sems.at[0]),
        pltpu.make_async_copy(feats_hbm, feats_ref, sems.at[1]),
    ]
    copies += [
        pltpu.make_async_copy(win_hbm.at[span], win_ref.at[span], sems.at[3 + i])
        for i, span in enumerate(spans)
    ]
    copies.append(pltpu.make_async_copy(wout_hbm, wout_ref, sems.at[2]))
    for copy in copies:
        copy.start()
    copies[0].wait()
    text = text_ref[...].astype(F32)
    emb_ref[...] = (text * lax.rsqrt(jnp.sum(text * text, axis=-1, keepdims=True) + EPS)).astype(BF)
    copies[1].wait()
    for i, span in enumerate(spans):
        copies[2 + i].wait()
        pre = lax.dot_general(win_ref[span, :], feats_ref[...], NT, preferred_element_type=F32)
        hidden_ref[span, :] = gelu_val(pre, gelu_tanh(pre)).astype(BF)
        pre_ref[span, :] = pre.astype(BF)
    copies[-1].wait()
    partial_ref[...] = lax.dot_general(
        hidden_ref[...], wout_ref[...], (((0,), (0,)), ((), ())), preferred_element_type=F32
    ).astype(BF)


def feats_kernel(where_ref, feats_ref, *out_refs):
    x_index, l_index, c_index = where_ref[0], where_ref[1], where_ref[2]
    rows, width = feats_ref.shape
    h_count = out_refs[0].shape[1] // LANES
    chunk = width // (8 * h_count)
    source = lax.broadcasted_iota(jnp.int32, (2 * LANES, LANES), 0)
    target = lax.broadcasted_iota(jnp.int32, (2 * LANES, LANES), 1)
    inside = (target >= OUT_COLS) & (target < OUT_COLS + chunk)
    for rx, rl, rc in [(a, b, c) for a in range(2) for b in range(2) for c in range(2)]:
        for h in range(h_count):
            place = ((rx ^ x_index) * h_count + h) * 2 + (rl ^ l_index)
            begin = (place * 2 + (rc ^ c_index)) * chunk
            window = jnp.minimum(begin // LANES * LANES, width - 2 * LANES)
            shift = begin - window - OUT_COLS
            move = jnp.where(inside & (source == target + shift), 1.0, 0.0).astype(BF)
            piece = feats_ref[:, pl.ds(pl.multiple_of(window, LANES), 2 * LANES)]
            piece = jnp.dot(piece, move, preferred_element_type=F32).astype(BF)
            out_refs[rx * 2 + rl][rc * rows : (rc + 1) * rows, h * LANES : (h + 1) * LANES] = piece


def unit_kernel(got_ref, unit_ref, inv_ref, spread_ref):
    projected = jnp.sum(got_ref[...].astype(F32), axis=0)
    inv_norm = lax.rsqrt(jnp.sum(projected * projected, axis=-1, keepdims=True) + EPS)
    unit = projected * inv_norm
    unit_ref[...] = unit
    inv_ref[...] = jnp.broadcast_to(inv_norm, inv_ref.shape)
    spread_ref[...] = jnp.broadcast_to(unit.astype(BF)[None], spread_ref.shape)


def expo_block(scale_val, video_ref, text):
    count, own_rows, emb = video_ref.shape
    video = video_ref[...].reshape(count * own_rows, emb)
    return jnp.exp(scale_val * lax.dot_general(video, text, NT, preferred_element_type=F32))


def column_place(where_ref, block):
    return lax.rem(where_ref[4] + block, 4) * 2


def logits_kernel(where_ref, scale_ref, video_ref, *refs):
    text_refs, (spread_ref, col_ref) = refs[:4], refs[4:]
    for block in range(4):
        expo = expo_block(scale_ref[0], video_ref, text_refs[block][...])
        col_part = jnp.sum(expo, axis=0, keepdims=True)
        for half in range(2):
            col_ref[pl.ds(column_place(where_ref, block) + half, 1), :] = col_part[
                :, half * LANES : (half + 1) * LANES
            ]
    spread_ref[...] = jnp.broadcast_to(col_ref[...][None], spread_ref.shape)


def weights_kernel(where_ref, scale_ref, video_ref, *refs):
    text_refs, (got_ref, packed_ref, log_ref, inv_ref) = refs[:4], refs[4:]
    count, own_rows, emb = video_ref.shape
    rows = count * own_rows
    col_sum = jnp.sum(got_ref[...], axis=0)
    log_ref[...] = jnp.log(col_sum)
    inv_ref[...] = 1.0 / col_sum
    first = jnp.zeros((rows, emb), F32)
    second = jnp.zeros((rows, emb), F32)
    row_part = jnp.zeros((rows, 1), F32)
    for block in range(4):
        text = text_refs[block][...]
        expo = expo_block(scale_ref[0], video_ref, text)
        row_part += jnp.sum(expo, axis=1, keepdims=True)
        place = column_place(where_ref, block)
        inv = jnp.concatenate([inv_ref[pl.ds(place + half, 1), :] for half in range(2)], axis=1)
        first += jnp.dot(expo.astype(BF), text, preferred_element_type=F32)
        second += jnp.dot((expo * inv).astype(BF), text, preferred_element_type=F32)
    packed_ref[:, :, :emb] = first.astype(BF).reshape(count, own_rows, emb)
    packed_ref[:, :, emb : 2 * emb] = second.astype(BF).reshape(count, own_rows, emb)
    row_hi = row_part.astype(BF).astype(F32)
    lane = lax.broadcasted_iota(jnp.int32, (rows, LANES), 1)
    both = jnp.where(lane < LANES // 2, row_hi, row_part - row_hi)
    packed_ref[:, :, 2 * emb :] = both.astype(BF).reshape(count, own_rows, LANES)


def proj_kernel(where_ref, scale_ref, back_ref, unit_ref, inv_ref, text_ref, log_ref, out_ref, *, sharers):
    scale_val = scale_ref[0]
    own_rows, emb = unit_ref.shape
    back = jnp.sum(back_ref[...].astype(F32), axis=0)
    half = 2 * emb + LANES // 2
    row_sum = back[:, 2 * emb : 2 * emb + 1] + back[:, half : half + 1]
    weighted = back[:, :emb] / row_sum + back[:, emb : 2 * emb]
    text = text_ref[where_ref[3]].astype(F32)
    unit = unit_ref[...]
    positive = scale_val * jnp.sum(unit.astype(BF).astype(F32) * text, axis=-1, keepdims=True)
    rows_piece = jnp.sum(jnp.log(row_sum) - 2.0 * positive, axis=0, keepdims=True)
    cols_piece = jnp.sum(jnp.sum(log_ref[...], axis=0, keepdims=True), axis=1, keepdims=True)
    a, b, c = split3(rows_piece + cols_piece / sharers)
    grad_emb = 0.5 * scale_val * weighted - scale_val * text
    grad_proj = inv_ref[:, :1] * (
        grad_emb - unit * jnp.sum(unit * grad_emb, axis=-1, keepdims=True)
    )
    lane = lax.broadcasted_iota(jnp.int32, (own_rows, LANES), 1)
    row = lax.broadcasted_iota(jnp.int32, (own_rows, LANES), 0)
    loss = jnp.where(lane == 0, a, jnp.where(lane == 1, b, jnp.where(lane == 2, c, 0.0)))
    loss = jnp.where(row == 0, loss, 0.0)
    sent = jnp.concatenate([grad_proj, loss], axis=1).astype(BF)
    out_ref[...] = jnp.broadcast_to(sent[None], out_ref.shape)


def gelu_kernel(*refs):
    pre_refs, (hidden_ref, der_ref) = refs[:8], refs[8:]
    rows = pre_refs[0].shape[1]
    for block in range(8):
        pre = pre_refs[block][...].astype(F32)
        tanh_val = gelu_tanh(pre)
        span = slice(block * rows, (block + 1) * rows)
        hidden_ref[:, span] = gelu_val(pre, tanh_val).astype(BF)
        der_ref[:, span] = gelu_der(pre, tanh_val).astype(BF)


def grads_kernel(where_ref, own_hbm, other_hbm, wout_hbm, der_hbm, hidden_hbm, *refs):
    feats_hbm, refs = refs[:8], refs[8:]
    out_ref, grads_ref, wout_ref, der_ref, hidden_ref, feats_ref, sems = refs
    x_index, l_index, c_index = where_ref[0], where_ref[1], where_ref[2]
    rows = own_hbm.shape[1]
    emb = wout_ref.shape[1]
    hid = wout_ref.shape[0]
    h_count = out_ref.shape[0]
    copies = []
    for block in range(8):
        rx, rl, rc = block // 4, block // 2 % 2, block % 2
        source = other_hbm if rc else own_hbm
        copies.append((source.at[(rx ^ x_index) * 2 + (rl ^ l_index)], grads_ref.at[block]))
    copies.append((wout_hbm, wout_ref))
    copies.append((der_hbm, der_ref))
    for block in range(8):
        side = block % 2 * rows
        copies.append((feats_hbm[block].at[pl.ds(side, rows)], feats_ref.at[pl.ds(block * rows, rows)]))
    copies.append((hidden_hbm, hidden_ref))
    copies = [pltpu.make_async_copy(a, b, sems.at[i]) for i, (a, b) in enumerate(copies)]
    for copy in copies:
        copy.start()
    source = lax.broadcasted_iota(jnp.int32, (emb, LANES), 0)
    target = lax.broadcasted_iota(jnp.int32, (emb, LANES), 1)
    column = ((target // OUT_COLS) * 2 + l_index) * 2 + c_index
    column = x_index * (emb // 2) + column * OUT_COLS + target % OUT_COLS
    pick = (target < h_count * OUT_COLS) & (source == column)
    pick = jnp.where(pick, 1.0, 0.0).astype(BF)
    for copy in copies[:9]:
        copy.wait()
    grads = grads_ref[:, :, :emb].reshape(8 * rows, emb)
    picked = jnp.dot(grads, pick, preferred_element_type=F32).astype(BF)
    loss = jnp.zeros((1, LANES), F32)
    for block in range(8):
        loss += jnp.sum(grads_ref[block, :, emb:].astype(F32), axis=0, keepdims=True)
    a, b, c = split3(jnp.sum(loss, axis=1, keepdims=True))
    spans = parts_of(hid, 2)
    for i, span in enumerate(spans):
        size = span.stop - span.start
        lane = lax.broadcasted_iota(jnp.int32, (size, LANES), 1)
        grad_hidden = lax.dot_general(wout_ref[span, :], grads, NT, preferred_element_type=F32)
        if i == 0:
            copies[9].wait()
        grad_pre = (grad_hidden * der_ref[span, :].astype(F32)).astype(BF)
        if i == 0:
            for copy in copies[10:]:
                copy.wait()
        total = jnp.dot(grad_pre, feats_ref[...], preferred_element_type=F32)
        outer = jnp.dot(hidden_ref[span, :], picked, preferred_element_type=F32)
        for h in range(h_count):
            moved = outer if h == 0 else pltpu.roll(outer, LANES - h * OUT_COLS, 1)
            value = jnp.where(lane < OUT_COLS, moved, total[:, h * LANES : (h + 1) * LANES])
            if i == 0:
                row = lax.broadcasted_iota(jnp.int32, (size, LANES), 0)
                extra = jnp.where(row == 0, a, jnp.where(row == 1, b, c))
                value = jnp.where((lane == LANES - 1) & (row < 3), extra, value)
            out_ref[h, span, :] = value.astype(BF)


def final_kernel(got_ref, in_ref, out_ref, loss_ref, *, batch_total):
    total = jnp.sum(got_ref[...].astype(F32), axis=0)
    turned = total.T
    in_rows = in_ref.shape[0]
    out_ref[...] = turned[:OUT_COLS]
    in_ref[...] = turned[OUT_COLS : OUT_COLS + in_rows]
    loss = jnp.sum(total[:3, LANES - 1 :], axis=0, keepdims=True) / (2.0 * batch_total)
    loss_ref[...] = loss


def ring(value, step):
    return lax.ppermute(value, "zh", [(i, (i - step) % 4) for i in range(4)])


def on_device(video_feats, text_feats, weight_in, weight_out, logit_scale):
    rows, d_in = video_feats.shape
    hid, emb = weight_out.shape
    mp_count = lax.axis_size(MP)
    h_count = lax.axis_size("zh")
    own_rows = rows // mp_count
    batch_total = rows * lax.axis_size(DP)
    where = [lax.axis_index(name) for name in ("x_lo", "zl", "core", MP, "zh")]
    where = jnp.stack(where).astype(jnp.int32)

    partial_value, pre_bf, text_emb = call(
        head_kernel, [((rows, emb), BF), ((hid, rows), BF), ((rows, emb), BF)], LIM[0],
        text_feats, video_feats, weight_in.T, weight_out, raw=True,
        scratch=[
            pltpu.VMEM((rows, emb), BF), pltpu.VMEM((rows, d_in), BF), pltpu.VMEM((hid, d_in), BF),
            pltpu.VMEM((hid, emb), BF), pltpu.VMEM((hid, rows), BF), pltpu.SemaphoreType.DMA((6,)),
        ],
    )
    got = exchange(partial_value.reshape(mp_count, own_rows, emb), MP)

    texts = [ring(text_emb, step) for step in (1, 2, 3)]
    feats = call(
        feats_kernel, [((2 * rows, h_count * LANES), BF)] * 4, LIM[1], where, video_feats, scalars=1
    )
    unit, inv_norm, video = call(
        unit_kernel,
        [((own_rows, emb), F32), ((own_rows, LANES), F32), ((8, own_rows, emb), BF)],
        LIM[2], got, after=(feats[0],),
    )
    give_l, give_x, give_xl, pre_bf = gate(inv_norm, feats[1], feats[2], feats[3], pre_bf)
    feats_x = swap(give_x, "x_lo")
    feats_l = swap(give_l, "zl")
    feats_xl = swap(swap(give_xl, "x_lo"), "zl")
    pre_l = swap(pre_bf, "zl")
    sides = [pre_bf, pre_l, swap(pre_bf, "x_lo"), swap(pre_l, "x_lo")]
    pre = [value for side in sides for value in (side, swap(side, "core"))]

    video_rows = exchange(video, CUBE)
    (cols,) = call(
        logits_kernel, [((4 * mp_count, 8, LANES), F32)], LIM[3],
        where, logit_scale, video_rows, text_emb, *texts, scalars=2,
        scratch=[pltpu.VMEM((8, LANES), F32)],
    )
    cols = exchange(cols, COLS)
    packed, logs = call(
        weights_kernel, [((8, own_rows, 2 * emb + LANES), BF), ((8, LANES), F32)], LIM[4],
        where, logit_scale, video_rows, text_emb, *texts, cols, scalars=2,
        scratch=[pltpu.VMEM((8, LANES), F32)],
    )
    back = exchange(packed, CUBE)
    (sent,) = call(
        functools.partial(proj_kernel, sharers=4 * mp_count),
        [((4 * mp_count, own_rows, emb + LANES), BF)], LIM[5],
        where, logit_scale, back, unit, inv_norm, text_emb.reshape(mp_count, own_rows, emb), logs,
        scalars=2, after=(feats_x, feats_l, feats_xl, *pre[1:]),
    )
    grads = exchange(sent, SPREAD).reshape(4, rows, emb + LANES)
    other = swap(grads, "core")
    feats_q = [
        value for side in (feats[0], feats_l, feats_x, feats_xl) for value in (side, swap(side, "core"))
    ]
    hidden_all, der_all = call(
        gelu_kernel, [((hid, 8 * rows), BF), ((hid, 8 * rows), BF)], LIM[6], *pre
    )
    (packed,) = call(
        grads_kernel, [((h_count, hid, LANES), BF)], LIM[7],
        where, grads, other, weight_out, der_all, hidden_all, *feats_q, scalars=1, raw=True,
        scratch=[
            pltpu.VMEM((8, rows, emb + LANES), BF), pltpu.VMEM((hid, emb), BF),
            pltpu.VMEM((hid, 8 * rows), BF), pltpu.VMEM((hid, 8 * rows), BF),
            pltpu.VMEM((8 * rows, h_count * LANES), BF), pltpu.SemaphoreType.DMA((19,)),
        ],
    )
    final = exchange(packed, "zh")
    in_rows = d_in // lax.axis_size(DP)
    grad_in, grad_out, loss = call(
        functools.partial(final_kernel, batch_total=batch_total),
        [((in_rows, hid), F32), ((OUT_COLS, hid), F32), ((1, 1), F32)],
        LIM[8], final,
    )
    return (loss.reshape(1), grad_in, grad_out.T)


def solution(mesh):
    fine = Mesh(mesh.devices.reshape(2, 4, 2, 2, mesh.devices.shape[1] // 2, 2), DP + MP)
    in_specs = (P(DP, None), P(DP, None), P(None, MP), P(MP, None), P())
    out_specs = (P(), P(DP, MP), P(MP, DP))
    return jax.shard_map(
        on_device, mesh=fine, in_specs=in_specs, out_specs=out_specs, check_vma=False
    )
```

time: 182 us -> 219 us (1.20)
  Pallas kernels: 16.3 us -> 43.3 us
  starting transfers between devices: 31.3 us -> 56.9 us
  blocking collectives: 61.9 us -> 50.9 us
  waiting for transfers between devices: 50.5 us -> 58.8 us
  local copies, waits for them, and re-layouts: 13.6 us -> 6.84 us
  matrix products: 6.61 us -> 0 us
    pallas_call x9 -> x10, Pallas kernels: 16.3 us -> 43.3 us  [the longest x9 43.3 us: call(): pl.pallas_call(body, grid=(1,), out_shape=[jax.ShapeDtypeStruct(s, d) for...]
    ppermute x0 -> x3, waiting for transfers between devices: none -> 18.4 us  [ring(): return lax.ppermute(value, 'zh', [(i, (i - step) % 4) for i in range(4)])]
    all_to_all x4, waiting for transfers between devices: 26.2 us -> 8.6 us  [exchange(): return lax.all_to_all(value, axis, 0, 0)]
    all_to_all x2, blocking collectives: 61.9 us -> 50.9 us  [exchange(): return lax.all_to_all(value, axis, 0, 0)]
    ppermute x9 -> x16, starting transfers between devices: 7.96 us -> 18.4 us  [swap(): return lax.ppermute(value, axis, [(0, 1), (1, 0)])]
    ppermute x0 -> x3, starting transfers between devices: none -> 9.28 us  [ring(): return lax.ppermute(value, 'zh', [(i, (i - step) % 4) for i in range(4)])]
    ppermute x9 -> x16, waiting for transfers between devices: 24.2 us -> 31.8 us  [swap(): return lax.ppermute(value, axis, [(0, 1), (1, 0)])]
    dot_general x2 -> x0, matrix products: 6.61 us -> none  [the longest x1 5.36 us: on_device(): lax.dot_general(weight_in, video_feats, (((0,), (1,)), ((), ())), preferr...]
  transfers between devices with their start and end apart: 13 -> 23, of which waited for: 6 -> 7; matrix products, arithmetic and copies ran while one was open for 2% -> 0% of each run, Pallas kernels for 4% -> 8%
where the time goes in v3:
time: 219 us; the launch traced here: 218 us
  waiting for transfers between devices  58.8 us (27%)
  starting transfers between devices  56.9 us (26%)
  blocking collectives  50.9 us (23%)
  Pallas kernels  43.3 us (20%)
  local copies, waits for them, and re-layouts  6.84 us (3%)
    all_to_all x2, blocking collectives, exchange(): return lax.all_to_all(value, axis, 0, 0)  50.9 us
    pallas_call x9, Pallas kernels, call(): pl.pallas_call(body, grid=(1,), out_shape=[jax.ShapeDtypeStruct(s, d) for...  43.3 us
    ppermute x16, waiting for transfers between devices, swap(): return lax.ppermute(value, axis, [(0, 1), (1, 0)])  31.8 us
    all_to_all x4, starting transfers between devices, exchange(): return lax.all_to_all(value, axis, 0, 0)  29.2 us
    ppermute x16, starting transfers between devices, swap(): return lax.ppermute(value, axis, [(0, 1), (1, 0)])  18.4 us
    ppermute x3, waiting for transfers between devices, ring(): return lax.ppermute(value, 'zh', [(i, (i - step) % 4) for i in range(4)])  18.4 us
    ppermute x3, starting transfers between devices, ring(): return lax.ppermute(value, 'zh', [(i, (i - step) % 4) for i in range(4)])  9.28 us
    all_to_all x4, waiting for transfers between devices, exchange(): return lax.all_to_all(value, axis, 0, 0)  8.6 us
  transfers between devices with their start and end apart: 23, of which 7 were waited for; matrix products, arithmetic and copies ran while one was open for 0% of the time, Pallas kernels for 8%

profile of v3, /device:TPU:1, one launch (start us, length us, event | category | flops | bytes accessed | tf_op | source)
XLA Modules:
  0.0 218.5 jit_solution(14746772946948547348)
XLA Ops:
  0.6 6.7 %shard_map.76 = (bf16[256,512]{1,0:T(8,128)(2,1)}, bf16[800,256]{1,0:T(8,128)(2,1)}, bf16[256,512]{1,0:T(8,128)(2,1)}) custom-call(bf16[256,512]{1,0:T(8,128)(2,1)} %refs_0_.1, bf16[256,3200]{1,0:T(8,128)(2,1)} %refs_1_.6, bf16[800,3200]{1,0:T(8,128)(2,1)} %bitcast.13, bf16[800,512]{1,0:T(8,128)(2,1)} %refs_3_.3), custom_call_target="tpu_custom_call" | custom-call | flops 1024 | bytes 1024 | tf_op jit(solution)/shard_map/pallas_call | solution.py:80
  7.4 7.6 %all-to-all-start = ((bf16[8,32,512]{2,1,0:T(8,128)(2,1)}), bf16[8,32,512]{2,1,0:T(8,128)(2,1)S(1)}, u32[]{:S(2)}, u32[]{:S(2)}) async-start(bf16[8,32,512]{2,1,0:T(8,128)(2,1)} %bitcast.15), calls=%async_computation | async-start | bytes 524288 | tf_op jit(solution)/shard_map/all_to_all | solution.py:46
  15.0 0.6 stack.23.refs_0_
  15.6 4.4 %shard_map.77 = (bf16[512,512]{1,0:T(8,128)(2,1)}, bf16[512,512]{1,0:T(8,128)(2,1)}, bf16[512,512]{1,0:T(8,128)(2,1)}, bf16[512,512]{1,0:T(8,128)(2,1)}) custom-call(s32[5]{0:T(128)} %stack.23.refs_0_, bf16[256,3200]{1,0:T(8,128)(2,1)} %refs_1_.6), custom_call_target="tpu_custom_call" | custom-call | flops 1024 | bytes 1024 | tf_op jit(solution)/shard_map/pallas_call | solution.py:80
  20.0 2.7 %all-to-all-done.refs_0_ = bf16[8,32,512]{2,1,0:T(8,128)(2,1)S(1)} async-done(((bf16[8,32,512]{2,1,0:T(8,128)(2,1)}), bf16[8,32,512]{2,1,0:T(8,128)(2,1)S(1)}, u32[]{:S(2)}, u32[]{:S(2)}) %all-to-all-start) | async-done | bytes 262176 | tf_op jit(solution)/shard_map/all_to_all | solution.py:46
  22.6 1.0 copy-done
  23.7 0.9 shard_map.78
  24.6 0.6 copy-done.2
  25.2 0.6 copy-done.3
  25.8 5.4 %all-to-all-start.1 = ((bf16[8,32,512]{2,1,0:T(8,128)(2,1)}), bf16[8,32,512]{2,1,0:T(8,128)(2,1)S(1)}, u32[]{:S(2)}, u32[]{:S(2)}) async-start(bf16[8,32,512]{2,1,0:T(8,128)(2,1)} %get-tuple-element.26), calls=%async_computation.1 | async-start | bytes 524288 | tf_op jit(solution)/shard_map/all_to_all | solution.py:46
  31.2 6.0 %collective-permute-start = (bf16[256,512]{1,0:T(8,128)(2,1)S(1)}, bf16[256,512]{1,0:T(8,128)(2,1)S(1)}, u32[]{:S(2)}, u32[]{:S(2)}) collective-permute-start(bf16[256,512]{1,0:T(8,128)(2,1)S(1)} %copy-done.6), channel_id=1, source_target_pairs={{0,96},{32,0},{64,32},{96,64},{1,97},{33,1},{65,33},{97,65},{2,98}... | collective-permute-start | bytes 786440 | tf_op jit(solution)/shard_map/ppermute | solution.py:327
  37.2 1.0 collective-permute-start.1
  38.2 2.3 %collective-permute-start.2 = (bf16[256,512]{1,0:T(8,128)(2,1)S(1)}, bf16[256,512]{1,0:T(8,128)(2,1)S(1)}, u32[]{:S(2)}, u32[]{:S(2)}) collective-permute-start(bf16[256,512]{1,0:T(8,128)(2,1)S(1)} %copy-done.6), channel_id=1, source_target_pairs={{0,32},{32,64},{64,96},{96,0},{1,33},{33,65},{65,97},{97,1},{2,34}... | collective-permute-start | bytes 786440 | tf_op jit(solution)/shard_map/ppermute | solution.py:327
  41.1 18.4 %collective-permute-done.refs_4_ = bf16[256,512]{1,0:T(8,128)(2,1)S(1)} collective-permute-done((bf16[256,512]{1,0:T(8,128)(2,1)S(1)}, bf16[256,512]{1,0:T(8,128)(2,1)S(1)}, u32[]{:S(2)}, u32[]{:S(2)}) %collective-permute-start) | collective-permute-done | bytes 262176 | tf_op jit(solution)/shard_map/ppermute | solution.py:327
  59.5 0.0 collective-permute-done.1.refs_5_
  59.5 0.0 collective-permute-done.2.refs_6_
  59.5 0.0 all-to-all-done.1.refs_2_
  59.5 0.7 copy-done.20
  60.2 0.1 copy-done.21
  60.3 0.1 copy-done.22
  60.4 0.7 copy-done.7
  61.1 3.1 %shard_map.79 = f32[32,8,128]{2,1,0:T(8,128)} custom-call(s32[5]{0:T(128)} %stack.23.refs_0_, f32[1]{0:T(128)S(6)} %copy.16.refs_1_, bf16[8,32,512]{2,1,0:T(8,128)(2,1)} %copy-done.7, bf16[256,512]{1,0:T(8,128)(2,1)} %get-tuple-element.27.refs_3_, bf16[256,512]{1,0:T(8,128)(2,1)} %copy-done.20, bf16[256,512]{1,0:T(8,128)(2,1)} %copy-done.21, ...), custom_call_target="tpu_custom_call" | custom-call | flops 1024 | bytes 1024 | tf_op jit(solution)/shard_map/pallas_call | solution.py:80
  64.2 7.7 %all-to-all-start.2 = ((f32[32,8,128]{2,1,0:T(8,128)}), f32[32,8,128]{2,1,0:T(8,128)S(1)}, u32[]{:S(2)}, u32[]{:S(2)}) async-start(f32[32,8,128]{2,1,0:T(8,128)} %shard_map.79), calls=%async_computation.2 | async-start | bytes 262144 | tf_op jit(solution)/shard_map/all_to_all | solution.py:46
  71.9 4.4 %collective-permute-start.8 = (bf16[800,256]{1,0:T(8,128)(2,1)}, bf16[800,256]{1,0:T(8,128)(2,1)S(1)}, u32[]{:S(2)}, u32[]{:S(2)}) collective-permute-start(bf16[800,256]{1,0:T(8,128)(2,1)} %get-tuple-element.39.refs_0_), channel_id=1, source_target_pairs={{0,16},{16,0},{1,17},{17,1},{2,18},{18,2},{3,19},{19,3},{4,20},{20... | collective-permute-start | bytes 1228808 | tf_op jit(solution)/shard_map/ppermute | solution.py:42
  76.3 0.8 collective-permute-start.5
  77.1 5.9 %all-to-all-done.2.refs_7_ = f32[32,8,128]{2,1,0:T(8,128)S(1)} async-done(((f32[32,8,128]{2,1,0:T(8,128)}), f32[32,8,128]{2,1,0:T(8,128)S(1)}, u32[]{:S(2)}, u32[]{:S(2)}) %all-to-all-start.2) | async-done | bytes 131104 | tf_op jit(solution)/shard_map/all_to_all | solution.py:46
  83.0 0.7 copy-done.24
  83.7 4.3 %shard_map.80 = (bf16[8,32,1152]{2,1,0:T(8,128)(2,1)}, f32[8,128]{1,0:T(8,128)}) custom-call(s32[5]{0:T(128)} %stack.23.refs_0_, f32[1]{0:T(128)S(6)} %copy.16.refs_1_, bf16[8,32,512]{2,1,0:T(8,128)(2,1)} %copy-done.7, bf16[256,512]{1,0:T(8,128)(2,1)} %get-tuple-element.27.refs_3_, bf16[256,512]{1,0:T(8,128)(2,1)} %copy-done.20, ...), custom_call_target="tpu_custom_call" | custom-call | flops 1024 | bytes 1024 | tf_op jit(solution)/shard_map/pallas_call | solution.py:80
  88.0 8.5 %all-to-all-start.3 = ((bf16[8,32,1152]{2,1,0:T(8,128)(2,1)}), bf16[8,32,1152]{2,1,0:T(8,128)(2,1)S(1)}, u32[]{:S(2)}, u32[]{:S(2)}) async-start(bf16[8,32,1152]{2,1,0:T(8,128)(2,1)} %get-tuple-element.28), calls=%async_computation.3 | async-start | bytes 1179648 | tf_op jit(solution)/shard_map/all_to_all | solution.py:46
  96.4 1.4 collective-permute-start.10
  97.8 0.1 collective-permute-start.3
  97.9 0.6 collective-permute-start.7
  98.5 0.0 collective-permute-done.8.refs_11_.refs_2_
  98.5 1.7 collective-permute-start.12
  100.2 13.7 %collective-permute-done.10.refs_13_.refs_4_ = bf16[800,256]{1,0:T(8,128)(2,1)S(1)} collective-permute-done((bf16[800,256]{1,0:T(8,128)(2,1)}, bf16[800,256]{1,0:T(8,128)(2,1)S(1)}, u32[]{:S(2)}, u32[]{:S(2)}) %collective-permute-start.10) | collective-permute-done | bytes 409632 | tf_op jit(solution)/shard_map/ppermute | solution.py:42
  113.9 1.6 collective-permute-start.4
  115.5 0.0 collective-permute-done.5
  115.5 0.3 collective-permute-start.6
  115.8 1.5 collective-permute-start.11
  117.3 7.8 %collective-permute-done.3.refs_7_.refs_10_ = bf16[512,512]{1,0:T(8,128)(2,1)S(1)} collective-permute-done((bf16[512,512]{1,0:T(8,128)(2,1)}, bf16[512,512]{1,0:T(8,128)(2,1)S(1)}, u32[]{:S(2)}, u32[]{:S(2)}) %collective-permute-start.3) | collective-permute-done | bytes 524320 | tf_op jit(solution)/shard_map/ppermute | solution.py:42
  125.1 1.3 collective-permute-start.9
  126.5 7.4 %collective-permute-done.12.refs_15_.refs_6_ = bf16[800,256]{1,0:T(8,128)(2,1)S(1)} collective-permute-done((bf16[800,256]{1,0:T(8,128)(2,1)S(1)}, bf16[800,256]{1,0:T(8,128)(2,1)S(1)}, u32[]{:S(2)}, u32[]{:S(2)}) %collective-permute-start.12) | collective-permute-done | bytes 409632 | tf_op jit(solution)/shard_map/ppermute | solution.py:42
  133.9 0.9 collective-permute-start.13
  134.8 0.0 collective-permute-done.4.refs_8_
  134.8 0.0 collective-permute-done.9.refs_12_.refs_3_
  134.8 2.8 %collective-permute-done.6.refs_9_.refs_12_ = bf16[512,512]{1,0:T(8,128)(2,1)S(1)} collective-permute-done((bf16[512,512]{1,0:T(8,128)(2,1)}, bf16[512,512]{1,0:T(8,128)(2,1)S(1)}, u32[]{:S(2)}, u32[]{:S(2)}) %collective-permute-start.6) | collective-permute-done | bytes 524320 | tf_op jit(solution)/shard_map/ppermute | solution.py:42
  137.7 0.0 all-to-all-done.3.refs_2_
  137.7 0.7 copy-done.12
  138.5 0.2 copy-done.5
  138.7 3.3 %shard_map.82 = bf16[32,32,640]{2,1,0:T(8,128)(2,1)} custom-call(s32[5]{0:T(128)} %stack.23.refs_0_, f32[1]{0:T(128)S(6)} %copy.16.refs_1_, bf16[8,32,1152]{2,1,0:T(8,128)(2,1)} %copy-done.5, f32[32,512]{1,0:T(8,128)} %copy-done.2, f32[32,128]{1,0:T(8,128)} %copy-done.3, bf16[8,32,512]{2,1,0:T(8,128)(2,1)} %bitcast.14, f32[8,128]{1,0:T(8,128)} %get-tuple-element.31.refs_6_, ...), custom_call_target="tpu_custom_call" | custom-call | flops 1024 | bytes 1024 | tf_op jit(solution)/shard_map/pallas_call | solution.py:80
  142.0 25.2 %all_to_all.30 = bf16[32,32,640]{2,1,0:T(8,128)(2,1)S(1)} all-to-all(bf16[32,32,640]{2,1,0:T(8,128)(2,1)} %shard_map.82), channel_id=1, replica_groups=mesh['x_lo'=2,'zh'=4,'zl'=2,'core'=2,'y'=4,'x_hi'=2] {'x_lo','zl','y','x..., dimensions={0} | all-to-all | bytes 2621440 | tf_op jit(solution)/shard_map/all_to_all | solution.py:46
  167.2 2.8 %collective-permute-start.14 = (bf16[4,256,640]{2,1,0:T(8,128)(2,1)S(1)}, bf16[4,256,640]{2,1,0:T(8,128)(2,1)}, u32[]{:S(2)}, u32[]{:S(2)}) collective-permute-start(bf16[4,256,640]{2,1,0:T(8,128)(2,1)S(1)} %bitcast.11), channel_id=1, source_target_pairs={{0,8},{8,0},{1,9},{9,1},{2,10},{10,2},{3,11},{11,3},{4,12},{12,4},... | collective-permute-start | bytes 3932168 | tf_op jit(solution)/shard_map/ppermute | solution.py:42
  170.1 0.1 collective-permute-start.15
  170.2 0.4 collective-permute-start.16
  170.6 0.1 collective-permute-start.17
  170.7 0.4 collective-permute-start.18
  171.1 9.3 %shard_map.83 = (bf16[800,2048]{1,0:T(8,128)(2,1)}, bf16[800,2048]{1,0:T(8,128)(2,1)}) custom-call(bf16[800,256]{1,0:T(8,128)(2,1)} %get-tuple-element.39.refs_0_, bf16[800,256]{1,0:T(8,128)(2,1)} %copy-done.16, bf16[800,256]{1,0:T(8,128)(2,1)} %copy-done.14, bf16[800,256]{1,0:T(8,128)(2,1)} %copy-done.19, bf16[800,256]{1,0:T(8,128)(2,1)} %copy-done.15, ...), custom_call_target="tpu_custom_call" | custom-call | flops 1024 | bytes 1024 | tf_op jit(solution)/shard_map/pallas_call | solution.py:80
  180.4 0.0 collective-permute-done.16.refs_9_
  180.4 0.0 collective-permute-done.17.refs_11_
  180.4 0.0 collective-permute-done.14.refs_2_
  180.4 0.8 copy-done.23
  181.2 10.4 %shard_map.84 = bf16[4,800,128]{2,1,0:T(8,128)(2,1)} custom-call(s32[5]{0:T(128)} %stack.23.refs_0_, bf16[4,256,640]{2,1,0:T(8,128)(2,1)} %bitcast.12, bf16[4,256,640]{2,1,0:T(8,128)(2,1)} %collective-permute-done.14.refs_2_, bf16[800,512]{1,0:T(8,128)(2,1)} %refs_3_.3, bf16[800,2048]{1,0:T(8,128)(2,1)} %get-tuple-element.40.refs_4_, ...), custom_call_target="tpu_custom_call" | custom-call | flops 1024 | bytes 1024 | tf_op jit(solution)/shard_map/pallas_call | solution.py:80
  191.6 25.6 %all_to_all.31.refs_0_ = bf16[4,800,128]{2,1,0:T(8,128)(2,1)S(1)} all-to-all(bf16[4,800,128]{2,1,0:T(8,128)(2,1)} %shard_map.84), channel_id=1, replica_groups=mesh['x_lo'=2,'zh'=4,'zl'=2,'core'=2,'y'=4,'x_hi'=2] {'zh'}, dimensions={0} | all-to-all | bytes 1638400 | tf_op jit(solution)/shard_map/all_to_all | solution.py:46
  217.2 1.0 shard_map.85
  (47 shorter events, 0.1 us)
Async XLA Ops:
  7.4 23.8 %copy-start.6 = (bf16[256,512]{1,0:T(8,128)(2,1)S(1)}, bf16[256,512]{1,0:T(8,128)(2,1)}, u32[]{:S(2)}) copy-start(bf16[256,512]{1,0:T(8,128)(2,1)} %get-tuple-element.27.refs_3_) | copy-start | bytes 786436
  7.4 15.3 %all-to-all-start = ((bf16[8,32,512]{2,1,0:T(8,128)(2,1)}), bf16[8,32,512]{2,1,0:T(8,128)(2,1)S(1)}, u32[]{:S(2)}, u32[]{:S(2)}) async-start(bf16[8,32,512]{2,1,0:T(8,128)(2,1)} %bitcast.15), calls=%async_computation | async-start | bytes 524288 | tf_op jit(solution)/shard_map/all_to_all | solution.py:46
  22.6 1.0 copy-start
  24.6 0.6 copy-start.2
  25.2 0.6 copy-start.3
  25.8 33.7 %all-to-all-start.1 = ((bf16[8,32,512]{2,1,0:T(8,128)(2,1)}), bf16[8,32,512]{2,1,0:T(8,128)(2,1)S(1)}, u32[]{:S(2)}, u32[]{:S(2)}) async-start(bf16[8,32,512]{2,1,0:T(8,128)(2,1)} %get-tuple-element.26), calls=%async_computation.1 | async-start | bytes 524288 | tf_op jit(solution)/shard_map/all_to_all | solution.py:46
  31.2 28.3 %collective-permute-start = (bf16[256,512]{1,0:T(8,128)(2,1)S(1)}, bf16[256,512]{1,0:T(8,128)(2,1)S(1)}, u32[]{:S(2)}, u32[]{:S(2)}) collective-permute-start(bf16[256,512]{1,0:T(8,128)(2,1)S(1)} %copy-done.6), channel_id=1, source_target_pairs={{0,96},{32,0},{64,32},{96,64},{1,97},{33,1},{65,33},{97,65},{2,98}... | collective-permute-start | bytes 786440 | tf_op jit(solution)/shard_map/ppermute | solution.py:327
  37.2 22.3 %collective-permute-start.1 = (bf16[256,512]{1,0:T(8,128)(2,1)S(1)}, bf16[256,512]{1,0:T(8,128)(2,1)S(1)}, u32[]{:S(2)}, u32[]{:S(2)}) collective-permute-start(bf16[256,512]{1,0:T(8,128)(2,1)S(1)} %copy-done.6), channel_id=1, source_target_pairs={{0,64},{32,96},{64,0},{96,32},{1,65},{33,97},{65,1},{97,33},{2,66}... | collective-permute-start | bytes 786440 | tf_op jit(solution)/shard_map/ppermute | solution.py:327
  38.2 21.3 %collective-permute-start.2 = (bf16[256,512]{1,0:T(8,128)(2,1)S(1)}, bf16[256,512]{1,0:T(8,128)(2,1)S(1)}, u32[]{:S(2)}, u32[]{:S(2)}) collective-permute-start(bf16[256,512]{1,0:T(8,128)(2,1)S(1)} %copy-done.6), channel_id=1, source_target_pairs={{0,32},{32,64},{64,96},{96,0},{1,33},{33,65},{65,97},{97,1},{2,34}... | collective-permute-start | bytes 786440 | tf_op jit(solution)/shard_map/ppermute | solution.py:327
  59.5 0.7 copy-start.20
  59.5 0.8 copy-start.21
  59.5 0.9 copy-start.22
  60.4 0.7 copy-start.7
  64.2 18.8 %all-to-all-start.2 = ((f32[32,8,128]{2,1,0:T(8,128)}), f32[32,8,128]{2,1,0:T(8,128)S(1)}, u32[]{:S(2)}, u32[]{:S(2)}) async-start(f32[32,8,128]{2,1,0:T(8,128)} %shard_map.79), calls=%async_computation.2 | async-start | bytes 262144 | tf_op jit(solution)/shard_map/all_to_all | solution.py:46
  71.9 42.0 %copy-start.25 = (bf16[512,512]{1,0:T(8,128)(2,1)S(1)}, bf16[512,512]{1,0:T(8,128)(2,1)}, u32[]{:S(2)}) copy-start(bf16[512,512]{1,0:T(8,128)(2,1)} %get-tuple-element.37) | copy-start | bytes 1572868
  71.9 26.6 %collective-permute-start.8 = (bf16[800,256]{1,0:T(8,128)(2,1)}, bf16[800,256]{1,0:T(8,128)(2,1)S(1)}, u32[]{:S(2)}, u32[]{:S(2)}) collective-permute-start(bf16[800,256]{1,0:T(8,128)(2,1)} %get-tuple-element.39.refs_0_), channel_id=1, source_target_pairs={{0,16},{16,0},{1,17},{17,1},{2,18},{18,2},{3,19},{19,3},{4,20},{20... | collective-permute-start | bytes 1228808 | tf_op jit(solution)/shard_map/ppermute | solution.py:42
  76.3 39.2 %collective-permute-start.5 = (bf16[512,512]{1,0:T(8,128)(2,1)}, bf16[512,512]{1,0:T(8,128)(2,1)}, u32[]{:S(2)}, u32[]{:S(2)}) collective-permute-start(bf16[512,512]{1,0:T(8,128)(2,1)} %get-tuple-element.38), channel_id=1, source_target_pairs={{0,128},{128,0},{1,129},{129,1},{2,130},{130,2},{3,131},{131,3},{4... | collective-permute-start | bytes 1572872 | tf_op jit(solution)/shard_map/ppermute | solution.py:42
  83.0 0.7 copy-start.24
  88.0 49.7 %all-to-all-start.3 = ((bf16[8,32,1152]{2,1,0:T(8,128)(2,1)}), bf16[8,32,1152]{2,1,0:T(8,128)(2,1)S(1)}, u32[]{:S(2)}, u32[]{:S(2)}) async-start(bf16[8,32,1152]{2,1,0:T(8,128)(2,1)} %get-tuple-element.28), calls=%async_computation.3 | async-start | bytes 1179648 | tf_op jit(solution)/shard_map/all_to_all | solution.py:46
  96.4 17.5 %collective-permute-start.10 = (bf16[800,256]{1,0:T(8,128)(2,1)}, bf16[800,256]{1,0:T(8,128)(2,1)S(1)}, u32[]{:S(2)}, u32[]{:S(2)}) collective-permute-start(bf16[800,256]{1,0:T(8,128)(2,1)} %get-tuple-element.39.refs_0_), channel_id=1, source_target_pairs={{0,128},{128,0},{1,129},{129,1},{2,130},{130,2},{3,131},{131,3},{4... | collective-permute-start | bytes 1228808 | tf_op jit(solution)/shard_map/ppermute | solution.py:42
  97.8 27.3 %collective-permute-start.3 = (bf16[512,512]{1,0:T(8,128)(2,1)}, bf16[512,512]{1,0:T(8,128)(2,1)S(1)}, u32[]{:S(2)}, u32[]{:S(2)}) collective-permute-start(bf16[512,512]{1,0:T(8,128)(2,1)} %get-tuple-element.36), channel_id=1, source_target_pairs={{0,128},{128,0},{1,129},{129,1},{2,130},{130,2},{3,131},{131,3},{4... | collective-permute-start | bytes 1572872 | tf_op jit(solution)/shard_map/ppermute | solution.py:42
  97.9 17.9 %collective-permute-start.7 = (bf16[800,256]{1,0:T(8,128)(2,1)}, bf16[800,256]{1,0:T(8,128)(2,1)S(1)}, u32[]{:S(2)}, u32[]{:S(2)}) collective-permute-start(bf16[800,256]{1,0:T(8,128)(2,1)} %get-tuple-element.39.refs_0_), channel_id=1, source_target_pairs={{0,8},{8,0},{1,9},{9,1},{2,10},{10,2},{3,11},{11,3},{4,12},{12,4},... | collective-permute-start | bytes 1228808 | tf_op jit(solution)/shard_map/ppermute | solution.py:42
  98.5 39.2 %copy-start.14 = (bf16[800,256]{1,0:T(8,128)(2,1)}, bf16[800,256]{1,0:T(8,128)(2,1)S(1)}, u32[]{:S(2)}) copy-start(bf16[800,256]{1,0:T(8,128)(2,1)S(1)} %collective-permute-done.8.refs_11_.refs_2_) | copy-start | bytes 1228804
  98.5 35.4 %collective-permute-start.12 = (bf16[800,256]{1,0:T(8,128)(2,1)S(1)}, bf16[800,256]{1,0:T(8,128)(2,1)S(1)}, u32[]{:S(2)}, u32[]{:S(2)}) collective-permute-start(bf16[800,256]{1,0:T(8,128)(2,1)S(1)} %collective-permute-done.8.refs_11_.refs_2_), channel_id=1, source_target_pairs={{0,128},{128,0},{1,129},{129,1},{2,130},{130,2},{3,131},{131,3},{4... | collective-permute-start | bytes 1228808 | tf_op jit(solution)/shard_map/ppermute | solution.py:42
  113.9 23.8 %copy-start.15 = (bf16[800,256]{1,0:T(8,128)(2,1)}, bf16[800,256]{1,0:T(8,128)(2,1)S(1)}, u32[]{:S(2)}) copy-start(bf16[800,256]{1,0:T(8,128)(2,1)S(1)} %collective-permute-done.10.refs_13_.refs_4_) | copy-start | bytes 1228804
  113.9 20.9 %collective-permute-start.4 = (bf16[512,512]{1,0:T(8,128)(2,1)S(1)}, bf16[512,512]{1,0:T(8,128)(2,1)S(1)}, u32[]{:S(2)}, u32[]{:S(2)}) collective-permute-start(bf16[512,512]{1,0:T(8,128)(2,1)S(1)} %copy-done.25), channel_id=1, source_target_pairs={{0,16},{16,0},{1,17},{17,1},{2,18},{18,2},{3,19},{19,3},{4,20},{20... | collective-permute-start | bytes 1572872 | tf_op jit(solution)/shard_map/ppermute | solution.py:42
  115.5 22.1 %collective-permute-start.6 = (bf16[512,512]{1,0:T(8,128)(2,1)}, bf16[512,512]{1,0:T(8,128)(2,1)S(1)}, u32[]{:S(2)}, u32[]{:S(2)}) collective-permute-start(bf16[512,512]{1,0:T(8,128)(2,1)} %collective-permute-done.5), channel_id=1, source_target_pairs={{0,16},{16,0},{1,17},{17,1},{2,18},{18,2},{3,19},{19,3},{4,20},{20... | collective-permute-start | bytes 1572872 | tf_op jit(solution)/shard_map/ppermute | solution.py:42
  115.8 21.9 %copy-start.16 = (bf16[800,256]{1,0:T(8,128)(2,1)}, bf16[800,256]{1,0:T(8,128)(2,1)S(1)}, u32[]{:S(2)}) copy-start(bf16[800,256]{1,0:T(8,128)(2,1)S(1)} %collective-permute-done.7.refs_10_.refs_1_) | copy-start | bytes 1228804
  115.8 19.0 %collective-permute-start.11 = (bf16[800,256]{1,0:T(8,128)(2,1)S(1)}, bf16[800,256]{1,0:T(8,128)(2,1)S(1)}, u32[]{:S(2)}, u32[]{:S(2)}) collective-permute-start(bf16[800,256]{1,0:T(8,128)(2,1)S(1)} %collective-permute-done.10.refs_13_.refs_4_), channel_id=1, source_target_pairs={{0,8},{8,0},{1,9},{9,1},{2,10},{10,2},{3,11},{11,3},{4,12},{12,4},... | collective-permute-start | bytes 1228808 | tf_op jit(solution)/shard_map/ppermute | solution.py:42
  125.1 12.6 %copy-start.8 = (bf16[512,512]{1,0:T(8,128)(2,1)}, bf16[512,512]{1,0:T(8,128)(2,1)S(1)}, u32[]{:S(2)}) copy-start(bf16[512,512]{1,0:T(8,128)(2,1)S(1)} %collective-permute-done.3.refs_7_.refs_10_) | copy-start | bytes 1572868
  125.1 9.7 %collective-permute-start.9 = (bf16[800,256]{1,0:T(8,128)(2,1)S(1)}, bf16[800,256]{1,0:T(8,128)(2,1)S(1)}, u32[]{:S(2)}, u32[]{:S(2)}) collective-permute-start(bf16[800,256]{1,0:T(8,128)(2,1)S(1)} %collective-permute-done.8.refs_11_.refs_2_), channel_id=1, source_target_pairs={{0,8},{8,0},{1,9},{9,1},{2,10},{10,2},{3,11},{11,3},{4,12},{12,4},... | collective-permute-start | bytes 1228808 | tf_op jit(solution)/shard_map/ppermute | solution.py:42
  133.9 3.8 %copy-start.17 = (bf16[800,256]{1,0:T(8,128)(2,1)}, bf16[800,256]{1,0:T(8,128)(2,1)S(1)}, u32[]{:S(2)}) copy-start(bf16[800,256]{1,0:T(8,128)(2,1)S(1)} %collective-permute-done.12.refs_15_.refs_6_) | copy-start | bytes 1228804
  133.9 3.8 %collective-permute-start.13 = (bf16[800,256]{1,0:T(8,128)(2,1)S(1)}, bf16[800,256]{1,0:T(8,128)(2,1)}, u32[]{:S(2)}, u32[]{:S(2)}) collective-permute-start(bf16[800,256]{1,0:T(8,128)(2,1)S(1)} %collective-permute-done.12.refs_15_.refs_6_), channel_id=1, source_target_pairs={{0,8},{8,0},{1,9},{9,1},{2,10},{10,2},{3,11},{11,3},{4,12},{12,4},... | collective-permute-start | bytes 1228808 | tf_op jit(solution)/shard_map/ppermute | solution.py:42
  134.8 3.0 %copy-start.10 = (bf16[512,512]{1,0:T(8,128)(2,1)}, bf16[512,512]{1,0:T(8,128)(2,1)S(1)}, u32[]{:S(2)}) copy-start(bf16[512,512]{1,0:T(8,128)(2,1)S(1)} %collective-permute-done.4.refs_8_) | copy-start | bytes 1572868
  134.8 2.9 %copy-start.18 = (bf16[800,256]{1,0:T(8,128)(2,1)}, bf16[800,256]{1,0:T(8,128)(2,1)S(1)}, u32[]{:S(2)}) copy-start(bf16[800,256]{1,0:T(8,128)(2,1)S(1)} %collective-permute-done.11.refs_14_.refs_5_) | copy-start | bytes 1228804
  134.8 2.9 %copy-start.19 = (bf16[800,256]{1,0:T(8,128)(2,1)}, bf16[800,256]{1,0:T(8,128)(2,1)S(1)}, u32[]{:S(2)}) copy-start(bf16[800,256]{1,0:T(8,128)(2,1)S(1)} %collective-permute-done.9.refs_12_.refs_3_) | copy-start | bytes 1228804
  137.7 0.8 copy-start.12
  137.7 1.0 copy-start.5
  142.0 28.1 %copy-start.1 = (bf16[512,512]{1,0:T(8,128)(2,1)S(1)}, bf16[512,512]{1,0:T(8,128)(2,1)}, u32[]{:S(2)}) copy-start(bf16[512,512]{1,0:T(8,128)(2,1)} %get-tuple-element.25.refs_1_.refs_6_) | copy-start | bytes 1572868
  142.0 28.2 %copy-start.11 = (bf16[512,512]{1,0:T(8,128)(2,1)S(1)}, bf16[512,512]{1,0:T(8,128)(2,1)}, u32[]{:S(2)}) copy-start(bf16[512,512]{1,0:T(8,128)(2,1)} %copy-done.10) | copy-start | bytes 1572868
  142.0 28.6 %copy-start.9 = (bf16[512,512]{1,0:T(8,128)(2,1)S(1)}, bf16[512,512]{1,0:T(8,128)(2,1)}, u32[]{:S(2)}) copy-start(bf16[512,512]{1,0:T(8,128)(2,1)} %copy-done.8) | copy-start | bytes 1572868
  142.0 28.7 %copy-start.13 = (bf16[512,512]{1,0:T(8,128)(2,1)S(1)}, bf16[512,512]{1,0:T(8,128)(2,1)}, u32[]{:S(2)}) copy-start(bf16[512,512]{1,0:T(8,128)(2,1)} %copy-done.12) | copy-start | bytes 1572868
  167.2 13.1 %copy-start.4 = (bf16[32,32,640]{2,1,0:T(8,128)(2,1)}, bf16[32,32,640]{2,1,0:T(8,128)(2,1)S(1)}, u32[]{:S(2)}) copy-start(bf16[32,32,640]{2,1,0:T(8,128)(2,1)S(1)} %all_to_all.30) | copy-start | bytes 3932164
  167.2 13.2 %collective-permute-start.14 = (bf16[4,256,640]{2,1,0:T(8,128)(2,1)S(1)}, bf16[4,256,640]{2,1,0:T(8,128)(2,1)}, u32[]{:S(2)}, u32[]{:S(2)}) collective-permute-start(bf16[4,256,640]{2,1,0:T(8,128)(2,1)S(1)} %bitcast.11), channel_id=1, source_target_pairs={{0,8},{8,0},{1,9},{9,1},{2,10},{10,2},{3,11},{11,3},{4,12},{12,4},... | collective-permute-start | bytes 3932168 | tf_op jit(solution)/shard_map/ppermute | solution.py:42
  170.1 10.3 %collective-permute-start.15 = (bf16[512,512]{1,0:T(8,128)(2,1)S(1)}, bf16[512,512]{1,0:T(8,128)(2,1)S(1)}, u32[]{:S(2)}, u32[]{:S(2)}) collective-permute-start(bf16[512,512]{1,0:T(8,128)(2,1)S(1)} %copy-done.1), channel_id=1, source_target_pairs={{0,8},{8,0},{1,9},{9,1},{2,10},{10,2},{3,11},{11,3},{4,12},{12,4},... | collective-permute-start | bytes 1572872 | tf_op jit(solution)/shard_map/ppermute | solution.py:42
  170.2 10.2 %collective-permute-start.16 = (bf16[512,512]{1,0:T(8,128)(2,1)S(1)}, bf16[512,512]{1,0:T(8,128)(2,1)}, u32[]{:S(2)}, u32[]{:S(2)}) collective-permute-start(bf16[512,512]{1,0:T(8,128)(2,1)S(1)} %copy-done.11), channel_id=1, source_target_pairs={{0,8},{8,0},{1,9},{9,1},{2,10},{10,2},{3,11},{11,3},{4,12},{12,4},... | collective-permute-start | bytes 1572872 | tf_op jit(solution)/shard_map/ppermute | solution.py:42
  170.6 9.8 %collective-permute-start.17 = (bf16[512,512]{1,0:T(8,128)(2,1)S(1)}, bf16[512,512]{1,0:T(8,128)(2,1)}, u32[]{:S(2)}, u32[]{:S(2)}) collective-permute-start(bf16[512,512]{1,0:T(8,128)(2,1)S(1)} %copy-done.9), channel_id=1, source_target_pairs={{0,8},{8,0},{1,9},{9,1},{2,10},{10,2},{3,11},{11,3},{4,12},{12,4},... | collective-permute-start | bytes 1572872 | tf_op jit(solution)/shard_map/ppermute | solution.py:42
  170.7 9.7 %collective-permute-start.18 = (bf16[512,512]{1,0:T(8,128)(2,1)S(1)}, bf16[512,512]{1,0:T(8,128)(2,1)}, u32[]{:S(2)}, u32[]{:S(2)}) collective-permute-start(bf16[512,512]{1,0:T(8,128)(2,1)S(1)} %copy-done.13), channel_id=1, source_target_pairs={{0,8},{8,0},{1,9},{9,1},{2,10},{10,2},{3,11},{11,3},{4,12},{12,4},... | collective-permute-start | bytes 1572872 | tf_op jit(solution)/shard_map/ppermute | solution.py:42
  180.4 0.8 copy-start.23

commit v4 on v3

--- a/solution.py
+++ b/solution.py
@@ -11,16 +11,15 @@
 GELU_C = 0.7978845608
 GELU_K = 0.044715
 MP = ("y", "x_hi")
-DP = ("x_lo", "zh", "zl", "core")
-CUBE = ("x_lo", "zl", "core")
-COLS = ("zh", "y", "x_hi")
-SPREAD = ("x_lo", "zl", "y", "x_hi")
+DP = ("x_lo", "z", "core")
+PLANE = ("x_lo", "core", "y", "x_hi")
+SPREAD = ("x_lo", "y", "x_hi")
 BF = jnp.bfloat16
 F32 = jnp.float32
 LANES = 128
 OUT_COLS = 16
 MIB = 1 << 20
-LIM = (60, 60, 8, 60, 60, 60, 60, 60, 16)
+LIM = (60, 60, 8, 8, 8, 60, 60, 60, 16)
 NT = (((1,), (1,)), ((), ()))
 
 
@@ -93,16 +92,17 @@
     return pl.BlockSpec(shape, lambda i: (0,) * len(shape), pipeline_mode=pl.Buffered(1))
 
 
-def gate(after, *arrays):
+def gate(first, *arrays, after=()):
+    after = (first, *after)
     anywhere = pl.BlockSpec(memory_space=pl.ANY)
     return pl.pallas_call(
         lambda *refs: None,
         out_shape=[jax.ShapeDtypeStruct(a.shape, a.dtype) for a in arrays],
-        in_specs=[anywhere] * (len(arrays) + 1),
+        in_specs=[anywhere] * (len(arrays) + len(after)),
         out_specs=[anywhere] * len(arrays),
-        input_output_aliases={i + 1: i for i in range(len(arrays))},
+        input_output_aliases={i + len(after): i for i in range(len(arrays))},
         compiler_params=pltpu.CompilerParams(vmem_limit_bytes=60 * MIB),
-    )(after, *arrays)
+    )(*after, *arrays)
 
 
 def parts_of(size, count):
@@ -141,24 +141,24 @@
     ).astype(BF)
 
 
-def feats_kernel(where_ref, feats_ref, *out_refs):
-    x_index, l_index, c_index = where_ref[0], where_ref[1], where_ref[2]
+def feats_kernel(where_ref, feats_ref, own_ref, give_ref):
+    x_index, c_index = where_ref[0], where_ref[1]
     rows, width = feats_ref.shape
-    h_count = out_refs[0].shape[1] // LANES
-    chunk = width // (8 * h_count)
+    z_count = own_ref.shape[1] // LANES
+    chunk = width // (4 * z_count)
     source = lax.broadcasted_iota(jnp.int32, (2 * LANES, LANES), 0)
     target = lax.broadcasted_iota(jnp.int32, (2 * LANES, LANES), 1)
     inside = (target >= OUT_COLS) & (target < OUT_COLS + chunk)
-    for rx, rl, rc in [(a, b, c) for a in range(2) for b in range(2) for c in range(2)]:
-        for h in range(h_count):
-            place = ((rx ^ x_index) * h_count + h) * 2 + (rl ^ l_index)
-            begin = (place * 2 + (rc ^ c_index)) * chunk
+    for rx, rc in [(a, b) for a in range(2) for b in range(2)]:
+        for z in range(z_count):
+            begin = (((rx ^ x_index) * z_count + z) * 2 + (rc ^ c_index)) * chunk
             window = jnp.minimum(begin // LANES * LANES, width - 2 * LANES)
             shift = begin - window - OUT_COLS
             move = jnp.where(inside & (source == target + shift), 1.0, 0.0).astype(BF)
             piece = feats_ref[:, pl.ds(pl.multiple_of(window, LANES), 2 * LANES)]
             piece = jnp.dot(piece, move, preferred_element_type=F32).astype(BF)
-            out_refs[rx * 2 + rl][rc * rows : (rc + 1) * rows, h * LANES : (h + 1) * LANES] = piece
+            out_ref = (own_ref, give_ref)[rx]
+            out_ref[rc * rows : (rc + 1) * rows, z * LANES : (z + 1) * LANES] = piece
 
 
 def unit_kernel(got_ref, unit_ref, inv_ref, spread_ref):
@@ -177,7 +177,7 @@
 
 
 def column_place(where_ref, block):
-    return lax.rem(where_ref[4] + block, 4) * 2
+    return (((block // 2) ^ where_ref[0]) * 2 + ((block % 2) ^ where_ref[1])) * 2
 
 
 def logits_kernel(where_ref, scale_ref, video_ref, *refs):
@@ -225,7 +225,7 @@
     half = 2 * emb + LANES // 2
     row_sum = back[:, 2 * emb : 2 * emb + 1] + back[:, half : half + 1]
     weighted = back[:, :emb] / row_sum + back[:, emb : 2 * emb]
-    text = text_ref[where_ref[3]].astype(F32)
+    text = text_ref[where_ref[2]].astype(F32)
     unit = unit_ref[...]
     positive = scale_val * jnp.sum(unit.astype(BF).astype(F32) * text, axis=-1, keepdims=True)
     rows_piece = jnp.sum(jnp.log(row_sum) - 2.0 * positive, axis=0, keepdims=True)
@@ -244,9 +244,9 @@
 
 
 def gelu_kernel(*refs):
-    pre_refs, (hidden_ref, der_ref) = refs[:8], refs[8:]
+    pre_refs, (hidden_ref, der_ref) = refs[:4], refs[4:]
     rows = pre_refs[0].shape[1]
-    for block in range(8):
+    for block in range(4):
         pre = pre_refs[block][...].astype(F32)
         tanh_val = gelu_tanh(pre)
         span = slice(block * rows, (block + 1) * rows)
@@ -254,63 +254,63 @@
         der_ref[:, span] = gelu_der(pre, tanh_val).astype(BF)
 
 
-def grads_kernel(where_ref, own_hbm, other_hbm, wout_hbm, der_hbm, hidden_hbm, *refs):
-    feats_hbm, refs = refs[:8], refs[8:]
+def grads_kernel(where_ref, own_hbm, other_hbm, wout_hbm, hidden_hbm, der_hbm, *refs):
+    feats_hbm, refs = refs[:4], refs[4:]
     out_ref, grads_ref, wout_ref, der_ref, hidden_ref, feats_ref, sems = refs
-    x_index, l_index, c_index = where_ref[0], where_ref[1], where_ref[2]
+    x_index, c_index = where_ref[0], where_ref[1]
     rows = own_hbm.shape[1]
-    emb = wout_ref.shape[1]
-    hid = wout_ref.shape[0]
-    h_count = out_ref.shape[0]
+    hid, emb = wout_ref.shape
+    z_count = out_ref.shape[0]
+    spans = parts_of(hid, 2)
     copies = []
-    for block in range(8):
-        rx, rl, rc = block // 4, block // 2 % 2, block % 2
+    for block in range(4):
+        rx, rc = block // 2, block % 2
         source = other_hbm if rc else own_hbm
-        copies.append((source.at[(rx ^ x_index) * 2 + (rl ^ l_index)], grads_ref.at[block]))
+        copies.append((source.at[rx ^ x_index], grads_ref.at[block]))
     copies.append((wout_hbm, wout_ref))
-    copies.append((der_hbm, der_ref))
-    for block in range(8):
-        side = block % 2 * rows
-        copies.append((feats_hbm[block].at[pl.ds(side, rows)], feats_ref.at[pl.ds(block * rows, rows)]))
-    copies.append((hidden_hbm, hidden_ref))
+    copies.append((der_hbm.at[spans[0]], der_ref.at[spans[0]]))
+    for block in range(4):
+        side = pl.ds(block % 2 * rows, rows)
+        copies.append((feats_hbm[block].at[side], feats_ref.at[pl.ds(block * rows, rows)]))
+    copies.append((hidden_hbm.at[spans[0]], hidden_ref.at[spans[0]]))
+    copies.append((der_hbm.at[spans[1]], der_ref.at[spans[1]]))
+    copies.append((hidden_hbm.at[spans[1]], hidden_ref.at[spans[1]]))
     copies = [pltpu.make_async_copy(a, b, sems.at[i]) for i, (a, b) in enumerate(copies)]
     for copy in copies:
         copy.start()
     source = lax.broadcasted_iota(jnp.int32, (emb, LANES), 0)
     target = lax.broadcasted_iota(jnp.int32, (emb, LANES), 1)
-    column = ((target // OUT_COLS) * 2 + l_index) * 2 + c_index
+    column = (target // OUT_COLS) * 2 + c_index
     column = x_index * (emb // 2) + column * OUT_COLS + target % OUT_COLS
-    pick = (target < h_count * OUT_COLS) & (source == column)
-    pick = jnp.where(pick, 1.0, 0.0).astype(BF)
-    for copy in copies[:9]:
+    pick = jnp.where(source == column, 1.0, 0.0).astype(BF)
+    for copy in copies[:5]:
         copy.wait()
-    grads = grads_ref[:, :, :emb].reshape(8 * rows, emb)
+    grads = grads_ref[:, :, :emb].reshape(4 * rows, emb)
     picked = jnp.dot(grads, pick, preferred_element_type=F32).astype(BF)
     loss = jnp.zeros((1, LANES), F32)
-    for block in range(8):
+    for block in range(4):
         loss += jnp.sum(grads_ref[block, :, emb:].astype(F32), axis=0, keepdims=True)
     a, b, c = split3(jnp.sum(loss, axis=1, keepdims=True))
-    spans = parts_of(hid, 2)
     for i, span in enumerate(spans):
         size = span.stop - span.start
         lane = lax.broadcasted_iota(jnp.int32, (size, LANES), 1)
         grad_hidden = lax.dot_general(wout_ref[span, :], grads, NT, preferred_element_type=F32)
-        if i == 0:
-            copies[9].wait()
+        copies[(5, 11)[i]].wait()
         grad_pre = (grad_hidden * der_ref[span, :].astype(F32)).astype(BF)
         if i == 0:
-            for copy in copies[10:]:
+            for copy in copies[6:10]:
                 copy.wait()
         total = jnp.dot(grad_pre, feats_ref[...], preferred_element_type=F32)
+        copies[(10, 12)[i]].wait()
         outer = jnp.dot(hidden_ref[span, :], picked, preferred_element_type=F32)
-        for h in range(h_count):
-            moved = outer if h == 0 else pltpu.roll(outer, LANES - h * OUT_COLS, 1)
-            value = jnp.where(lane < OUT_COLS, moved, total[:, h * LANES : (h + 1) * LANES])
+        for z in range(z_count):
+            moved = outer if z == 0 else pltpu.roll(outer, LANES - z * OUT_COLS, 1)
+            value = jnp.where(lane < OUT_COLS, moved, total[:, z * LANES : (z + 1) * LANES])
             if i == 0:
                 row = lax.broadcasted_iota(jnp.int32, (size, LANES), 0)
                 extra = jnp.where(row == 0, a, jnp.where(row == 1, b, c))
                 value = jnp.where((lane == LANES - 1) & (row < 3), extra, value)
-            out_ref[h, span, :] = value.astype(BF)
+            out_ref[z, span, :] = value.astype(BF)
 
 
 def final_kernel(got_ref, in_ref, out_ref, loss_ref, *, batch_total):
@@ -323,18 +323,13 @@
     loss_ref[...] = loss
 
 
-def ring(value, step):
-    return lax.ppermute(value, "zh", [(i, (i - step) % 4) for i in range(4)])
-
-
 def on_device(video_feats, text_feats, weight_in, weight_out, logit_scale):
     rows, d_in = video_feats.shape
     hid, emb = weight_out.shape
     mp_count = lax.axis_size(MP)
-    h_count = lax.axis_size("zh")
     own_rows = rows // mp_count
     batch_total = rows * lax.axis_size(DP)
-    where = [lax.axis_index(name) for name in ("x_lo", "zl", "core", MP, "zh")]
+    where = [lax.axis_index(name) for name in ("x_lo", "core", MP)]
     where = jnp.stack(where).astype(jnp.int32)
 
     partial_value, pre_bf, text_emb = call(
@@ -347,60 +342,56 @@
     )
     got = exchange(partial_value.reshape(mp_count, own_rows, emb), MP)
 
-    texts = [ring(text_emb, step) for step in (1, 2, 3)]
-    feats = call(
-        feats_kernel, [((2 * rows, h_count * LANES), BF)] * 4, LIM[1], where, video_feats, scalars=1
+    text_x = swap(text_emb, "x_lo")
+    texts = [swap(text_emb, "core"), text_x, swap(text_x, "core")]
+    z_count = lax.axis_size("z")
+    feats, give_x = call(
+        feats_kernel, [((2 * rows, z_count * LANES), BF)] * 2, LIM[1], where, video_feats, scalars=1
     )
     unit, inv_norm, video = call(
         unit_kernel,
         [((own_rows, emb), F32), ((own_rows, LANES), F32), ((8, own_rows, emb), BF)],
-        LIM[2], got, after=(feats[0],),
-    )
-    give_l, give_x, give_xl, pre_bf = gate(inv_norm, feats[1], feats[2], feats[3], pre_bf)
+        LIM[2], got, after=(feats, text_x),
+    )
+    give_x, pre_own = gate(inv_norm, give_x, pre_bf)
     feats_x = swap(give_x, "x_lo")
-    feats_l = swap(give_l, "zl")
-    feats_xl = swap(swap(give_xl, "x_lo"), "zl")
-    pre_l = swap(pre_bf, "zl")
-    sides = [pre_bf, pre_l, swap(pre_bf, "x_lo"), swap(pre_l, "x_lo")]
-    pre = [value for side in sides for value in (side, swap(side, "core"))]
-
-    video_rows = exchange(video, CUBE)
+
+    video_rows = exchange(video, "z")
     (cols,) = call(
         logits_kernel, [((4 * mp_count, 8, LANES), F32)], LIM[3],
         where, logit_scale, video_rows, text_emb, *texts, scalars=2,
         scratch=[pltpu.VMEM((8, LANES), F32)],
     )
-    cols = exchange(cols, COLS)
+    cols = exchange(cols, PLANE)
+    pre_x = swap(pre_own, "x_lo")
+    pre = (pre_own, swap(pre_own, "core"), pre_x, swap(pre_x, "core"))
     packed, logs = call(
         weights_kernel, [((8, own_rows, 2 * emb + LANES), BF), ((8, LANES), F32)], LIM[4],
         where, logit_scale, video_rows, text_emb, *texts, cols, scalars=2,
         scratch=[pltpu.VMEM((8, LANES), F32)],
     )
-    back = exchange(packed, CUBE)
+    feats_q = (feats, swap(feats, "core"), feats_x, swap(feats_x, "core"))
+    back = exchange(packed, "z")
     (sent,) = call(
         functools.partial(proj_kernel, sharers=4 * mp_count),
-        [((4 * mp_count, own_rows, emb + LANES), BF)], LIM[5],
+        [((2 * mp_count, own_rows, emb + LANES), BF)], LIM[5],
         where, logit_scale, back, unit, inv_norm, text_emb.reshape(mp_count, own_rows, emb), logs,
-        scalars=2, after=(feats_x, feats_l, feats_xl, *pre[1:]),
-    )
-    grads = exchange(sent, SPREAD).reshape(4, rows, emb + LANES)
+        scalars=2, after=(feats_q[1], feats_q[3], pre[1], pre[3]),
+    )
+    gelus = call(gelu_kernel, [((hid, 4 * rows), BF)] * 2, LIM[6], *pre, after=(sent,))
+    grads = exchange(sent, SPREAD).reshape(2, rows, emb + LANES)
+    (grads,) = gate(gelus[0], grads, after=(gelus[1],))
     other = swap(grads, "core")
-    feats_q = [
-        value for side in (feats[0], feats_l, feats_x, feats_xl) for value in (side, swap(side, "core"))
-    ]
-    hidden_all, der_all = call(
-        gelu_kernel, [((hid, 8 * rows), BF), ((hid, 8 * rows), BF)], LIM[6], *pre
-    )
     (packed,) = call(
-        grads_kernel, [((h_count, hid, LANES), BF)], LIM[7],
-        where, grads, other, weight_out, der_all, hidden_all, *feats_q, scalars=1, raw=True,
+        grads_kernel, [((z_count, hid, LANES), BF)], LIM[7],
+        where, grads, other, weight_out, *gelus, *feats_q, scalars=1, raw=True,
         scratch=[
-            pltpu.VMEM((8, rows, emb + LANES), BF), pltpu.VMEM((hid, emb), BF),
-            pltpu.VMEM((hid, 8 * rows), BF), pltpu.VMEM((hid, 8 * rows), BF),
-            pltpu.VMEM((8 * rows, h_count * LANES), BF), pltpu.SemaphoreType.DMA((19,)),
+            pltpu.VMEM((4, rows, emb + LANES), BF), pltpu.VMEM((hid, emb), BF),
+            pltpu.VMEM((hid, 4 * rows), BF), pltpu.VMEM((hid, 4 * rows), BF),
+            pltpu.VMEM((4 * rows, z_count * LANES), BF), pltpu.SemaphoreType.DMA((13,)),
         ],
     )
-    final = exchange(packed, "zh")
+    final = exchange(packed, "z")
     in_rows = d_in // lax.axis_size(DP)
     grad_in, grad_out, loss = call(
         functools.partial(final_kernel, batch_total=batch_total),
@@ -411,7 +402,7 @@
 
 
 def solution(mesh):
-    fine = Mesh(mesh.devices.reshape(2, 4, 2, 2, mesh.devices.shape[1] // 2, 2), DP + MP)
+    fine = Mesh(mesh.devices.reshape(2, -1, 2, mesh.devices.shape[1] // 2, 2), DP + MP)
     in_specs = (P(DP, None), P(DP, None), P(None, MP), P(MP, None), P())
     out_specs = (P(), P(DP, MP), P(MP, DP))
     return jax.shard_map(

time: 219 us -> 169 us (0.77)
  waiting for transfers between devices: 58.8 us -> 40.1 us
  starting transfers between devices: 56.9 us -> 40.4 us
  Pallas kernels: 43.3 us -> 35 us
  blocking collectives: 50.9 us -> 45.3 us
    ppermute x3 -> x0, waiting for transfers between devices: 18.4 us -> none  [ring(): return lax.ppermute(value, 'zh', [(i, (i - step) % 4) for i in range(4)])]
    ppermute x16 -> x10, waiting for transfers between devices: 31.8 us -> 14.4 us  [swap(): return lax.ppermute(value, axis, [(0, 1), (1, 0)])]
    all_to_all x4 -> x5, waiting for transfers between devices: 8.6 us -> 25.7 us  [exchange(): return lax.all_to_all(value, axis, 0, 0)]
    ppermute x3 -> x0, starting transfers between devices: 9.28 us -> none  [ring(): return lax.ppermute(value, 'zh', [(i, (i - step) % 4) for i in range(4)])]
    ppermute x16 -> x10, starting transfers between devices: 18.4 us -> 9.86 us  [swap(): return lax.ppermute(value, axis, [(0, 1), (1, 0)])]
    pallas_call x9, Pallas kernels: 43.3 us -> 35 us  [call(): pl.pallas_call(body, grid=(1,), out_shape=[jax.ShapeDtypeStruct(s, d) for...]
    all_to_all x2 -> x1, blocking collectives: 50.9 us -> 45.3 us  [exchange(): return lax.all_to_all(value, axis, 0, 0)]
    all_to_all x4 -> x5, starting transfers between devices: 29.2 us -> 30.5 us  [exchange(): return lax.all_to_all(value, axis, 0, 0)]
  transfers between devices with their start and end apart: 23 -> 15, of which waited for: 7 -> 10; matrix products, arithmetic and copies ran while one was open for 0% -> 0% of each run, Pallas kernels for 8% -> 9%
where the time goes in v4:
time: 169 us
  blocking collectives  45.3 us (27%)
  starting transfers between devices  40.4 us (24%)
  waiting for transfers between devices  40.1 us (24%)
  Pallas kernels  35 us (21%)
  local copies, waits for them, and re-layouts  5.55 us (3%)
    all_to_all x1, blocking collectives, exchange(): return lax.all_to_all(value, axis, 0, 0)  45.3 us
    pallas_call x9, Pallas kernels, call(): pl.pallas_call(body, grid=(1,), out_shape=[jax.ShapeDtypeStruct(s, d) for...  35 us
    all_to_all x5, starting transfers between devices, exchange(): return lax.all_to_all(value, axis, 0, 0)  30.5 us
    all_to_all x5, waiting for transfers between devices, exchange(): return lax.all_to_all(value, axis, 0, 0)  25.7 us
    ppermute x10, waiting for transfers between devices, swap(): return lax.ppermute(value, axis, [(0, 1), (1, 0)])  14.4 us
    ppermute x10, starting transfers between devices, swap(): return lax.ppermute(value, axis, [(0, 1), (1, 0)])  9.86 us
    unnamed x26, local copies, waits for them, and re-layouts  5.55 us
  transfers between devices with their start and end apart: 15, of which 10 were waited for; matrix products, arithmetic and copies ran while one was open for 0% of the time, Pallas kernels for 9%

profile of v4, /device:TPU:1, one launch (start us, length us, event | category | flops | bytes accessed | tf_op | source)
XLA Modules:
  0.0 168.7 jit_solution(3245610360115004779)
XLA Ops:
  0.6 6.7 %shard_map.76 = (bf16[256,512]{1,0:T(8,128)(2,1)}, bf16[800,256]{1,0:T(8,128)(2,1)}, bf16[256,512]{1,0:T(8,128)(2,1)}) custom-call(bf16[256,512]{1,0:T(8,128)(2,1)} %refs_0_.1, bf16[256,3200]{1,0:T(8,128)(2,1)} %refs_1_.6, bf16[800,3200]{1,0:T(8,128)(2,1)} %bitcast.11, bf16[800,512]{1,0:T(8,128)(2,1)} %refs_3_.3), custom_call_target="tpu_custom_call" | custom-call | flops 1024 | bytes 1024 | tf_op jit(solution)/shard_map/pallas_call | solution.py:79
  7.4 2.1 %collective-permute-start = (bf16[256,512]{1,0:T(8,128)(2,1)}, bf16[256,512]{1,0:T(8,128)(2,1)S(1)}, u32[]{:S(2)}, u32[]{:S(2)}) collective-permute-start(bf16[256,512]{1,0:T(8,128)(2,1)} %get-tuple-element.22.refs_3_), channel_id=1, source_target_pairs={{0,128},{128,0},{1,129},{129,1},{2,130},{130,2},{3,131},{131,3},{4... | collective-permute-start | bytes 786440 | tf_op jit(solution)/shard_map/ppermute | solution.py:41
  9.5 6.4 %all-to-all-start = ((bf16[8,32,512]{2,1,0:T(8,128)(2,1)}), bf16[8,32,512]{2,1,0:T(8,128)(2,1)S(1)}, u32[]{:S(2)}, u32[]{:S(2)}) async-start(bf16[8,32,512]{2,1,0:T(8,128)(2,1)} %bitcast.12), calls=%async_computation | async-start | bytes 524288 | tf_op jit(solution)/shard_map/all_to_all | solution.py:45
  15.9 0.7 pad_add_fusion.refs_0_
  16.5 4.5 %shard_map.77 = (bf16[512,1024]{1,0:T(8,128)(2,1)}, bf16[512,1024]{1,0:T(8,128)(2,1)}) custom-call(s32[3]{0:T(128)} %pad_add_fusion.refs_0_, bf16[256,3200]{1,0:T(8,128)(2,1)} %refs_1_.6), custom_call_target="tpu_custom_call" | custom-call | flops 1024 | bytes 1024 | tf_op jit(solution)/shard_map/pallas_call | solution.py:79
  21.0 2.5 %all-to-all-done.refs_0_ = bf16[8,32,512]{2,1,0:T(8,128)(2,1)S(1)} async-done(((bf16[8,32,512]{2,1,0:T(8,128)(2,1)}), bf16[8,32,512]{2,1,0:T(8,128)(2,1)S(1)}, u32[]{:S(2)}, u32[]{:S(2)}) %all-to-all-start) | async-done | bytes 262176 | tf_op jit(solution)/shard_map/all_to_all | solution.py:45
  23.5 0.0 collective-permute-done.refs_2_.refs_5_
  23.5 0.0 copy-start
  23.5 1.2 copy-done
  24.7 0.0 copy-start.2
  24.7 0.0 copy-start.5
  24.7 0.9 shard_map.78
  25.6 0.0 copy-start.3
  25.6 0.6 copy-done.3
  26.2 0.0 copy-start.4
  26.2 0.6 copy-done.4
  26.8 0.0 copy-start.1
  26.8 0.0 collective-permute-start.7
  26.8 8.3 %all-to-all-start.1 = ((bf16[8,32,512]{2,1,0:T(8,128)(2,1)}), bf16[8,32,512]{2,1,0:T(8,128)(2,1)S(1)}, u32[]{:S(2)}, u32[]{:S(2)}) async-start(bf16[8,32,512]{2,1,0:T(8,128)(2,1)} %get-tuple-element.27), calls=%async_computation.1 | async-start | bytes 524288 | tf_op jit(solution)/shard_map/all_to_all | solution.py:45
  35.1 0.0 copy-done.2
  35.1 3.0 %collective-permute-start.4 = (bf16[256,512]{1,0:T(8,128)(2,1)S(1)}, bf16[256,512]{1,0:T(8,128)(2,1)S(1)}, u32[]{:S(2)}, u32[]{:S(2)}) collective-permute-start(bf16[256,512]{1,0:T(8,128)(2,1)S(1)} %copy-done.2), channel_id=1, source_target_pairs={{0,8},{8,0},{1,9},{9,1},{2,10},{10,2},{3,11},{11,3},{4,12},{12,4},... | collective-permute-start | bytes 786440 | tf_op jit(solution)/shard_map/ppermute | solution.py:41
  38.1 0.1 collective-permute-start.5
  38.9 0.4 collective-permute-done.4.refs_4_
  39.3 0.4 collective-permute-done.5.refs_6_
  39.7 4.9 %all-to-all-done.1.refs_2_ = bf16[8,32,512]{2,1,0:T(8,128)(2,1)S(1)} async-done(((bf16[8,32,512]{2,1,0:T(8,128)(2,1)}), bf16[8,32,512]{2,1,0:T(8,128)(2,1)S(1)}, u32[]{:S(2)}, u32[]{:S(2)}) %all-to-all-start.1) | async-done | bytes 262176 | tf_op jit(solution)/shard_map/all_to_all | solution.py:45
  44.5 0.0 copy-done.5
  44.5 1.8 %shard_map.80 = f32[32,8,128]{2,1,0:T(8,128)} custom-call(s32[3]{0:T(128)S(1)} %copy-done.5, f32[1]{0:T(128)S(6)} %copy.14.refs_1_, bf16[8,32,512]{2,1,0:T(8,128)(2,1)S(1)} %all-to-all-done.1.refs_2_, bf16[256,512]{1,0:T(8,128)(2,1)S(1)} %copy-done.2, bf16[256,512]{1,0:T(8,128)(2,1)S(1)} %collective-permute-done.4.refs_4_, ...), custom_call_target="tpu_custom_call" | custom-call | flops 1024 | bytes 1024 | tf_op jit(solution)/shard_map/pallas_call | solution.py:79
  46.4 8.5 %all-to-all-start.2 = ((f32[32,8,128]{2,1,0:T(8,128)}), f32[32,8,128]{2,1,0:T(8,128)S(1)}, u32[]{:S(2)}, u32[]{:S(2)}) async-start(f32[32,8,128]{2,1,0:T(8,128)} %shard_map.80), calls=%async_computation.2 | async-start | bytes 262144 | tf_op jit(solution)/shard_map/all_to_all | solution.py:45
  54.9 0.0 copy-done.1
  54.9 0.3 collective-permute-start.6
  55.2 0.0 collective-permute-done.7.refs_8_
  55.2 0.3 collective-permute-start.8
  55.5 7.1 %all-to-all-done.2.refs_7_ = f32[32,8,128]{2,1,0:T(8,128)S(1)} async-done(((f32[32,8,128]{2,1,0:T(8,128)}), f32[32,8,128]{2,1,0:T(8,128)S(1)}, u32[]{:S(2)}, u32[]{:S(2)}) %all-to-all-start.2) | async-done | bytes 131104 | tf_op jit(solution)/shard_map/all_to_all | solution.py:45
  62.6 3.1 %shard_map.81 = (bf16[8,32,1152]{2,1,0:T(8,128)(2,1)}, f32[8,128]{1,0:T(8,128)S(1)}) custom-call(s32[3]{0:T(128)S(1)} %copy-done.5, f32[1]{0:T(128)S(6)} %copy.14.refs_1_, bf16[8,32,512]{2,1,0:T(8,128)(2,1)S(1)} %all-to-all-done.1.refs_2_, bf16[256,512]{1,0:T(8,128)(2,1)S(1)} %copy-done.2, bf16[256,512]{1,0:T(8,128)(2,1)S(1)} %collective-permute-done.4.refs_4_, ...), custom_call_target="tpu_custom_call" | custom-call | flops 1024 | bytes 1024 | tf_op jit(solution)/shard_map/pallas_call | solution.py:79
  65.7 0.0 copy-start.6
  65.7 0.6 copy-done.6
  66.3 3.5 %all-to-all-start.3 = ((bf16[8,32,1152]{2,1,0:T(8,128)(2,1)}), bf16[8,32,1152]{2,1,0:T(8,128)(2,1)S(1)}, u32[]{:S(2)}, u32[]{:S(2)}) async-start(bf16[8,32,1152]{2,1,0:T(8,128)(2,1)} %get-tuple-element.28), calls=%async_computation.3 | async-start | bytes 1179648 | tf_op jit(solution)/shard_map/all_to_all | solution.py:45
  69.8 0.4 collective-permute-start.2
  70.2 0.5 collective-permute-start.1
  70.7 10.2 %collective-permute-done.2.refs_2_ = bf16[800,256]{1,0:T(8,128)(2,1)S(1)} collective-permute-done((bf16[800,256]{1,0:T(8,128)(2,1)}, bf16[800,256]{1,0:T(8,128)(2,1)S(1)}, u32[]{:S(2)}, u32[]{:S(2)}) %collective-permute-start.2) | collective-permute-done | bytes 409632 | tf_op jit(solution)/shard_map/ppermute | solution.py:41
  80.9 0.0 copy-start.12
  80.9 1.1 collective-permute-start.3
  82.0 0.0 collective-permute-done.1.refs_9_.refs_1_
  82.0 0.0 copy-start.10
  82.0 0.0 collective-permute-done.6.refs_7_
  82.0 0.0 copy-done.12
  82.0 0.0 copy-start.8
  82.0 1.5 collective-permute-done.3.refs_10_.refs_3_
  83.5 5.7 %all-to-all-done.3.refs_2_ = bf16[8,32,1152]{2,1,0:T(8,128)(2,1)S(1)} async-done(((bf16[8,32,1152]{2,1,0:T(8,128)(2,1)}), bf16[8,32,1152]{2,1,0:T(8,128)(2,1)S(1)}, u32[]{:S(2)}, u32[]{:S(2)}) %all-to-all-start.3) | async-done | bytes 589856 | tf_op jit(solution)/shard_map/all_to_all | solution.py:45
  89.2 0.0 collective-permute-done.8.refs_8_.refs_9_
  89.2 0.0 copy-done.10
  89.2 0.0 copy-done.8
  89.2 0.8 copy-done.9
  90.0 3.0 %shard_map.82.refs_4_ = bf16[16,32,640]{2,1,0:T(8,128)(2,1)} custom-call(s32[3]{0:T(128)} %pad_add_fusion.refs_0_, f32[1]{0:T(128)S(6)} %copy.14.refs_1_, bf16[8,32,1152]{2,1,0:T(8,128)(2,1)} %copy-done.9, f32[32,512]{1,0:T(8,128)} %copy-done.3, f32[32,128]{1,0:T(8,128)} %copy-done.4, bf16[8,32,512]{2,1,0:T(8,128)(2,1)} %bitcast.9, f32[8,128]{1,0:T(8,128)} %copy-done.6, ...), custom_call_target="tpu_custom_call" | custom-call | flops 1024 | bytes 1024 | tf_op jit(solution)/shard_map/pallas_call | solution.py:79
  93.0 3.8 %all-to-all-start.4 = ((bf16[16,32,640]{2,1,0:T(8,128)(2,1)}), bf16[16,32,640]{2,1,0:T(8,128)(2,1)S(1)}, u32[]{:S(2)}, u32[]{:S(2)}) async-start(bf16[16,32,640]{2,1,0:T(8,128)(2,1)} %shard_map.82.refs_4_), calls=%async_computation.4 | async-start | bytes 1310720 | tf_op jit(solution)/shard_map/all_to_all | solution.py:45
  96.8 5.3 %shard_map.83 = (bf16[800,1024]{1,0:T(8,128)(2,1)}, bf16[800,1024]{1,0:T(8,128)(2,1)}) custom-call(bf16[800,256]{1,0:T(8,128)(2,1)} %get-tuple-element.26.refs_0_, bf16[800,256]{1,0:T(8,128)(2,1)} %copy-done.10, bf16[800,256]{1,0:T(8,128)(2,1)} %copy-done.12, bf16[800,256]{1,0:T(8,128)(2,1)} %collective-permute-done.3.refs_10_.refs_3_, ...), custom_call_target="tpu_custom_call" | custom-call | flops 1024 | bytes 1024 | tf_op jit(solution)/shard_map/pallas_call | solution.py:79
  102.1 5.6 %all-to-all-done.4 = bf16[16,32,640]{2,1,0:T(8,128)(2,1)S(1)} async-done(((bf16[16,32,640]{2,1,0:T(8,128)(2,1)}), bf16[16,32,640]{2,1,0:T(8,128)(2,1)S(1)}, u32[]{:S(2)}, u32[]{:S(2)}) %all-to-all-start.4) | async-done | bytes 655392 | tf_op jit(solution)/shard_map/all_to_all | solution.py:45
  107.7 0.9 copy-done.7
  108.6 2.1 %collective-permute-start.9 = (bf16[2,256,640]{2,1,0:T(8,128)(2,1)}, bf16[2,256,640]{2,1,0:T(8,128)(2,1)S(1)}, u32[]{:S(2)}, u32[]{:S(2)}) collective-permute-start(bf16[2,256,640]{2,1,0:T(8,128)(2,1)} %shard_map.84.refs_1_), channel_id=1, source_target_pairs={{0,8},{8,0},{1,9},{9,1},{2,10},{10,2},{3,11},{11,3},{4,12},{12,4},... | collective-permute-start | bytes 1966088 | tf_op jit(solution)/shard_map/ppermute | solution.py:41
  110.6 1.9 %collective-permute-done.9.refs_2_ = bf16[2,256,640]{2,1,0:T(8,128)(2,1)S(1)} collective-permute-done((bf16[2,256,640]{2,1,0:T(8,128)(2,1)}, bf16[2,256,640]{2,1,0:T(8,128)(2,1)S(1)}, u32[]{:S(2)}, u32[]{:S(2)}) %collective-permute-start.9) | collective-permute-done | bytes 655392 | tf_op jit(solution)/shard_map/ppermute | solution.py:41
  112.6 0.8 copy-done.11
  113.4 8.5 %shard_map.85 = bf16[8,800,128]{2,1,0:T(8,128)(2,1)} custom-call(s32[3]{0:T(128)} %pad_add_fusion.refs_0_, bf16[2,256,640]{2,1,0:T(8,128)(2,1)} %shard_map.84.refs_1_, bf16[2,256,640]{2,1,0:T(8,128)(2,1)} %copy-done.11, bf16[800,512]{1,0:T(8,128)(2,1)} %refs_3_.3, bf16[800,1024]{1,0:T(8,128)(2,1)} %get-tuple-element.32.refs_0_.refs_4_, ...), custom_call_target="tpu_custom_call" | custom-call | flops 1024 | bytes 1024 | tf_op jit(solution)/shard_map/pallas_call | solution.py:79
  121.9 45.3 %all_to_all.30.refs_0_ = bf16[8,800,128]{2,1,0:T(8,128)(2,1)S(1)} all-to-all(bf16[8,800,128]{2,1,0:T(8,128)(2,1)} %shard_map.85), channel_id=1, replica_groups=mesh['x_lo'=2,'z'=8,'core'=2,'y'=4,'x_hi'=2] {'z'}, dimensions={0} | all-to-all | bytes 3276800 | tf_op jit(solution)/shard_map/all_to_all | solution.py:45
  167.3 1.2 shard_map.86
  (5 shorter events, 0.0 us)
Async XLA Ops:
  7.4 16.1 %collective-permute-start = (bf16[256,512]{1,0:T(8,128)(2,1)}, bf16[256,512]{1,0:T(8,128)(2,1)S(1)}, u32[]{:S(2)}, u32[]{:S(2)}) collective-permute-start(bf16[256,512]{1,0:T(8,128)(2,1)} %get-tuple-element.22.refs_3_), channel_id=1, source_target_pairs={{0,128},{128,0},{1,129},{129,1},{2,130},{130,2},{3,131},{131,3},{4... | collective-permute-start | bytes 786440 | tf_op jit(solution)/shard_map/ppermute | solution.py:41
  9.5 14.0 %all-to-all-start = ((bf16[8,32,512]{2,1,0:T(8,128)(2,1)}), bf16[8,32,512]{2,1,0:T(8,128)(2,1)S(1)}, u32[]{:S(2)}, u32[]{:S(2)}) async-start(bf16[8,32,512]{2,1,0:T(8,128)(2,1)} %bitcast.12), calls=%async_computation | async-start | bytes 524288 | tf_op jit(solution)/shard_map/all_to_all | solution.py:45
  23.5 1.2 copy-start
  24.7 10.4 %copy-start.2 = (bf16[256,512]{1,0:T(8,128)(2,1)S(1)}, bf16[256,512]{1,0:T(8,128)(2,1)}, u32[]{:S(2)}) copy-start(bf16[256,512]{1,0:T(8,128)(2,1)} %get-tuple-element.22.refs_3_) | copy-start | bytes 786436
  24.7 19.8 %copy-start.5 = (s32[3]{0:T(128)S(1)}, s32[3]{0:T(128)}, u32[]{:S(2)}) copy-start(s32[3]{0:T(128)} %pad_add_fusion.refs_0_) | copy-start | bytes 40
  25.6 0.6 copy-start.3
  26.2 0.6 copy-start.4
  26.8 28.1 %copy-start.1 = (bf16[512,1024]{1,0:T(8,128)(2,1)S(1)}, bf16[512,1024]{1,0:T(8,128)(2,1)}, u32[]{:S(2)}) copy-start(bf16[512,1024]{1,0:T(8,128)(2,1)} %get-tuple-element.21.refs_1_.refs_6_) | copy-start | bytes 3145732
  26.8 28.4 %collective-permute-start.7 = (bf16[512,1024]{1,0:T(8,128)(2,1)}, bf16[512,1024]{1,0:T(8,128)(2,1)}, u32[]{:S(2)}, u32[]{:S(2)}) collective-permute-start(bf16[512,1024]{1,0:T(8,128)(2,1)} %get-tuple-element.31), channel_id=1, source_target_pairs={{0,128},{128,0},{1,129},{129,1},{2,130},{130,2},{3,131},{131,3},{4... | collective-permute-start | bytes 3145736 | tf_op jit(solution)/shard_map/ppermute | solution.py:41
  26.8 17.7 %all-to-all-start.1 = ((bf16[8,32,512]{2,1,0:T(8,128)(2,1)}), bf16[8,32,512]{2,1,0:T(8,128)(2,1)S(1)}, u32[]{:S(2)}, u32[]{:S(2)}) async-start(bf16[8,32,512]{2,1,0:T(8,128)(2,1)} %get-tuple-element.27), calls=%async_computation.1 | async-start | bytes 524288 | tf_op jit(solution)/shard_map/all_to_all | solution.py:45
  35.1 4.1 %collective-permute-start.4 = (bf16[256,512]{1,0:T(8,128)(2,1)S(1)}, bf16[256,512]{1,0:T(8,128)(2,1)S(1)}, u32[]{:S(2)}, u32[]{:S(2)}) collective-permute-start(bf16[256,512]{1,0:T(8,128)(2,1)S(1)} %copy-done.2), channel_id=1, source_target_pairs={{0,8},{8,0},{1,9},{9,1},{2,10},{10,2},{3,11},{11,3},{4,12},{12,4},... | collective-permute-start | bytes 786440 | tf_op jit(solution)/shard_map/ppermute | solution.py:41
  38.1 1.5 collective-permute-start.5
  46.4 16.2 %all-to-all-start.2 = ((f32[32,8,128]{2,1,0:T(8,128)}), f32[32,8,128]{2,1,0:T(8,128)S(1)}, u32[]{:S(2)}, u32[]{:S(2)}) async-start(f32[32,8,128]{2,1,0:T(8,128)} %shard_map.80), calls=%async_computation.2 | async-start | bytes 262144 | tf_op jit(solution)/shard_map/all_to_all | solution.py:45
  54.9 27.1 %collective-permute-start.6 = (bf16[512,1024]{1,0:T(8,128)(2,1)S(1)}, bf16[512,1024]{1,0:T(8,128)(2,1)S(1)}, u32[]{:S(2)}, u32[]{:S(2)}) collective-permute-start(bf16[512,1024]{1,0:T(8,128)(2,1)S(1)} %copy-done.1), channel_id=1, source_target_pairs={{0,8},{8,0},{1,9},{9,1},{2,10},{10,2},{3,11},{11,3},{4,12},{12,4},... | collective-permute-start | bytes 3145736 | tf_op jit(solution)/shard_map/ppermute | solution.py:41
  55.2 33.9 %collective-permute-start.8 = (bf16[512,1024]{1,0:T(8,128)(2,1)}, bf16[512,1024]{1,0:T(8,128)(2,1)}, u32[]{:S(2)}, u32[]{:S(2)}) collective-permute-start(bf16[512,1024]{1,0:T(8,128)(2,1)} %collective-permute-done.7.refs_8_), channel_id=1, source_target_pairs={{0,8},{8,0},{1,9},{9,1},{2,10},{10,2},{3,11},{11,3},{4,12},{12,4},... | collective-permute-start | bytes 3145736 | tf_op jit(solution)/shard_map/ppermute | solution.py:41
  65.7 0.6 copy-start.6
  66.3 22.9 %all-to-all-start.3 = ((bf16[8,32,1152]{2,1,0:T(8,128)(2,1)}), bf16[8,32,1152]{2,1,0:T(8,128)(2,1)S(1)}, u32[]{:S(2)}, u32[]{:S(2)}) async-start(bf16[8,32,1152]{2,1,0:T(8,128)(2,1)} %get-tuple-element.28), calls=%async_computation.3 | async-start | bytes 1179648 | tf_op jit(solution)/shard_map/all_to_all | solution.py:45
  69.8 11.1 %collective-permute-start.2 = (bf16[800,256]{1,0:T(8,128)(2,1)}, bf16[800,256]{1,0:T(8,128)(2,1)S(1)}, u32[]{:S(2)}, u32[]{:S(2)}) collective-permute-start(bf16[800,256]{1,0:T(8,128)(2,1)} %get-tuple-element.26.refs_0_), channel_id=1, source_target_pairs={{0,128},{128,0},{1,129},{129,1},{2,130},{130,2},{3,131},{131,3},{4... | collective-permute-start | bytes 1228808 | tf_op jit(solution)/shard_map/ppermute | solution.py:41
  70.2 11.8 %collective-permute-start.1 = (bf16[800,256]{1,0:T(8,128)(2,1)}, bf16[800,256]{1,0:T(8,128)(2,1)S(1)}, u32[]{:S(2)}, u32[]{:S(2)}) collective-permute-start(bf16[800,256]{1,0:T(8,128)(2,1)} %get-tuple-element.26.refs_0_), channel_id=1, source_target_pairs={{0,8},{8,0},{1,9},{9,1},{2,10},{10,2},{3,11},{11,3},{4,12},{12,4},... | collective-permute-start | bytes 1228808 | tf_op jit(solution)/shard_map/ppermute | solution.py:41
  80.9 1.1 copy-start.12
  80.9 2.6 %collective-permute-start.3 = (bf16[800,256]{1,0:T(8,128)(2,1)S(1)}, bf16[800,256]{1,0:T(8,128)(2,1)}, u32[]{:S(2)}, u32[]{:S(2)}) collective-permute-start(bf16[800,256]{1,0:T(8,128)(2,1)S(1)} %collective-permute-done.2.refs_2_), channel_id=1, source_target_pairs={{0,8},{8,0},{1,9},{9,1},{2,10},{10,2},{3,11},{11,3},{4,12},{12,4},... | collective-permute-start | bytes 1228808 | tf_op jit(solution)/shard_map/ppermute | solution.py:41
  82.0 7.2 %copy-start.10 = (bf16[800,256]{1,0:T(8,128)(2,1)}, bf16[800,256]{1,0:T(8,128)(2,1)S(1)}, u32[]{:S(2)}) copy-start(bf16[800,256]{1,0:T(8,128)(2,1)S(1)} %collective-permute-done.1.refs_9_.refs_1_) | copy-start | bytes 1228804
  82.0 7.2 %copy-start.8 = (bf16[512,1024]{1,0:T(8,128)(2,1)}, bf16[512,1024]{1,0:T(8,128)(2,1)S(1)}, u32[]{:S(2)}) copy-start(bf16[512,1024]{1,0:T(8,128)(2,1)S(1)} %collective-permute-done.6.refs_7_) | copy-start | bytes 3145732
  89.2 0.8 copy-start.9
  93.0 14.7 %all-to-all-start.4 = ((bf16[16,32,640]{2,1,0:T(8,128)(2,1)}), bf16[16,32,640]{2,1,0:T(8,128)(2,1)S(1)}, u32[]{:S(2)}, u32[]{:S(2)}) async-start(bf16[16,32,640]{2,1,0:T(8,128)(2,1)} %shard_map.82.refs_4_), calls=%async_computation.4 | async-start | bytes 1310720 | tf_op jit(solution)/shard_map/all_to_all | solution.py:45
  107.7 0.9 copy-start.7
  108.6 4.0 %collective-permute-start.9 = (bf16[2,256,640]{2,1,0:T(8,128)(2,1)}, bf16[2,256,640]{2,1,0:T(8,128)(2,1)S(1)}, u32[]{:S(2)}, u32[]{:S(2)}) collective-permute-start(bf16[2,256,640]{2,1,0:T(8,128)(2,1)} %shard_map.84.refs_1_), channel_id=1, source_target_pairs={{0,8},{8,0},{1,9},{9,1},{2,10},{10,2},{3,11},{11,3},{4,12},{12,4},... | collective-permute-start | bytes 1966088 | tf_op jit(solution)/shard_map/ppermute | solution.py:41
  112.6 0.8 copy-start.11

commit v5 on v4

--- a/solution.py
+++ b/solution.py
@@ -18,8 +18,9 @@
 F32 = jnp.float32
 LANES = 128
 OUT_COLS = 16
+FAR = 4
 MIB = 1 << 20
-LIM = (60, 60, 8, 8, 8, 60, 60, 60, 16)
+LIM = (60, 60, 60, 8, 8, 60, 60, 60, 16, 16)
 NT = (((1,), (1,)), ((), ()))
 
 
@@ -151,7 +152,8 @@
     inside = (target >= OUT_COLS) & (target < OUT_COLS + chunk)
     for rx, rc in [(a, b) for a in range(2) for b in range(2)]:
         for z in range(z_count):
-            begin = (((rx ^ x_index) * z_count + z) * 2 + (rc ^ c_index)) * chunk
+            target_z = lax.rem(where_ref[3] + z, z_count)
+            begin = (((rx ^ x_index) * z_count + target_z) * 2 + (rc ^ c_index)) * chunk
             window = jnp.minimum(begin // LANES * LANES, width - 2 * LANES)
             shift = begin - window - OUT_COLS
             move = jnp.where(inside & (source == target + shift), 1.0, 0.0).astype(BF)
@@ -255,12 +257,12 @@
 
 
 def grads_kernel(where_ref, own_hbm, other_hbm, wout_hbm, hidden_hbm, der_hbm, *refs):
-    feats_hbm, refs = refs[:4], refs[4:]
-    out_ref, grads_ref, wout_ref, der_ref, hidden_ref, feats_ref, sems = refs
+    feats_hbm, out_refs, refs = refs[:4], refs[4:13], refs[13:]
+    grads_ref, wout_ref, der_ref, hidden_ref, feats_ref, sems = refs
     x_index, c_index = where_ref[0], where_ref[1]
     rows = own_hbm.shape[1]
     hid, emb = wout_ref.shape
-    z_count = out_ref.shape[0]
+    z_count = feats_ref.shape[1] // LANES
     spans = parts_of(hid, 2)
     copies = []
     for block in range(4):
@@ -280,7 +282,7 @@
         copy.start()
     source = lax.broadcasted_iota(jnp.int32, (emb, LANES), 0)
     target = lax.broadcasted_iota(jnp.int32, (emb, LANES), 1)
-    column = (target // OUT_COLS) * 2 + c_index
+    column = lax.rem(where_ref[3] + target // OUT_COLS, z_count) * 2 + c_index
     column = x_index * (emb // 2) + column * OUT_COLS + target % OUT_COLS
     pick = jnp.where(source == column, 1.0, 0.0).astype(BF)
     for copy in copies[:5]:
@@ -310,11 +312,25 @@
                 row = lax.broadcasted_iota(jnp.int32, (size, LANES), 0)
                 extra = jnp.where(row == 0, a, jnp.where(row == 1, b, c))
                 value = jnp.where((lane == LANES - 1) & (row < 3), extra, value)
-            out_ref[z, span, :] = value.astype(BF)
-
-
-def final_kernel(got_ref, in_ref, out_ref, loss_ref, *, batch_total):
-    total = jnp.sum(got_ref[...].astype(F32), axis=0)
+            if z == FAR:
+                out_refs[FAR + 4 * i][...] = value.astype(BF)
+            else:
+                out_refs[z][span, :] = value.astype(BF)
+
+
+def near_kernel(up_ref, down_ref, up_far_ref, down_far_ref, up_out, down_out):
+    first = up_far_ref.shape[0]
+    up_out[:first] = (up_ref[:first].astype(F32) + up_far_ref[...].astype(F32)).astype(BF)
+    up_out[first:] = up_ref[first:]
+    down_out[:first] = down_ref[:first]
+    down_out[first:] = (down_ref[first:].astype(F32) + down_far_ref[...].astype(F32)).astype(BF)
+
+
+def final_kernel(*refs, batch_total):
+    got, (in_ref, out_ref, loss_ref) = refs[:7], refs[7:]
+    total = got[0][...].astype(F32)
+    for ref in got[1:]:
+        total += ref[...].astype(F32)
     turned = total.T
     in_rows = in_ref.shape[0]
     out_ref[...] = turned[:OUT_COLS]
@@ -323,13 +339,17 @@
     loss_ref[...] = loss
 
 
+def ahead(value, step):
+    return lax.ppermute(value, "z", [(i, (i + step) % 8) for i in range(8)])
+
+
 def on_device(video_feats, text_feats, weight_in, weight_out, logit_scale):
     rows, d_in = video_feats.shape
     hid, emb = weight_out.shape
     mp_count = lax.axis_size(MP)
     own_rows = rows // mp_count
     batch_total = rows * lax.axis_size(DP)
-    where = [lax.axis_index(name) for name in ("x_lo", "core", MP)]
+    where = [lax.axis_index(name) for name in ("x_lo", "core", MP, "z")]
     where = jnp.stack(where).astype(jnp.int32)
 
     partial_value, pre_bf, text_emb = call(
@@ -382,8 +402,10 @@
     grads = exchange(sent, SPREAD).reshape(2, rows, emb + LANES)
     (grads,) = gate(gelus[0], grads, after=(gelus[1],))
     other = swap(grads, "core")
-    (packed,) = call(
-        grads_kernel, [((z_count, hid, LANES), BF)], LIM[7],
+    first = parts_of(hid, 2)[0].stop
+    sizes = [hid] * FAR + [first] + [hid] * (7 - FAR) + [hid - first]
+    pieces = call(
+        grads_kernel, [((size, LANES), BF) for size in sizes], LIM[7],
         where, grads, other, weight_out, *gelus, *feats_q, scalars=1, raw=True,
         scratch=[
             pltpu.VMEM((4, rows, emb + LANES), BF), pltpu.VMEM((hid, emb), BF),
@@ -391,12 +413,17 @@
             pltpu.VMEM((4 * rows, z_count * LANES), BF), pltpu.SemaphoreType.DMA((13,)),
         ],
     )
-    final = exchange(packed, "z")
+    near = call(
+        near_kernel, [((hid, LANES), BF)] * 2, LIM[9],
+        pieces[3], pieces[5], ahead(pieces[FAR], 1), ahead(pieces[8], -1),
+    )
+    final = [pieces[0], ahead(near[0], 3), ahead(near[1], -3)]
+    final += [ahead(pieces[step], step) for step in (2, 6, 1, 7)]
     in_rows = d_in // lax.axis_size(DP)
     grad_in, grad_out, loss = call(
         functools.partial(final_kernel, batch_total=batch_total),
         [((in_rows, hid), F32), ((OUT_COLS, hid), F32), ((1, 1), F32)],
-        LIM[8], final,
+        LIM[8], *final,
     )
     return (loss.reshape(1), grad_in, grad_out.T)
 

time: 169 us -> 160 us (0.947)
  blocking collectives: 45.3 us -> 0 us
  waiting for transfers between devices: 40.1 us -> 61.1 us
  starting transfers between devices: 40.4 us -> 50.1 us
  Pallas kernels: 35 us -> 38.5 us
    all_to_all x1 -> x0, blocking collectives: 45.3 us -> none  [exchange(): return lax.all_to_all(value, axis, 0, 0)]
    ppermute x0 -> x8, waiting for transfers between devices: none -> 21 us  [ahead(): return lax.ppermute(value, 'z', [(i, (i + step) % 8) for i in range(8)])]
    ppermute x0 -> x8, starting transfers between devices: none -> 9.66 us  [ahead(): return lax.ppermute(value, 'z', [(i, (i + step) % 8) for i in range(8)])]
    pallas_call x9 -> x10, Pallas kernels: 35 us -> 38.5 us  [call(): pl.pallas_call(body, grid=(1,), out_shape=[jax.ShapeDtypeStruct(s, d) for...]
    unnamed x26 -> x32, local copies, waits for them, and re-layouts: 5.55 us -> 6.78 us
  transfers between devices with their start and end apart: 15 -> 23, of which waited for: 10 -> 12; matrix products, arithmetic and copies ran while one was open for 0% -> 0% of each run, Pallas kernels for 9% -> 10%
where the time goes in v5:
time: 160 us; the launch traced here: 159 us
  waiting for transfers between devices  61.1 us (38%)
  starting transfers between devices  50.1 us (31%)
  Pallas kernels  38.5 us (24%)
  local copies, waits for them, and re-layouts  6.78 us (4%)
  between operations  1.67 us (1%)
    pallas_call x10, Pallas kernels, call(): pl.pallas_call(body, grid=(1,), out_shape=[jax.ShapeDtypeStruct(s, d) for...  38.5 us
    all_to_all x5, starting transfers between devices, exchange(): return lax.all_to_all(value, axis, 0, 0)  30.5 us
    all_to_all x5, waiting for transfers between devices, exchange(): return lax.all_to_all(value, axis, 0, 0)  25.7 us
    ppermute x8, waiting for transfers between devices, ahead(): return lax.ppermute(value, 'z', [(i, (i + step) % 8) for i in range(8)])  21 us
    ppermute x10, waiting for transfers between devices, swap(): return lax.ppermute(value, axis, [(0, 1), (1, 0)])  14.4 us
    ppermute x10, starting transfers between devices, swap(): return lax.ppermute(value, axis, [(0, 1), (1, 0)])  9.94 us
    ppermute x8, starting transfers between devices, ahead(): return lax.ppermute(value, 'z', [(i, (i + step) % 8) for i in range(8)])  9.66 us
    unnamed x32, local copies, waits for them, and re-layouts  6.78 us
  transfers between devices with their start and end apart: 23, of which 12 were waited for; matrix products, arithmetic and copies ran while one was open for 0% of the time, Pallas kernels for 10%

profile of v5, /device:TPU:1, one launch (start us, length us, event | category | flops | bytes accessed | tf_op | source)
XLA Modules:
  0.0 158.8 jit_solution(13726795546447612971)
XLA Ops:
  0.6 6.7 %shard_map.76 = (bf16[256,512]{1,0:T(8,128)(2,1)}, bf16[800,256]{1,0:T(8,128)(2,1)}, bf16[256,512]{1,0:T(8,128)(2,1)}) custom-call(bf16[256,512]{1,0:T(8,128)(2,1)} %refs_0_.1, bf16[256,3200]{1,0:T(8,128)(2,1)} %refs_1_.6, bf16[800,3200]{1,0:T(8,128)(2,1)} %bitcast.12, bf16[800,512]{1,0:T(8,128)(2,1)} %refs_3_.3), custom_call_target="tpu_custom_call" | custom-call | flops 1024 | bytes 1024 | tf_op jit(solution)/shard_map/pallas_call | solution.py:80
  7.4 2.1 %collective-permute-start = (bf16[256,512]{1,0:T(8,128)(2,1)}, bf16[256,512]{1,0:T(8,128)(2,1)S(1)}, u32[]{:S(2)}, u32[]{:S(2)}) collective-permute-start(bf16[256,512]{1,0:T(8,128)(2,1)} %get-tuple-element.33.refs_3_), channel_id=1, source_target_pairs={{0,128},{128,0},{1,129},{129,1},{2,130},{130,2},{3,131},{131,3},{4... | collective-permute-start | bytes 786440 | tf_op jit(solution)/shard_map/ppermute | solution.py:42
  9.5 6.4 %all-to-all-start = ((bf16[8,32,512]{2,1,0:T(8,128)(2,1)}), bf16[8,32,512]{2,1,0:T(8,128)(2,1)S(1)}, u32[]{:S(2)}, u32[]{:S(2)}) async-start(bf16[8,32,512]{2,1,0:T(8,128)(2,1)} %bitcast.13), calls=%async_computation | async-start | bytes 524288 | tf_op jit(solution)/shard_map/all_to_all | solution.py:46
  15.9 0.7 pad_add_fusion.refs_0_
  16.5 4.5 %shard_map.77 = (bf16[512,1024]{1,0:T(8,128)(2,1)}, bf16[512,1024]{1,0:T(8,128)(2,1)}) custom-call(s32[4]{0:T(128)} %pad_add_fusion.refs_0_, bf16[256,3200]{1,0:T(8,128)(2,1)} %refs_1_.6), custom_call_target="tpu_custom_call" | custom-call | flops 1024 | bytes 1024 | tf_op jit(solution)/shard_map/pallas_call | solution.py:80
  21.0 2.5 %all-to-all-done.refs_0_ = bf16[8,32,512]{2,1,0:T(8,128)(2,1)S(1)} async-done(((bf16[8,32,512]{2,1,0:T(8,128)(2,1)}), bf16[8,32,512]{2,1,0:T(8,128)(2,1)S(1)}, u32[]{:S(2)}, u32[]{:S(2)}) %all-to-all-start) | async-done | bytes 262176 | tf_op jit(solution)/shard_map/all_to_all | solution.py:46
  23.5 0.0 collective-permute-done.refs_2_.refs_5_
  23.5 0.7 copy-done.13
  24.2 0.1 copy-done.1
  24.3 1.8 %shard_map.78 = (f32[32,512]{1,0:T(8,128)}, f32[32,128]{1,0:T(8,128)}, bf16[8,32,512]{2,1,0:T(8,128)(2,1)}) custom-call(bf16[8,32,512]{2,1,0:T(8,128)(2,1)} %copy-done.13, bf16[512,1024]{1,0:T(8,128)(2,1)} %get-tuple-element.32.refs_1_.refs_6_, bf16[256,512]{1,0:T(8,128)(2,1)} %copy-done.1), custom_call_target="tpu_custom_call" | custom-call | flops 1024 | bytes 1024 | tf_op jit(solution)/shard_map/pallas_call | solution.py:80
  26.2 0.1 collective-permute-start.7
  26.3 8.3 %all-to-all-start.1 = ((bf16[8,32,512]{2,1,0:T(8,128)(2,1)}), bf16[8,32,512]{2,1,0:T(8,128)(2,1)S(1)}, u32[]{:S(2)}, u32[]{:S(2)}) async-start(bf16[8,32,512]{2,1,0:T(8,128)(2,1)} %get-tuple-element.38), calls=%async_computation.1 | async-start | bytes 524288 | tf_op jit(solution)/shard_map/all_to_all | solution.py:46
  34.6 2.9 %collective-permute-start.4 = (bf16[256,512]{1,0:T(8,128)(2,1)S(1)}, bf16[256,512]{1,0:T(8,128)(2,1)S(1)}, u32[]{:S(2)}, u32[]{:S(2)}) collective-permute-start(bf16[256,512]{1,0:T(8,128)(2,1)S(1)} %copy-done), channel_id=1, source_target_pairs={{0,8},{8,0},{1,9},{9,1},{2,10},{10,2},{3,11},{11,3},{4,12},{12,4},... | collective-permute-start | bytes 786440 | tf_op jit(solution)/shard_map/ppermute | solution.py:42
  37.6 0.1 collective-permute-start.5
  38.3 0.4 collective-permute-done.4.refs_4_
  38.7 0.4 collective-permute-done.5.refs_6_
  39.1 4.9 %all-to-all-done.1.refs_2_ = bf16[8,32,512]{2,1,0:T(8,128)(2,1)S(1)} async-done(((bf16[8,32,512]{2,1,0:T(8,128)(2,1)}), bf16[8,32,512]{2,1,0:T(8,128)(2,1)S(1)}, u32[]{:S(2)}, u32[]{:S(2)}) %all-to-all-start.1) | async-done | bytes 262176 | tf_op jit(solution)/shard_map/all_to_all | solution.py:46
  44.0 1.8 %shard_map.80 = f32[32,8,128]{2,1,0:T(8,128)} custom-call(s32[4]{0:T(128)S(1)} %copy-done.6, f32[1]{0:T(128)S(6)} %copy.14.refs_1_, bf16[8,32,512]{2,1,0:T(8,128)(2,1)S(1)} %all-to-all-done.1.refs_2_, bf16[256,512]{1,0:T(8,128)(2,1)S(1)} %copy-done, bf16[256,512]{1,0:T(8,128)(2,1)S(1)} %collective-permute-done.4.refs_4_, bf16[256,512]{1,0:T(8,128)(2,1)S(1)} %copy-done.2, ...), custom_call_target="tpu_custom_call" | custom-call | flops 1024 | bytes 1024 | tf_op jit(solution)/shard_map/pallas_call | solution.py:80
  45.9 8.5 %all-to-all-start.2 = ((f32[32,8,128]{2,1,0:T(8,128)}), f32[32,8,128]{2,1,0:T(8,128)S(1)}, u32[]{:S(2)}, u32[]{:S(2)}) async-start(f32[32,8,128]{2,1,0:T(8,128)} %shard_map.80), calls=%async_computation.2 | async-start | bytes 262144 | tf_op jit(solution)/shard_map/all_to_all | solution.py:46
  54.4 0.3 collective-permute-start.6
  54.7 0.0 collective-permute-done.7.refs_8_
  54.7 0.3 collective-permute-start.8
  55.0 7.1 %all-to-all-done.2.refs_7_ = f32[32,8,128]{2,1,0:T(8,128)S(1)} async-done(((f32[32,8,128]{2,1,0:T(8,128)}), f32[32,8,128]{2,1,0:T(8,128)S(1)}, u32[]{:S(2)}, u32[]{:S(2)}) %all-to-all-start.2) | async-done | bytes 131104 | tf_op jit(solution)/shard_map/all_to_all | solution.py:46
  62.0 3.1 %shard_map.81 = (bf16[8,32,1152]{2,1,0:T(8,128)(2,1)}, f32[8,128]{1,0:T(8,128)S(1)}) custom-call(s32[4]{0:T(128)S(1)} %copy-done.6, f32[1]{0:T(128)S(6)} %copy.14.refs_1_, bf16[8,32,512]{2,1,0:T(8,128)(2,1)S(1)} %all-to-all-done.1.refs_2_, bf16[256,512]{1,0:T(8,128)(2,1)S(1)} %copy-done, bf16[256,512]{1,0:T(8,128)(2,1)S(1)} %collective-permute-done.4.refs_4_, ...), custom_call_target="tpu_custom_call" | custom-call | flops 1024 | bytes 1024 | tf_op jit(solution)/shard_map/pallas_call | solution.py:80
  65.1 0.0 copy-start.7
  65.1 0.6 copy-done.7
  65.7 3.5 %all-to-all-start.3 = ((bf16[8,32,1152]{2,1,0:T(8,128)(2,1)}), bf16[8,32,1152]{2,1,0:T(8,128)(2,1)S(1)}, u32[]{:S(2)}, u32[]{:S(2)}) async-start(bf16[8,32,1152]{2,1,0:T(8,128)(2,1)} %get-tuple-element.39), calls=%async_computation.3 | async-start | bytes 1179648 | tf_op jit(solution)/shard_map/all_to_all | solution.py:46
  69.3 0.4 collective-permute-start.2
  69.7 0.5 collective-permute-start.1
  70.2 10.2 %collective-permute-done.2.refs_2_ = bf16[800,256]{1,0:T(8,128)(2,1)S(1)} collective-permute-done((bf16[800,256]{1,0:T(8,128)(2,1)}, bf16[800,256]{1,0:T(8,128)(2,1)S(1)}, u32[]{:S(2)}, u32[]{:S(2)}) %collective-permute-start.2) | collective-permute-done | bytes 409632 | tf_op jit(solution)/shard_map/ppermute | solution.py:42
  80.4 1.1 collective-permute-start.3
  81.5 0.0 collective-permute-done.1.refs_9_.refs_1_
  81.5 1.5 collective-permute-done.3.refs_10_.refs_3_
  83.0 5.7 %all-to-all-done.3.refs_2_ = bf16[8,32,1152]{2,1,0:T(8,128)(2,1)S(1)} async-done(((bf16[8,32,1152]{2,1,0:T(8,128)(2,1)}), bf16[8,32,1152]{2,1,0:T(8,128)(2,1)S(1)}, u32[]{:S(2)}, u32[]{:S(2)}) %all-to-all-start.3) | async-done | bytes 589856 | tf_op jit(solution)/shard_map/all_to_all | solution.py:46
  88.6 0.8 copy-done.11
  89.5 3.1 %shard_map.82.refs_4_ = bf16[16,32,640]{2,1,0:T(8,128)(2,1)} custom-call(s32[4]{0:T(128)} %pad_add_fusion.refs_0_, f32[1]{0:T(128)S(6)} %copy.14.refs_1_, bf16[8,32,1152]{2,1,0:T(8,128)(2,1)} %copy-done.11, f32[32,512]{1,0:T(8,128)} %get-tuple-element.40.refs_3_, f32[32,128]{1,0:T(8,128)} %get-tuple-element.34.refs_0_.refs_4_, bf16[8,32,512]{2,1,0:T(8,128)(2,1)} %bitcast.10, ...), custom_call_target="tpu_custom_call" | custom-call | flops 1024 | bytes 1024 | tf_op jit(solution)/shard_map/pallas_call | solution.py:80
  92.5 3.8 %all-to-all-start.4 = ((bf16[16,32,640]{2,1,0:T(8,128)(2,1)}), bf16[16,32,640]{2,1,0:T(8,128)(2,1)S(1)}, u32[]{:S(2)}, u32[]{:S(2)}) async-start(bf16[16,32,640]{2,1,0:T(8,128)(2,1)} %shard_map.82.refs_4_), calls=%async_computation.4 | async-start | bytes 1310720 | tf_op jit(solution)/shard_map/all_to_all | solution.py:46
  96.3 5.3 %shard_map.83 = (bf16[800,1024]{1,0:T(8,128)(2,1)}, bf16[800,1024]{1,0:T(8,128)(2,1)}) custom-call(bf16[800,256]{1,0:T(8,128)(2,1)} %get-tuple-element.37.refs_0_, bf16[800,256]{1,0:T(8,128)(2,1)} %copy-done.12, bf16[800,256]{1,0:T(8,128)(2,1)} %copy-done.15, bf16[800,256]{1,0:T(8,128)(2,1)} %collective-permute-done.3.refs_10_.refs_3_, ...), custom_call_target="tpu_custom_call" | custom-call | flops 1024 | bytes 1024 | tf_op jit(solution)/shard_map/pallas_call | solution.py:80
  101.6 5.6 %all-to-all-done.4 = bf16[16,32,640]{2,1,0:T(8,128)(2,1)S(1)} async-done(((bf16[16,32,640]{2,1,0:T(8,128)(2,1)}), bf16[16,32,640]{2,1,0:T(8,128)(2,1)S(1)}, u32[]{:S(2)}, u32[]{:S(2)}) %all-to-all-start.4) | async-done | bytes 655392 | tf_op jit(solution)/shard_map/all_to_all | solution.py:46
  107.2 0.9 copy-done.8
  108.1 2.1 %collective-permute-start.9 = (bf16[2,256,640]{2,1,0:T(8,128)(2,1)}, bf16[2,256,640]{2,1,0:T(8,128)(2,1)S(1)}, u32[]{:S(2)}, u32[]{:S(2)}) collective-permute-start(bf16[2,256,640]{2,1,0:T(8,128)(2,1)} %shard_map.84.refs_1_), channel_id=1, source_target_pairs={{0,8},{8,0},{1,9},{9,1},{2,10},{10,2},{3,11},{11,3},{4,12},{12,4},... | collective-permute-start | bytes 1966088 | tf_op jit(solution)/shard_map/ppermute | solution.py:42
  110.2 1.9 %collective-permute-done.9.refs_2_ = bf16[2,256,640]{2,1,0:T(8,128)(2,1)S(1)} collective-permute-done((bf16[2,256,640]{2,1,0:T(8,128)(2,1)}, bf16[2,256,640]{2,1,0:T(8,128)(2,1)S(1)}, u32[]{:S(2)}, u32[]{:S(2)}) %collective-permute-start.9) | collective-permute-done | bytes 655392 | tf_op jit(solution)/shard_map/ppermute | solution.py:42
  112.1 0.9 copy-done.14
  113.0 8.4 %shard_map.85 = (bf16[800,128]{1,0:T(8,128)(2,1)}, bf16[800,128]{1,0:T(8,128)(2,1)}, bf16[800,128]{1,0:T(8,128)(2,1)}, bf16[800,128]{1,0:T(8,128)(2,1)}, bf16[40...) custom-call(s32[4]{0:T(128)} %pad_add_fusion.refs_0_, ...), custom_call_target="tpu_custom_call" | custom-call | flops 1024 | bytes 1024 | tf_op jit(solution)/shard_map/pallas_call | solution.py:80
  121.4 0.1 collective-permute-start.14
  121.5 0.1 collective-permute-start.10
  121.6 2.7 %collective-permute-start.11 = (bf16[400,128]{1,0:T(8,128)(2,1)}, bf16[400,128]{1,0:T(8,128)(2,1)S(1)}, u32[]{:S(2)}, u32[]{:S(2)}) collective-permute-start(bf16[400,128]{1,0:T(8,128)(2,1)} %get-tuple-element.49), channel_id=1, source_target_pairs={{0,112},{16,0},{32,16},{48,32},{64,48},{80,64},{96,80},{112,96},{1... | collective-permute-start | bytes 307208 | tf_op jit(solution)/shard_map/ppermute | solution.py:343
  124.3 2.3 %collective-permute-start.15 = (bf16[800,128]{1,0:T(8,128)(2,1)}, bf16[800,128]{1,0:T(8,128)(2,1)S(1)}, u32[]{:S(2)}, u32[]{:S(2)}) collective-permute-start(bf16[800,128]{1,0:T(8,128)(2,1)} %get-tuple-element.53), channel_id=1, source_target_pairs={{0,96},{16,112},{32,0},{48,16},{64,32},{80,48},{96,64},{112,80},{1... | collective-permute-start | bytes 614408 | tf_op jit(solution)/shard_map/ppermute | solution.py:343
  126.6 8.6 %collective-permute-done.10.refs_2_ = bf16[400,128]{1,0:T(8,128)(2,1)S(1)} collective-permute-done((bf16[400,128]{1,0:T(8,128)(2,1)}, bf16[400,128]{1,0:T(8,128)(2,1)S(1)}, u32[]{:S(2)}, u32[]{:S(2)}) %collective-permute-start.10) | collective-permute-done | bytes 102432 | tf_op jit(solution)/shard_map/ppermute | solution.py:343
  135.2 0.0 collective-permute-start.17
  135.2 0.0 collective-permute-done.11.refs_3_
  135.2 0.9 copy-done.3
  136.1 0.9 copy-done.4
  137.1 0.8 shard_map.86
  137.9 0.5 collective-permute-start.12
  138.4 0.0 collective-permute-done.14.refs_3_
  138.4 4.1 %collective-permute-start.13 = (bf16[800,128]{1,0:T(8,128)(2,1)S(1)}, bf16[800,128]{1,0:T(8,128)(2,1)S(1)}, u32[]{:S(2)}, u32[]{:S(2)}) collective-permute-start(bf16[800,128]{1,0:T(8,128)(2,1)S(1)} %get-tuple-element.51), channel_id=1, source_target_pairs={{0,80},{16,96},{32,112},{48,0},{64,16},{80,32},{96,48},{112,64},{1... | collective-permute-start | bytes 614408 | tf_op jit(solution)/shard_map/ppermute | solution.py:343
  142.5 0.0 collective-permute-done.15.refs_4_
  142.5 0.0 collective-permute-done.16.refs_5_
  142.5 0.0 collective-permute-done.17.refs_6_
  142.5 12.4 %collective-permute-done.12.refs_1_ = bf16[800,128]{1,0:T(8,128)(2,1)S(1)} collective-permute-done((bf16[800,128]{1,0:T(8,128)(2,1)S(1)}, bf16[800,128]{1,0:T(8,128)(2,1)S(1)}, u32[]{:S(2)}, u32[]{:S(2)}) %collective-permute-start.12) | collective-permute-done | bytes 204832 | tf_op jit(solution)/shard_map/ppermute | solution.py:343
  154.9 0.0 collective-permute-done.13.refs_2_
  154.9 0.9 copy-done.5
  155.8 2.9 %shard_map.87 = (f32[100,800]{1,0:T(8,128)}, f32[16,800]{1,0:T(8,128)}, f32[1,1]{1,0:T(1,128)}) custom-call(bf16[800,128]{1,0:T(8,128)(2,1)S(1)} %copy-done.5, bf16[800,128]{1,0:T(8,128)(2,1)S(1)} %collective-permute-done.12.refs_1_, bf16[800,128]{1,0:T(8,128)(2,1)S(1)} %collective-permute-done.13.refs_2_, ...), custom_call_target="tpu_custom_call" | custom-call | flops 1024 | bytes 1024 | tf_op jit(solution)/shard_map/pallas_call | solution.py:80
  (27 shorter events, 0.1 us)
Async XLA Ops:
  7.4 16.1 %collective-permute-start = (bf16[256,512]{1,0:T(8,128)(2,1)}, bf16[256,512]{1,0:T(8,128)(2,1)S(1)}, u32[]{:S(2)}, u32[]{:S(2)}) collective-permute-start(bf16[256,512]{1,0:T(8,128)(2,1)} %get-tuple-element.33.refs_3_), channel_id=1, source_target_pairs={{0,128},{128,0},{1,129},{129,1},{2,130},{130,2},{3,131},{131,3},{4... | collective-permute-start | bytes 786440 | tf_op jit(solution)/shard_map/ppermute | solution.py:42
  9.5 14.0 %all-to-all-start = ((bf16[8,32,512]{2,1,0:T(8,128)(2,1)}), bf16[8,32,512]{2,1,0:T(8,128)(2,1)S(1)}, u32[]{:S(2)}, u32[]{:S(2)}) async-start(bf16[8,32,512]{2,1,0:T(8,128)(2,1)} %bitcast.13), calls=%async_computation | async-start | bytes 524288 | tf_op jit(solution)/shard_map/all_to_all | solution.py:46
  23.5 0.7 copy-start.13
  23.5 0.8 copy-start.1
  24.3 10.3 %copy-start = (bf16[256,512]{1,0:T(8,128)(2,1)S(1)}, bf16[256,512]{1,0:T(8,128)(2,1)}, u32[]{:S(2)}) copy-start(bf16[256,512]{1,0:T(8,128)(2,1)} %get-tuple-element.33.refs_3_) | copy-start | bytes 786436
  24.3 19.7 %copy-start.6 = (s32[4]{0:T(128)S(1)}, s32[4]{0:T(128)}, u32[]{:S(2)}) copy-start(s32[4]{0:T(128)} %pad_add_fusion.refs_0_) | copy-start | bytes 52
  26.1 11.4 %copy-start.2 = (bf16[256,512]{1,0:T(8,128)(2,1)S(1)}, bf16[256,512]{1,0:T(8,128)(2,1)}, u32[]{:S(2)}) copy-start(bf16[256,512]{1,0:T(8,128)(2,1)} %copy-done.1) | copy-start | bytes 786436
  26.2 28.2 %copy-start.9 = (bf16[512,1024]{1,0:T(8,128)(2,1)S(1)}, bf16[512,1024]{1,0:T(8,128)(2,1)}, u32[]{:S(2)}) copy-start(bf16[512,1024]{1,0:T(8,128)(2,1)} %get-tuple-element.32.refs_1_.refs_6_) | copy-start | bytes 3145732
  26.2 28.5 %collective-permute-start.7 = (bf16[512,1024]{1,0:T(8,128)(2,1)}, bf16[512,1024]{1,0:T(8,128)(2,1)}, u32[]{:S(2)}, u32[]{:S(2)}) collective-permute-start(bf16[512,1024]{1,0:T(8,128)(2,1)} %get-tuple-element.42), channel_id=1, source_target_pairs={{0,128},{128,0},{1,129},{129,1},{2,130},{130,2},{3,131},{131,3},{4... | collective-permute-start | bytes 3145736 | tf_op jit(solution)/shard_map/ppermute | solution.py:42
  26.3 17.7 %all-to-all-start.1 = ((bf16[8,32,512]{2,1,0:T(8,128)(2,1)}), bf16[8,32,512]{2,1,0:T(8,128)(2,1)S(1)}, u32[]{:S(2)}, u32[]{:S(2)}) async-start(bf16[8,32,512]{2,1,0:T(8,128)(2,1)} %get-tuple-element.38), calls=%async_computation.1 | async-start | bytes 524288 | tf_op jit(solution)/shard_map/all_to_all | solution.py:46
  34.6 4.1 %collective-permute-start.4 = (bf16[256,512]{1,0:T(8,128)(2,1)S(1)}, bf16[256,512]{1,0:T(8,128)(2,1)S(1)}, u32[]{:S(2)}, u32[]{:S(2)}) collective-permute-start(bf16[256,512]{1,0:T(8,128)(2,1)S(1)} %copy-done), channel_id=1, source_target_pairs={{0,8},{8,0},{1,9},{9,1},{2,10},{10,2},{3,11},{11,3},{4,12},{12,4},... | collective-permute-start | bytes 786440 | tf_op jit(solution)/shard_map/ppermute | solution.py:42
  37.6 1.5 collective-permute-start.5
  45.9 16.2 %all-to-all-start.2 = ((f32[32,8,128]{2,1,0:T(8,128)}), f32[32,8,128]{2,1,0:T(8,128)S(1)}, u32[]{:S(2)}, u32[]{:S(2)}) async-start(f32[32,8,128]{2,1,0:T(8,128)} %shard_map.80), calls=%async_computation.2 | async-start | bytes 262144 | tf_op jit(solution)/shard_map/all_to_all | solution.py:46
  54.4 27.1 %collective-permute-start.6 = (bf16[512,1024]{1,0:T(8,128)(2,1)S(1)}, bf16[512,1024]{1,0:T(8,128)(2,1)S(1)}, u32[]{:S(2)}, u32[]{:S(2)}) collective-permute-start(bf16[512,1024]{1,0:T(8,128)(2,1)S(1)} %copy-done.9), channel_id=1, source_target_pairs={{0,8},{8,0},{1,9},{9,1},{2,10},{10,2},{3,11},{11,3},{4,12},{12,4},... | collective-permute-start | bytes 3145736 | tf_op jit(solution)/shard_map/ppermute | solution.py:42
  54.7 34.0 %collective-permute-start.8 = (bf16[512,1024]{1,0:T(8,128)(2,1)}, bf16[512,1024]{1,0:T(8,128)(2,1)}, u32[]{:S(2)}, u32[]{:S(2)}) collective-permute-start(bf16[512,1024]{1,0:T(8,128)(2,1)} %collective-permute-done.7.refs_8_), channel_id=1, source_target_pairs={{0,8},{8,0},{1,9},{9,1},{2,10},{10,2},{3,11},{11,3},{4,12},{12,4},... | collective-permute-start | bytes 3145736 | tf_op jit(solution)/shard_map/ppermute | solution.py:42
  65.1 0.6 copy-start.7
  65.7 22.9 %all-to-all-start.3 = ((bf16[8,32,1152]{2,1,0:T(8,128)(2,1)}), bf16[8,32,1152]{2,1,0:T(8,128)(2,1)S(1)}, u32[]{:S(2)}, u32[]{:S(2)}) async-start(bf16[8,32,1152]{2,1,0:T(8,128)(2,1)} %get-tuple-element.39), calls=%async_computation.3 | async-start | bytes 1179648 | tf_op jit(solution)/shard_map/all_to_all | solution.py:46
  69.3 11.1 %collective-permute-start.2 = (bf16[800,256]{1,0:T(8,128)(2,1)}, bf16[800,256]{1,0:T(8,128)(2,1)S(1)}, u32[]{:S(2)}, u32[]{:S(2)}) collective-permute-start(bf16[800,256]{1,0:T(8,128)(2,1)} %get-tuple-element.37.refs_0_), channel_id=1, source_target_pairs={{0,128},{128,0},{1,129},{129,1},{2,130},{130,2},{3,131},{131,3},{4... | collective-permute-start | bytes 1228808 | tf_op jit(solution)/shard_map/ppermute | solution.py:42
  69.7 11.8 %collective-permute-start.1 = (bf16[800,256]{1,0:T(8,128)(2,1)}, bf16[800,256]{1,0:T(8,128)(2,1)S(1)}, u32[]{:S(2)}, u32[]{:S(2)}) collective-permute-start(bf16[800,256]{1,0:T(8,128)(2,1)} %get-tuple-element.37.refs_0_), channel_id=1, source_target_pairs={{0,8},{8,0},{1,9},{9,1},{2,10},{10,2},{3,11},{11,3},{4,12},{12,4},... | collective-permute-start | bytes 1228808 | tf_op jit(solution)/shard_map/ppermute | solution.py:42
  80.4 1.1 copy-start.15
  80.4 2.6 %collective-permute-start.3 = (bf16[800,256]{1,0:T(8,128)(2,1)S(1)}, bf16[800,256]{1,0:T(8,128)(2,1)}, u32[]{:S(2)}, u32[]{:S(2)}) collective-permute-start(bf16[800,256]{1,0:T(8,128)(2,1)S(1)} %collective-permute-done.2.refs_2_), channel_id=1, source_target_pairs={{0,8},{8,0},{1,9},{9,1},{2,10},{10,2},{3,11},{11,3},{4,12},{12,4},... | collective-permute-start | bytes 1228808 | tf_op jit(solution)/shard_map/ppermute | solution.py:42
  81.5 7.2 %copy-start.12 = (bf16[800,256]{1,0:T(8,128)(2,1)}, bf16[800,256]{1,0:T(8,128)(2,1)S(1)}, u32[]{:S(2)}) copy-start(bf16[800,256]{1,0:T(8,128)(2,1)S(1)} %collective-permute-done.1.refs_9_.refs_1_) | copy-start | bytes 1228804
  81.5 7.2 %copy-start.10 = (bf16[512,1024]{1,0:T(8,128)(2,1)}, bf16[512,1024]{1,0:T(8,128)(2,1)S(1)}, u32[]{:S(2)}) copy-start(bf16[512,1024]{1,0:T(8,128)(2,1)S(1)} %collective-permute-done.6.refs_7_) | copy-start | bytes 3145732
  88.6 0.8 copy-start.11
  92.5 14.7 %all-to-all-start.4 = ((bf16[16,32,640]{2,1,0:T(8,128)(2,1)}), bf16[16,32,640]{2,1,0:T(8,128)(2,1)S(1)}, u32[]{:S(2)}, u32[]{:S(2)}) async-start(bf16[16,32,640]{2,1,0:T(8,128)(2,1)} %shard_map.82.refs_4_), calls=%async_computation.4 | async-start | bytes 1310720 | tf_op jit(solution)/shard_map/all_to_all | solution.py:46
  107.2 0.9 copy-start.8
  108.1 4.0 %collective-permute-start.9 = (bf16[2,256,640]{2,1,0:T(8,128)(2,1)}, bf16[2,256,640]{2,1,0:T(8,128)(2,1)S(1)}, u32[]{:S(2)}, u32[]{:S(2)}) collective-permute-start(bf16[2,256,640]{2,1,0:T(8,128)(2,1)} %shard_map.84.refs_1_), channel_id=1, source_target_pairs={{0,8},{8,0},{1,9},{9,1},{2,10},{10,2},{3,11},{11,3},{4,12},{12,4},... | collective-permute-start | bytes 1966088 | tf_op jit(solution)/shard_map/ppermute | solution.py:42
  112.1 0.9 copy-start.14
  121.4 16.9 %collective-permute-start.14 = (bf16[800,128]{1,0:T(8,128)(2,1)}, bf16[800,128]{1,0:T(8,128)(2,1)S(1)}, u32[]{:S(2)}, u32[]{:S(2)}) collective-permute-start(bf16[800,128]{1,0:T(8,128)(2,1)} %get-tuple-element.52), channel_id=1, source_target_pairs={{0,32},{16,48},{32,64},{48,80},{64,96},{80,112},{96,0},{112,16},{1... | collective-permute-start | bytes 614408 | tf_op jit(solution)/shard_map/ppermute | solution.py:343
  121.5 13.7 %collective-permute-start.10 = (bf16[400,128]{1,0:T(8,128)(2,1)}, bf16[400,128]{1,0:T(8,128)(2,1)S(1)}, u32[]{:S(2)}, u32[]{:S(2)}) collective-permute-start(bf16[400,128]{1,0:T(8,128)(2,1)} %get-tuple-element.48), channel_id=1, source_target_pairs={{0,16},{16,32},{32,48},{48,64},{64,80},{80,96},{96,112},{112,0},{1... | collective-permute-start | bytes 307208 | tf_op jit(solution)/shard_map/ppermute | solution.py:343
  121.6 13.6 %collective-permute-start.11 = (bf16[400,128]{1,0:T(8,128)(2,1)}, bf16[400,128]{1,0:T(8,128)(2,1)S(1)}, u32[]{:S(2)}, u32[]{:S(2)}) collective-permute-start(bf16[400,128]{1,0:T(8,128)(2,1)} %get-tuple-element.49), channel_id=1, source_target_pairs={{0,112},{16,0},{32,16},{48,32},{64,48},{80,64},{96,80},{112,96},{1... | collective-permute-start | bytes 307208 | tf_op jit(solution)/shard_map/ppermute | solution.py:343
  124.3 18.2 %collective-permute-start.15 = (bf16[800,128]{1,0:T(8,128)(2,1)}, bf16[800,128]{1,0:T(8,128)(2,1)S(1)}, u32[]{:S(2)}, u32[]{:S(2)}) collective-permute-start(bf16[800,128]{1,0:T(8,128)(2,1)} %get-tuple-element.53), channel_id=1, source_target_pairs={{0,96},{16,112},{32,0},{48,16},{64,32},{80,48},{96,64},{112,80},{1... | collective-permute-start | bytes 614408 | tf_op jit(solution)/shard_map/ppermute | solution.py:343
  126.6 15.9 %collective-permute-start.16 = (bf16[800,128]{1,0:T(8,128)(2,1)}, bf16[800,128]{1,0:T(8,128)(2,1)S(1)}, u32[]{:S(2)}, u32[]{:S(2)}) collective-permute-start(bf16[800,128]{1,0:T(8,128)(2,1)} %get-tuple-element.54), channel_id=1, source_target_pairs={{0,16},{16,32},{32,48},{48,64},{64,80},{80,96},{96,112},{112,0},{1... | collective-permute-start | bytes 614408 | tf_op jit(solution)/shard_map/ppermute | solution.py:343
  135.2 7.3 %collective-permute-start.17 = (bf16[800,128]{1,0:T(8,128)(2,1)}, bf16[800,128]{1,0:T(8,128)(2,1)S(1)}, u32[]{:S(2)}, u32[]{:S(2)}) collective-permute-start(bf16[800,128]{1,0:T(8,128)(2,1)} %get-tuple-element.55), channel_id=1, source_target_pairs={{0,112},{16,0},{32,16},{48,32},{64,48},{80,64},{96,80},{112,96},{1... | collective-permute-start | bytes 614408 | tf_op jit(solution)/shard_map/ppermute | solution.py:343
  135.2 0.9 copy-start.3
  136.1 0.9 copy-start.4
  137.9 16.9 %collective-permute-start.12 = (bf16[800,128]{1,0:T(8,128)(2,1)S(1)}, bf16[800,128]{1,0:T(8,128)(2,1)S(1)}, u32[]{:S(2)}, u32[]{:S(2)}) collective-permute-start(bf16[800,128]{1,0:T(8,128)(2,1)S(1)} %get-tuple-element.50), channel_id=1, source_target_pairs={{0,48},{16,64},{32,80},{48,96},{64,112},{80,0},{96,16},{112,32},{1... | collective-permute-start | bytes 614408 | tf_op jit(solution)/shard_map/ppermute | solution.py:343
  138.4 16.5 %collective-permute-start.13 = (bf16[800,128]{1,0:T(8,128)(2,1)S(1)}, bf16[800,128]{1,0:T(8,128)(2,1)S(1)}, u32[]{:S(2)}, u32[]{:S(2)}) collective-permute-start(bf16[800,128]{1,0:T(8,128)(2,1)S(1)} %get-tuple-element.51), channel_id=1, source_target_pairs={{0,80},{16,96},{32,112},{48,0},{64,16},{80,32},{96,48},{112,64},{1... | collective-permute-start | bytes 614408 | tf_op jit(solution)/shard_map/ppermute | solution.py:343
  154.9 0.9 copy-start.5

commit v6 on v5

--- a/solution.py
+++ b/solution.py
@@ -52,7 +52,8 @@
     return first, second, value - first - second
 
 
-def call(kernel, outs, vmem, *args, scalars=0, scratch=(), after=(), raw=False):
+def call(kernel, outs, vmem, *args, scalars=0, scratch=(), after=(), raw=False, direct=False):
+    raw = raw or direct
     held = [] if raw else list(args[scalars:])
     total = len(args) + len(after)
 
@@ -77,11 +78,13 @@
     if held:
         places.append(pltpu.SemaphoreType.DMA((len(held),)))
     anywhere = pl.BlockSpec(memory_space=pl.ANY)
+    place = pl.BlockSpec(memory_space=pltpu.VMEM) if direct else anywhere
     return pl.pallas_call(
         body,
         grid=(1,),
         out_shape=[jax.ShapeDtypeStruct(s, d) for s, d in outs],
-        in_specs=[pl.BlockSpec(memory_space=pltpu.SMEM)] * scalars + [anywhere] * (total - scalars),
+        in_specs=[pl.BlockSpec(memory_space=pltpu.SMEM)] * scalars
+        + [place] * (len(args) - scalars) + [anywhere] * len(after),
         out_specs=[whole(s) for s, _ in outs],
         scratch_shapes=[*places, *scratch],
         compiler_params=pltpu.CompilerParams(vmem_limit_bytes=vmem * MIB),
@@ -115,7 +118,7 @@
     text_hbm, feats_hbm, win_hbm, wout_hbm, partial_ref, pre_ref, emb_ref,
     text_ref, feats_ref, win_ref, wout_ref, hidden_ref, sems,
 ):
-    spans = parts_of(win_ref.shape[0], 3)
+    spans = parts_of(win_ref.shape[0], 1)
     copies = [
         pltpu.make_async_copy(text_hbm, text_ref, sems.at[0]),
         pltpu.make_async_copy(feats_hbm, feats_ref, sems.at[1]),
@@ -379,7 +382,7 @@
     video_rows = exchange(video, "z")
     (cols,) = call(
         logits_kernel, [((4 * mp_count, 8, LANES), F32)], LIM[3],
-        where, logit_scale, video_rows, text_emb, *texts, scalars=2,
+        where, logit_scale, video_rows, text_emb, *texts, scalars=2, direct=True,
         scratch=[pltpu.VMEM((8, LANES), F32)],
     )
     cols = exchange(cols, PLANE)
@@ -387,7 +390,7 @@
     pre = (pre_own, swap(pre_own, "core"), pre_x, swap(pre_x, "core"))
     packed, logs = call(
         weights_kernel, [((8, own_rows, 2 * emb + LANES), BF), ((8, LANES), F32)], LIM[4],
-        where, logit_scale, video_rows, text_emb, *texts, cols, scalars=2,
+        where, logit_scale, video_rows, text_emb, *texts, cols, scalars=2, direct=True,
         scratch=[pltpu.VMEM((8, LANES), F32)],
     )
     feats_q = (feats, swap(feats, "core"), feats_x, swap(feats_x, "core"))
@@ -415,7 +418,7 @@
     )
     near = call(
         near_kernel, [((hid, LANES), BF)] * 2, LIM[9],
-        pieces[3], pieces[5], ahead(pieces[FAR], 1), ahead(pieces[8], -1),
+        pieces[3], pieces[5], ahead(pieces[FAR], 1), ahead(pieces[8], -1), direct=True,
     )
     final = [pieces[0], ahead(near[0], 3), ahead(near[1], -3)]
     final += [ahead(pieces[step], step) for step in (2, 6, 1, 7)]
@@ -423,7 +426,7 @@
     grad_in, grad_out, loss = call(
         functools.partial(final_kernel, batch_total=batch_total),
         [((in_rows, hid), F32), ((OUT_COLS, hid), F32), ((1, 1), F32)],
-        LIM[8], *final,
+        LIM[8], *final, direct=True,
     )
     return (loss.reshape(1), grad_in, grad_out.T)
 

time: 160 us -> 157 us (0.981)
  Pallas kernels: 38.5 us -> 35.1 us
    pallas_call x10, Pallas kernels: 38.5 us -> 35.1 us  [call(): pl.pallas_call(body, grid=(1,), out_shape=[jax.ShapeDtypeStruct(s, d) for...]
  transfers between devices with their start and end apart: 23 -> 23, of which waited for: 12 -> 12; matrix products, arithmetic and copies ran while one was open for 0% -> 0% of each run, Pallas kernels for 10% -> 9%
where the time goes in v6:
time: 157 us; the launch traced here: 155 us
  waiting for transfers between devices  61.2 us (39%)
  starting transfers between devices  50.1 us (32%)
  Pallas kernels  35.1 us (22%)
  local copies, waits for them, and re-layouts  6.79 us (4%)
    pallas_call x10, Pallas kernels, call(): pl.pallas_call(body, grid=(1,), out_shape=[jax.ShapeDtypeStruct(s, d) for...  35.1 us
    all_to_all x5, starting transfers between devices, exchange(): return lax.all_to_all(value, axis, 0, 0)  30.5 us
    all_to_all x5, waiting for transfers between devices, exchange(): return lax.all_to_all(value, axis, 0, 0)  25.7 us
    ppermute x8, waiting for transfers between devices, ahead(): return lax.ppermute(value, 'z', [(i, (i + step) % 8) for i in range(8)])  21.1 us
    ppermute x10, waiting for transfers between devices, swap(): return lax.ppermute(value, axis, [(0, 1), (1, 0)])  14.4 us
    ppermute x10, starting transfers between devices, swap(): return lax.ppermute(value, axis, [(0, 1), (1, 0)])  9.95 us
    ppermute x8, starting transfers between devices, ahead(): return lax.ppermute(value, 'z', [(i, (i + step) % 8) for i in range(8)])  9.66 us
    unnamed x32, local copies, waits for them, and re-layouts  6.79 us
  transfers between devices with their start and end apart: 23, of which 12 were waited for; matrix products, arithmetic and copies ran while one was open for 0% of the time, Pallas kernels for 9%

profile of v6, /device:TPU:1, one launch (start us, length us, event | category | flops | bytes accessed | tf_op | source)
XLA Modules:
  0.0 155.3 jit_solution(6005110281571403444)
XLA Ops:
  0.6 6.4 %shard_map.76 = (bf16[256,512]{1,0:T(8,128)(2,1)}, bf16[800,256]{1,0:T(8,128)(2,1)}, bf16[256,512]{1,0:T(8,128)(2,1)}) custom-call(bf16[256,512]{1,0:T(8,128)(2,1)} %refs_0_.1, bf16[256,3200]{1,0:T(8,128)(2,1)} %refs_1_.6, bf16[800,3200]{1,0:T(8,128)(2,1)} %bitcast.12, bf16[800,512]{1,0:T(8,128)(2,1)} %refs_3_.3), custom_call_target="tpu_custom_call" | custom-call | flops 1024 | bytes 1024 | tf_op jit(solution)/shard_map/pallas_call | solution.py:82
  7.1 2.1 %collective-permute-start = (bf16[256,512]{1,0:T(8,128)(2,1)}, bf16[256,512]{1,0:T(8,128)(2,1)S(1)}, u32[]{:S(2)}, u32[]{:S(2)}) collective-permute-start(bf16[256,512]{1,0:T(8,128)(2,1)} %get-tuple-element.33.refs_3_), channel_id=1, source_target_pairs={{0,128},{128,0},{1,129},{129,1},{2,130},{130,2},{3,131},{131,3},{4... | collective-permute-start | bytes 786440 | tf_op jit(solution)/shard_map/ppermute | solution.py:42
  9.2 6.4 %all-to-all-start = ((bf16[8,32,512]{2,1,0:T(8,128)(2,1)}), bf16[8,32,512]{2,1,0:T(8,128)(2,1)S(1)}, u32[]{:S(2)}, u32[]{:S(2)}) async-start(bf16[8,32,512]{2,1,0:T(8,128)(2,1)} %bitcast.13), calls=%async_computation | async-start | bytes 524288 | tf_op jit(solution)/shard_map/all_to_all | solution.py:46
  15.6 0.7 pad_add_fusion.refs_0_
  16.2 4.5 %shard_map.77 = (bf16[512,1024]{1,0:T(8,128)(2,1)}, bf16[512,1024]{1,0:T(8,128)(2,1)}) custom-call(s32[4]{0:T(128)} %pad_add_fusion.refs_0_, bf16[256,3200]{1,0:T(8,128)(2,1)} %refs_1_.6), custom_call_target="tpu_custom_call" | custom-call | flops 1024 | bytes 1024 | tf_op jit(solution)/shard_map/pallas_call | solution.py:82
  20.7 2.5 %all-to-all-done.refs_0_ = bf16[8,32,512]{2,1,0:T(8,128)(2,1)S(1)} async-done(((bf16[8,32,512]{2,1,0:T(8,128)(2,1)}), bf16[8,32,512]{2,1,0:T(8,128)(2,1)S(1)}, u32[]{:S(2)}, u32[]{:S(2)}) %all-to-all-start) | async-done | bytes 262176 | tf_op jit(solution)/shard_map/all_to_all | solution.py:46
  23.2 0.0 collective-permute-done.refs_2_.refs_5_
  23.2 0.7 copy-done.13
  23.9 0.1 copy-done.1
  24.0 1.8 %shard_map.78 = (f32[32,512]{1,0:T(8,128)}, f32[32,128]{1,0:T(8,128)}, bf16[8,32,512]{2,1,0:T(8,128)(2,1)}) custom-call(bf16[8,32,512]{2,1,0:T(8,128)(2,1)} %copy-done.13, bf16[512,1024]{1,0:T(8,128)(2,1)} %get-tuple-element.32.refs_1_.refs_6_, bf16[256,512]{1,0:T(8,128)(2,1)} %copy-done.1), custom_call_target="tpu_custom_call" | custom-call | flops 1024 | bytes 1024 | tf_op jit(solution)/shard_map/pallas_call | solution.py:82
  25.9 0.1 collective-permute-start.7
  26.0 8.3 %all-to-all-start.1 = ((bf16[8,32,512]{2,1,0:T(8,128)(2,1)}), bf16[8,32,512]{2,1,0:T(8,128)(2,1)S(1)}, u32[]{:S(2)}, u32[]{:S(2)}) async-start(bf16[8,32,512]{2,1,0:T(8,128)(2,1)} %get-tuple-element.38), calls=%async_computation.1 | async-start | bytes 524288 | tf_op jit(solution)/shard_map/all_to_all | solution.py:46
  34.3 2.9 %collective-permute-start.4 = (bf16[256,512]{1,0:T(8,128)(2,1)S(1)}, bf16[256,512]{1,0:T(8,128)(2,1)S(1)}, u32[]{:S(2)}, u32[]{:S(2)}) collective-permute-start(bf16[256,512]{1,0:T(8,128)(2,1)S(1)} %copy-done), channel_id=1, source_target_pairs={{0,8},{8,0},{1,9},{9,1},{2,10},{10,2},{3,11},{11,3},{4,12},{12,4},... | collective-permute-start | bytes 786440 | tf_op jit(solution)/shard_map/ppermute | solution.py:42
  37.3 0.1 collective-permute-start.5
  38.0 0.4 collective-permute-done.4.refs_4_
  38.4 0.4 collective-permute-done.5.refs_6_
  38.8 4.9 %all-to-all-done.1.refs_2_ = bf16[8,32,512]{2,1,0:T(8,128)(2,1)S(1)} async-done(((bf16[8,32,512]{2,1,0:T(8,128)(2,1)}), bf16[8,32,512]{2,1,0:T(8,128)(2,1)S(1)}, u32[]{:S(2)}, u32[]{:S(2)}) %all-to-all-start.1) | async-done | bytes 262176 | tf_op jit(solution)/shard_map/all_to_all | solution.py:46
  43.7 1.7 %shard_map.80 = f32[32,8,128]{2,1,0:T(8,128)} custom-call(s32[4]{0:T(128)S(1)} %copy-done.6, f32[1]{0:T(128)S(6)} %copy.14.refs_1_, bf16[8,32,512]{2,1,0:T(8,128)(2,1)S(1)} %all-to-all-done.1.refs_2_, bf16[256,512]{1,0:T(8,128)(2,1)S(1)} %copy-done, bf16[256,512]{1,0:T(8,128)(2,1)S(1)} %collective-permute-done.4.refs_4_, bf16[256,512]{1,0:T(8,128)(2,1)S(1)} %copy-done.2, ...), custom_call_target="tpu_custom_call" | custom-call | flops 1024 | bytes 1024 | tf_op jit(solution)/shard_map/pallas_call | solution.py:82
  45.4 8.5 %all-to-all-start.2 = ((f32[32,8,128]{2,1,0:T(8,128)}), f32[32,8,128]{2,1,0:T(8,128)S(1)}, u32[]{:S(2)}, u32[]{:S(2)}) async-start(f32[32,8,128]{2,1,0:T(8,128)} %shard_map.80), calls=%async_computation.2 | async-start | bytes 262144 | tf_op jit(solution)/shard_map/all_to_all | solution.py:46
  53.9 0.3 collective-permute-start.6
  54.2 0.0 collective-permute-done.7.refs_8_
  54.2 0.3 collective-permute-start.8
  54.5 7.1 %all-to-all-done.2.refs_7_ = f32[32,8,128]{2,1,0:T(8,128)S(1)} async-done(((f32[32,8,128]{2,1,0:T(8,128)}), f32[32,8,128]{2,1,0:T(8,128)S(1)}, u32[]{:S(2)}, u32[]{:S(2)}) %all-to-all-start.2) | async-done | bytes 131104 | tf_op jit(solution)/shard_map/all_to_all | solution.py:46
  61.6 2.8 %shard_map.81 = (bf16[8,32,1152]{2,1,0:T(8,128)(2,1)}, f32[8,128]{1,0:T(8,128)S(1)}) custom-call(s32[4]{0:T(128)S(1)} %copy-done.6, f32[1]{0:T(128)S(6)} %copy.14.refs_1_, bf16[8,32,512]{2,1,0:T(8,128)(2,1)S(1)} %all-to-all-done.1.refs_2_, bf16[256,512]{1,0:T(8,128)(2,1)S(1)} %copy-done, bf16[256,512]{1,0:T(8,128)(2,1)S(1)} %collective-permute-done.4.refs_4_, ...), custom_call_target="tpu_custom_call" | custom-call | flops 1024 | bytes 1024 | tf_op jit(solution)/shard_map/pallas_call | solution.py:82
  64.4 0.6 copy-done.7
  65.0 3.5 %all-to-all-start.3 = ((bf16[8,32,1152]{2,1,0:T(8,128)(2,1)}), bf16[8,32,1152]{2,1,0:T(8,128)(2,1)S(1)}, u32[]{:S(2)}, u32[]{:S(2)}) async-start(bf16[8,32,1152]{2,1,0:T(8,128)(2,1)} %get-tuple-element.39), calls=%async_computation.3 | async-start | bytes 1179648 | tf_op jit(solution)/shard_map/all_to_all | solution.py:46
  68.5 0.4 collective-permute-start.2
  68.9 0.5 collective-permute-start.1
  69.4 10.2 %collective-permute-done.2.refs_2_ = bf16[800,256]{1,0:T(8,128)(2,1)S(1)} collective-permute-done((bf16[800,256]{1,0:T(8,128)(2,1)}, bf16[800,256]{1,0:T(8,128)(2,1)S(1)}, u32[]{:S(2)}, u32[]{:S(2)}) %collective-permute-start.2) | collective-permute-done | bytes 409632 | tf_op jit(solution)/shard_map/ppermute | solution.py:42
  79.6 1.1 collective-permute-start.3
  80.7 0.0 collective-permute-done.1.refs_9_.refs_1_
  80.7 0.0 collective-permute-done.6.refs_7_
  80.7 1.5 collective-permute-done.3.refs_10_.refs_3_
  82.2 5.7 %all-to-all-done.3.refs_2_ = bf16[8,32,1152]{2,1,0:T(8,128)(2,1)S(1)} async-done(((bf16[8,32,1152]{2,1,0:T(8,128)(2,1)}), bf16[8,32,1152]{2,1,0:T(8,128)(2,1)S(1)}, u32[]{:S(2)}, u32[]{:S(2)}) %all-to-all-start.3) | async-done | bytes 589856 | tf_op jit(solution)/shard_map/all_to_all | solution.py:46
  87.8 0.0 collective-permute-done.8.refs_8_.refs_9_
  87.9 0.8 copy-done.11
  88.7 3.1 %shard_map.82.refs_4_ = bf16[16,32,640]{2,1,0:T(8,128)(2,1)} custom-call(s32[4]{0:T(128)} %pad_add_fusion.refs_0_, f32[1]{0:T(128)S(6)} %copy.14.refs_1_, bf16[8,32,1152]{2,1,0:T(8,128)(2,1)} %copy-done.11, f32[32,512]{1,0:T(8,128)} %get-tuple-element.40.refs_3_, f32[32,128]{1,0:T(8,128)} %get-tuple-element.34.refs_0_.refs_4_, bf16[8,32,512]{2,1,0:T(8,128)(2,1)} %bitcast.10, ...), custom_call_target="tpu_custom_call" | custom-call | flops 1024 | bytes 1024 | tf_op jit(solution)/shard_map/pallas_call | solution.py:82
  91.8 3.8 %all-to-all-start.4 = ((bf16[16,32,640]{2,1,0:T(8,128)(2,1)}), bf16[16,32,640]{2,1,0:T(8,128)(2,1)S(1)}, u32[]{:S(2)}, u32[]{:S(2)}) async-start(bf16[16,32,640]{2,1,0:T(8,128)(2,1)} %shard_map.82.refs_4_), calls=%async_computation.4 | async-start | bytes 1310720 | tf_op jit(solution)/shard_map/all_to_all | solution.py:46
  95.5 5.3 %shard_map.83 = (bf16[800,1024]{1,0:T(8,128)(2,1)}, bf16[800,1024]{1,0:T(8,128)(2,1)}) custom-call(bf16[800,256]{1,0:T(8,128)(2,1)} %get-tuple-element.37.refs_0_, bf16[800,256]{1,0:T(8,128)(2,1)} %copy-done.12, bf16[800,256]{1,0:T(8,128)(2,1)} %copy-done.15, bf16[800,256]{1,0:T(8,128)(2,1)} %collective-permute-done.3.refs_10_.refs_3_, ...), custom_call_target="tpu_custom_call" | custom-call | flops 1024 | bytes 1024 | tf_op jit(solution)/shard_map/pallas_call | solution.py:82
  100.8 5.6 %all-to-all-done.4 = bf16[16,32,640]{2,1,0:T(8,128)(2,1)S(1)} async-done(((bf16[16,32,640]{2,1,0:T(8,128)(2,1)}), bf16[16,32,640]{2,1,0:T(8,128)(2,1)S(1)}, u32[]{:S(2)}, u32[]{:S(2)}) %all-to-all-start.4) | async-done | bytes 655392 | tf_op jit(solution)/shard_map/all_to_all | solution.py:46
  106.4 0.9 copy-done.8
  107.3 2.1 %collective-permute-start.9 = (bf16[2,256,640]{2,1,0:T(8,128)(2,1)}, bf16[2,256,640]{2,1,0:T(8,128)(2,1)S(1)}, u32[]{:S(2)}, u32[]{:S(2)}) collective-permute-start(bf16[2,256,640]{2,1,0:T(8,128)(2,1)} %shard_map.84.refs_1_), channel_id=1, source_target_pairs={{0,8},{8,0},{1,9},{9,1},{2,10},{10,2},{3,11},{11,3},{4,12},{12,4},... | collective-permute-start | bytes 1966088 | tf_op jit(solution)/shard_map/ppermute | solution.py:42
  109.4 1.9 %collective-permute-done.9.refs_2_ = bf16[2,256,640]{2,1,0:T(8,128)(2,1)S(1)} collective-permute-done((bf16[2,256,640]{2,1,0:T(8,128)(2,1)}, bf16[2,256,640]{2,1,0:T(8,128)(2,1)S(1)}, u32[]{:S(2)}, u32[]{:S(2)}) %collective-permute-start.9) | collective-permute-done | bytes 655392 | tf_op jit(solution)/shard_map/ppermute | solution.py:42
  111.4 0.9 copy-done.14
  112.3 8.4 %shard_map.85 = (bf16[800,128]{1,0:T(8,128)(2,1)}, bf16[800,128]{1,0:T(8,128)(2,1)}, bf16[800,128]{1,0:T(8,128)(2,1)}, bf16[800,128]{1,0:T(8,128)(2,1)}, bf16[40...) custom-call(s32[4]{0:T(128)} %pad_add_fusion.refs_0_, ...), custom_call_target="tpu_custom_call" | custom-call | flops 1024 | bytes 1024 | tf_op jit(solution)/shard_map/pallas_call | solution.py:82
  120.7 0.1 collective-permute-start.14
  120.8 0.1 collective-permute-start.10
  120.8 2.7 %collective-permute-start.11 = (bf16[400,128]{1,0:T(8,128)(2,1)}, bf16[400,128]{1,0:T(8,128)(2,1)S(1)}, u32[]{:S(2)}, u32[]{:S(2)}) collective-permute-start(bf16[400,128]{1,0:T(8,128)(2,1)} %get-tuple-element.49), channel_id=1, source_target_pairs={{0,112},{16,0},{32,16},{48,32},{64,48},{80,64},{96,80},{112,96},{1... | collective-permute-start | bytes 307208 | tf_op jit(solution)/shard_map/ppermute | solution.py:346
  123.5 2.3 %collective-permute-start.15 = (bf16[800,128]{1,0:T(8,128)(2,1)}, bf16[800,128]{1,0:T(8,128)(2,1)S(1)}, u32[]{:S(2)}, u32[]{:S(2)}) collective-permute-start(bf16[800,128]{1,0:T(8,128)(2,1)} %get-tuple-element.53), channel_id=1, source_target_pairs={{0,96},{16,112},{32,0},{48,16},{64,32},{80,48},{96,64},{112,80},{1... | collective-permute-start | bytes 614408 | tf_op jit(solution)/shard_map/ppermute | solution.py:346
  125.8 0.0 collective-permute-start.16
  125.8 8.6 %collective-permute-done.10.refs_2_ = bf16[400,128]{1,0:T(8,128)(2,1)S(1)} collective-permute-done((bf16[400,128]{1,0:T(8,128)(2,1)}, bf16[400,128]{1,0:T(8,128)(2,1)S(1)}, u32[]{:S(2)}, u32[]{:S(2)}) %collective-permute-start.10) | collective-permute-done | bytes 102432 | tf_op jit(solution)/shard_map/ppermute | solution.py:346
  134.4 0.0 collective-permute-start.17
  134.4 0.0 collective-permute-done.11.refs_3_
  134.4 0.9 copy-done.3
  135.3 0.9 copy-done.4
  136.3 0.1 shard_map.86
  136.3 0.5 collective-permute-start.12
  136.8 0.0 collective-permute-done.14.refs_3_
  136.8 4.1 %collective-permute-start.13 = (bf16[800,128]{1,0:T(8,128)(2,1)S(1)}, bf16[800,128]{1,0:T(8,128)(2,1)S(1)}, u32[]{:S(2)}, u32[]{:S(2)}) collective-permute-start(bf16[800,128]{1,0:T(8,128)(2,1)S(1)} %get-tuple-element.51), channel_id=1, source_target_pairs={{0,80},{16,96},{32,112},{48,0},{64,16},{80,32},{96,48},{112,64},{1... | collective-permute-start | bytes 614408 | tf_op jit(solution)/shard_map/ppermute | solution.py:346
  140.9 0.0 collective-permute-done.15.refs_4_
  140.9 0.0 collective-permute-done.16.refs_5_
  140.9 12.4 %collective-permute-done.12.refs_1_ = bf16[800,128]{1,0:T(8,128)(2,1)S(1)} collective-permute-done((bf16[800,128]{1,0:T(8,128)(2,1)S(1)}, bf16[800,128]{1,0:T(8,128)(2,1)S(1)}, u32[]{:S(2)}, u32[]{:S(2)}) %collective-permute-start.12) | collective-permute-done | bytes 204832 | tf_op jit(solution)/shard_map/ppermute | solution.py:346
  153.3 0.9 copy-done.5
  154.3 1.0 shard_map.87
  (27 shorter events, 0.1 us)
Async XLA Ops:
  7.1 16.1 %collective-permute-start = (bf16[256,512]{1,0:T(8,128)(2,1)}, bf16[256,512]{1,0:T(8,128)(2,1)S(1)}, u32[]{:S(2)}, u32[]{:S(2)}) collective-permute-start(bf16[256,512]{1,0:T(8,128)(2,1)} %get-tuple-element.33.refs_3_), channel_id=1, source_target_pairs={{0,128},{128,0},{1,129},{129,1},{2,130},{130,2},{3,131},{131,3},{4... | collective-permute-start | bytes 786440 | tf_op jit(solution)/shard_map/ppermute | solution.py:42
  9.2 14.0 %all-to-all-start = ((bf16[8,32,512]{2,1,0:T(8,128)(2,1)}), bf16[8,32,512]{2,1,0:T(8,128)(2,1)S(1)}, u32[]{:S(2)}, u32[]{:S(2)}) async-start(bf16[8,32,512]{2,1,0:T(8,128)(2,1)} %bitcast.13), calls=%async_computation | async-start | bytes 524288 | tf_op jit(solution)/shard_map/all_to_all | solution.py:46
  23.2 0.7 copy-start.13
  23.2 0.8 copy-start.1
  24.0 10.3 %copy-start = (bf16[256,512]{1,0:T(8,128)(2,1)S(1)}, bf16[256,512]{1,0:T(8,128)(2,1)}, u32[]{:S(2)}) copy-start(bf16[256,512]{1,0:T(8,128)(2,1)} %get-tuple-element.33.refs_3_) | copy-start | bytes 786436
  24.0 19.7 %copy-start.6 = (s32[4]{0:T(128)S(1)}, s32[4]{0:T(128)}, u32[]{:S(2)}) copy-start(s32[4]{0:T(128)} %pad_add_fusion.refs_0_) | copy-start | bytes 52
  25.8 11.4 %copy-start.2 = (bf16[256,512]{1,0:T(8,128)(2,1)S(1)}, bf16[256,512]{1,0:T(8,128)(2,1)}, u32[]{:S(2)}) copy-start(bf16[256,512]{1,0:T(8,128)(2,1)} %copy-done.1) | copy-start | bytes 786436
  25.9 28.0 %copy-start.9 = (bf16[512,1024]{1,0:T(8,128)(2,1)S(1)}, bf16[512,1024]{1,0:T(8,128)(2,1)}, u32[]{:S(2)}) copy-start(bf16[512,1024]{1,0:T(8,128)(2,1)} %get-tuple-element.32.refs_1_.refs_6_) | copy-start | bytes 3145732
  25.9 28.3 %collective-permute-start.7 = (bf16[512,1024]{1,0:T(8,128)(2,1)}, bf16[512,1024]{1,0:T(8,128)(2,1)}, u32[]{:S(2)}, u32[]{:S(2)}) collective-permute-start(bf16[512,1024]{1,0:T(8,128)(2,1)} %get-tuple-element.42), channel_id=1, source_target_pairs={{0,128},{128,0},{1,129},{129,1},{2,130},{130,2},{3,131},{131,3},{4... | collective-permute-start | bytes 3145736 | tf_op jit(solution)/shard_map/ppermute | solution.py:42
  26.0 17.7 %all-to-all-start.1 = ((bf16[8,32,512]{2,1,0:T(8,128)(2,1)}), bf16[8,32,512]{2,1,0:T(8,128)(2,1)S(1)}, u32[]{:S(2)}, u32[]{:S(2)}) async-start(bf16[8,32,512]{2,1,0:T(8,128)(2,1)} %get-tuple-element.38), calls=%async_computation.1 | async-start | bytes 524288 | tf_op jit(solution)/shard_map/all_to_all | solution.py:46
  34.3 4.1 %collective-permute-start.4 = (bf16[256,512]{1,0:T(8,128)(2,1)S(1)}, bf16[256,512]{1,0:T(8,128)(2,1)S(1)}, u32[]{:S(2)}, u32[]{:S(2)}) collective-permute-start(bf16[256,512]{1,0:T(8,128)(2,1)S(1)} %copy-done), channel_id=1, source_target_pairs={{0,8},{8,0},{1,9},{9,1},{2,10},{10,2},{3,11},{11,3},{4,12},{12,4},... | collective-permute-start | bytes 786440 | tf_op jit(solution)/shard_map/ppermute | solution.py:42
  37.3 1.5 collective-permute-start.5
  45.4 16.2 %all-to-all-start.2 = ((f32[32,8,128]{2,1,0:T(8,128)}), f32[32,8,128]{2,1,0:T(8,128)S(1)}, u32[]{:S(2)}, u32[]{:S(2)}) async-start(f32[32,8,128]{2,1,0:T(8,128)} %shard_map.80), calls=%async_computation.2 | async-start | bytes 262144 | tf_op jit(solution)/shard_map/all_to_all | solution.py:46
  53.9 26.8 %collective-permute-start.6 = (bf16[512,1024]{1,0:T(8,128)(2,1)S(1)}, bf16[512,1024]{1,0:T(8,128)(2,1)S(1)}, u32[]{:S(2)}, u32[]{:S(2)}) collective-permute-start(bf16[512,1024]{1,0:T(8,128)(2,1)S(1)} %copy-done.9), channel_id=1, source_target_pairs={{0,8},{8,0},{1,9},{9,1},{2,10},{10,2},{3,11},{11,3},{4,12},{12,4},... | collective-permute-start | bytes 3145736 | tf_op jit(solution)/shard_map/ppermute | solution.py:42
  54.2 33.6 %collective-permute-start.8 = (bf16[512,1024]{1,0:T(8,128)(2,1)}, bf16[512,1024]{1,0:T(8,128)(2,1)}, u32[]{:S(2)}, u32[]{:S(2)}) collective-permute-start(bf16[512,1024]{1,0:T(8,128)(2,1)} %collective-permute-done.7.refs_8_), channel_id=1, source_target_pairs={{0,8},{8,0},{1,9},{9,1},{2,10},{10,2},{3,11},{11,3},{4,12},{12,4},... | collective-permute-start | bytes 3145736 | tf_op jit(solution)/shard_map/ppermute | solution.py:42
  64.4 0.6 copy-start.7
  65.0 22.9 %all-to-all-start.3 = ((bf16[8,32,1152]{2,1,0:T(8,128)(2,1)}), bf16[8,32,1152]{2,1,0:T(8,128)(2,1)S(1)}, u32[]{:S(2)}, u32[]{:S(2)}) async-start(bf16[8,32,1152]{2,1,0:T(8,128)(2,1)} %get-tuple-element.39), calls=%async_computation.3 | async-start | bytes 1179648 | tf_op jit(solution)/shard_map/all_to_all | solution.py:46
  68.5 11.1 %collective-permute-start.2 = (bf16[800,256]{1,0:T(8,128)(2,1)}, bf16[800,256]{1,0:T(8,128)(2,1)S(1)}, u32[]{:S(2)}, u32[]{:S(2)}) collective-permute-start(bf16[800,256]{1,0:T(8,128)(2,1)} %get-tuple-element.37.refs_0_), channel_id=1, source_target_pairs={{0,128},{128,0},{1,129},{129,1},{2,130},{130,2},{3,131},{131,3},{4... | collective-permute-start | bytes 1228808 | tf_op jit(solution)/shard_map/ppermute | solution.py:42
  68.9 11.8 %collective-permute-start.1 = (bf16[800,256]{1,0:T(8,128)(2,1)}, bf16[800,256]{1,0:T(8,128)(2,1)S(1)}, u32[]{:S(2)}, u32[]{:S(2)}) collective-permute-start(bf16[800,256]{1,0:T(8,128)(2,1)} %get-tuple-element.37.refs_0_), channel_id=1, source_target_pairs={{0,8},{8,0},{1,9},{9,1},{2,10},{10,2},{3,11},{11,3},{4,12},{12,4},... | collective-permute-start | bytes 1228808 | tf_op jit(solution)/shard_map/ppermute | solution.py:42
  79.6 1.1 copy-start.15
  79.6 2.6 %collective-permute-start.3 = (bf16[800,256]{1,0:T(8,128)(2,1)S(1)}, bf16[800,256]{1,0:T(8,128)(2,1)}, u32[]{:S(2)}, u32[]{:S(2)}) collective-permute-start(bf16[800,256]{1,0:T(8,128)(2,1)S(1)} %collective-permute-done.2.refs_2_), channel_id=1, source_target_pairs={{0,8},{8,0},{1,9},{9,1},{2,10},{10,2},{3,11},{11,3},{4,12},{12,4},... | collective-permute-start | bytes 1228808 | tf_op jit(solution)/shard_map/ppermute | solution.py:42
  80.7 7.2 %copy-start.12 = (bf16[800,256]{1,0:T(8,128)(2,1)}, bf16[800,256]{1,0:T(8,128)(2,1)S(1)}, u32[]{:S(2)}) copy-start(bf16[800,256]{1,0:T(8,128)(2,1)S(1)} %collective-permute-done.1.refs_9_.refs_1_) | copy-start | bytes 1228804
  80.7 7.2 %copy-start.10 = (bf16[512,1024]{1,0:T(8,128)(2,1)}, bf16[512,1024]{1,0:T(8,128)(2,1)S(1)}, u32[]{:S(2)}) copy-start(bf16[512,1024]{1,0:T(8,128)(2,1)S(1)} %collective-permute-done.6.refs_7_) | copy-start | bytes 3145732
  87.8 0.8 copy-start.11
  91.8 14.7 %all-to-all-start.4 = ((bf16[16,32,640]{2,1,0:T(8,128)(2,1)}), bf16[16,32,640]{2,1,0:T(8,128)(2,1)S(1)}, u32[]{:S(2)}, u32[]{:S(2)}) async-start(bf16[16,32,640]{2,1,0:T(8,128)(2,1)} %shard_map.82.refs_4_), calls=%async_computation.4 | async-start | bytes 1310720 | tf_op jit(solution)/shard_map/all_to_all | solution.py:46
  106.4 0.9 copy-start.8
  107.3 4.0 %collective-permute-start.9 = (bf16[2,256,640]{2,1,0:T(8,128)(2,1)}, bf16[2,256,640]{2,1,0:T(8,128)(2,1)S(1)}, u32[]{:S(2)}, u32[]{:S(2)}) collective-permute-start(bf16[2,256,640]{2,1,0:T(8,128)(2,1)} %shard_map.84.refs_1_), channel_id=1, source_target_pairs={{0,8},{8,0},{1,9},{9,1},{2,10},{10,2},{3,11},{11,3},{4,12},{12,4},... | collective-permute-start | bytes 1966088 | tf_op jit(solution)/shard_map/ppermute | solution.py:42
  111.4 0.9 copy-start.14
  120.7 16.1 %collective-permute-start.14 = (bf16[800,128]{1,0:T(8,128)(2,1)}, bf16[800,128]{1,0:T(8,128)(2,1)S(1)}, u32[]{:S(2)}, u32[]{:S(2)}) collective-permute-start(bf16[800,128]{1,0:T(8,128)(2,1)} %get-tuple-element.52), channel_id=1, source_target_pairs={{0,32},{16,48},{32,64},{48,80},{64,96},{80,112},{96,0},{112,16},{1... | collective-permute-start | bytes 614408 | tf_op jit(solution)/shard_map/ppermute | solution.py:346
  120.8 13.6 %collective-permute-start.10 = (bf16[400,128]{1,0:T(8,128)(2,1)}, bf16[400,128]{1,0:T(8,128)(2,1)S(1)}, u32[]{:S(2)}, u32[]{:S(2)}) collective-permute-start(bf16[400,128]{1,0:T(8,128)(2,1)} %get-tuple-element.48), channel_id=1, source_target_pairs={{0,16},{16,32},{32,48},{48,64},{64,80},{80,96},{96,112},{112,0},{1... | collective-permute-start | bytes 307208 | tf_op jit(solution)/shard_map/ppermute | solution.py:346
  120.8 13.6 %collective-permute-start.11 = (bf16[400,128]{1,0:T(8,128)(2,1)}, bf16[400,128]{1,0:T(8,128)(2,1)S(1)}, u32[]{:S(2)}, u32[]{:S(2)}) collective-permute-start(bf16[400,128]{1,0:T(8,128)(2,1)} %get-tuple-element.49), channel_id=1, source_target_pairs={{0,112},{16,0},{32,16},{48,32},{64,48},{80,64},{96,80},{112,96},{1... | collective-permute-start | bytes 307208 | tf_op jit(solution)/shard_map/ppermute | solution.py:346
  123.5 17.4 %collective-permute-start.15 = (bf16[800,128]{1,0:T(8,128)(2,1)}, bf16[800,128]{1,0:T(8,128)(2,1)S(1)}, u32[]{:S(2)}, u32[]{:S(2)}) collective-permute-start(bf16[800,128]{1,0:T(8,128)(2,1)} %get-tuple-element.53), channel_id=1, source_target_pairs={{0,96},{16,112},{32,0},{48,16},{64,32},{80,48},{96,64},{112,80},{1... | collective-permute-start | bytes 614408 | tf_op jit(solution)/shard_map/ppermute | solution.py:346
  125.8 15.1 %collective-permute-start.16 = (bf16[800,128]{1,0:T(8,128)(2,1)}, bf16[800,128]{1,0:T(8,128)(2,1)S(1)}, u32[]{:S(2)}, u32[]{:S(2)}) collective-permute-start(bf16[800,128]{1,0:T(8,128)(2,1)} %get-tuple-element.54), channel_id=1, source_target_pairs={{0,16},{16,32},{32,48},{48,64},{64,80},{80,96},{96,112},{112,0},{1... | collective-permute-start | bytes 614408 | tf_op jit(solution)/shard_map/ppermute | solution.py:346
  134.4 6.5 %collective-permute-start.17 = (bf16[800,128]{1,0:T(8,128)(2,1)}, bf16[800,128]{1,0:T(8,128)(2,1)S(1)}, u32[]{:S(2)}, u32[]{:S(2)}) collective-permute-start(bf16[800,128]{1,0:T(8,128)(2,1)} %get-tuple-element.55), channel_id=1, source_target_pairs={{0,112},{16,0},{32,16},{48,32},{64,48},{80,64},{96,80},{112,96},{1... | collective-permute-start | bytes 614408 | tf_op jit(solution)/shard_map/ppermute | solution.py:346
  134.4 0.9 copy-start.3
  135.3 0.9 copy-start.4
  136.3 17.0 %collective-permute-start.12 = (bf16[800,128]{1,0:T(8,128)(2,1)S(1)}, bf16[800,128]{1,0:T(8,128)(2,1)S(1)}, u32[]{:S(2)}, u32[]{:S(2)}) collective-permute-start(bf16[800,128]{1,0:T(8,128)(2,1)S(1)} %get-tuple-element.50), channel_id=1, source_target_pairs={{0,48},{16,64},{32,80},{48,96},{64,112},{80,0},{96,16},{112,32},{1... | collective-permute-start | bytes 614408 | tf_op jit(solution)/shard_map/ppermute | solution.py:346
  136.8 16.5 %collective-permute-start.13 = (bf16[800,128]{1,0:T(8,128)(2,1)S(1)}, bf16[800,128]{1,0:T(8,128)(2,1)S(1)}, u32[]{:S(2)}, u32[]{:S(2)}) collective-permute-start(bf16[800,128]{1,0:T(8,128)(2,1)S(1)} %get-tuple-element.51), channel_id=1, source_target_pairs={{0,80},{16,96},{32,112},{48,0},{64,16},{80,32},{96,48},{112,64},{1... | collective-permute-start | bytes 614408 | tf_op jit(solution)/shard_map/ppermute | solution.py:346
  153.3 0.9 copy-start.5

commit v7 on v6

--- a/solution.py
+++ b/solution.py
@@ -19,6 +19,7 @@
 LANES = 128
 OUT_COLS = 16
 FAR = 4
+EXTRA = 16
 MIB = 1 << 20
 LIM = (60, 60, 60, 8, 8, 60, 60, 60, 16, 16)
 NT = (((1,), (1,)), ((), ()))
@@ -215,21 +216,34 @@
         inv = jnp.concatenate([inv_ref[pl.ds(place + half, 1), :] for half in range(2)], axis=1)
         first += jnp.dot(expo.astype(BF), text, preferred_element_type=F32)
         second += jnp.dot((expo * inv).astype(BF), text, preferred_element_type=F32)
-    packed_ref[:, :, :emb] = first.astype(BF).reshape(count, own_rows, emb)
-    packed_ref[:, :, emb : 2 * emb] = second.astype(BF).reshape(count, own_rows, emb)
+    tiles = emb // LANES
+    for i, side in enumerate((first, second)):
+        for tile in range(tiles):
+            begin = (i * tiles + tile) * own_rows
+            part = side[:, tile * LANES : (tile + 1) * LANES]
+            packed_ref[:, begin : begin + own_rows, :] = part.astype(BF).reshape(count, own_rows, LANES)
     row_hi = row_part.astype(BF).astype(F32)
-    lane = lax.broadcasted_iota(jnp.int32, (rows, LANES), 1)
-    both = jnp.where(lane < LANES // 2, row_hi, row_part - row_hi)
-    packed_ref[:, :, 2 * emb :] = both.astype(BF).reshape(count, own_rows, LANES)
+    row_lo = (row_part - row_hi).reshape(count, own_rows, 1)
+    row_hi = row_hi.reshape(count, own_rows, 1)
+    row = lax.broadcasted_iota(jnp.int32, (count, own_rows, LANES), 1)
+    lane = lax.broadcasted_iota(jnp.int32, (count, own_rows, LANES), 2)
+    turned = jnp.where(lane == row, row_hi, jnp.where(lane == row + own_rows, row_lo, 0.0))
+    turned = jnp.sum(turned, axis=1, keepdims=True)
+    packed_ref[:, 2 * tiles * own_rows :, :] = jnp.broadcast_to(turned, (count, EXTRA, LANES)).astype(BF)
 
 
 def proj_kernel(where_ref, scale_ref, back_ref, unit_ref, inv_ref, text_ref, log_ref, out_ref, *, sharers):
     scale_val = scale_ref[0]
     own_rows, emb = unit_ref.shape
     back = jnp.sum(back_ref[...].astype(F32), axis=0)
-    half = 2 * emb + LANES // 2
-    row_sum = back[:, 2 * emb : 2 * emb + 1] + back[:, half : half + 1]
-    weighted = back[:, :emb] / row_sum + back[:, emb : 2 * emb]
+    tiles = emb // LANES
+    parts = [back[i * own_rows : (i + 1) * own_rows] for i in range(2 * tiles)]
+    lane = lax.broadcasted_iota(jnp.int32, (own_rows, LANES), 1)
+    row = lax.broadcasted_iota(jnp.int32, (own_rows, LANES), 0)
+    sums = back[2 * tiles * own_rows : 2 * tiles * own_rows + 1]
+    sums = jnp.where((lane == row) | (lane == row + own_rows), sums, 0.0)
+    row_sum = jnp.sum(sums, axis=1, keepdims=True)
+    weighted = jnp.concatenate(parts[:tiles], axis=1) / row_sum + jnp.concatenate(parts[tiles:], axis=1)
     text = text_ref[where_ref[2]].astype(F32)
     unit = unit_ref[...]
     positive = scale_val * jnp.sum(unit.astype(BF).astype(F32) * text, axis=-1, keepdims=True)
@@ -240,11 +254,11 @@
     grad_proj = inv_ref[:, :1] * (
         grad_emb - unit * jnp.sum(unit * grad_emb, axis=-1, keepdims=True)
     )
-    lane = lax.broadcasted_iota(jnp.int32, (own_rows, LANES), 1)
-    row = lax.broadcasted_iota(jnp.int32, (own_rows, LANES), 0)
+    lane, row = lane[:EXTRA], row[:EXTRA]
     loss = jnp.where(lane == 0, a, jnp.where(lane == 1, b, jnp.where(lane == 2, c, 0.0)))
     loss = jnp.where(row == 0, loss, 0.0)
-    sent = jnp.concatenate([grad_proj, loss], axis=1).astype(BF)
+    sent = [grad_proj[:, i * LANES : (i + 1) * LANES] for i in range(tiles)]
+    sent = jnp.concatenate(sent + [loss], axis=0).astype(BF)
     out_ref[...] = jnp.broadcast_to(sent[None], out_ref.shape)
 
 
@@ -261,17 +275,24 @@
 
 def grads_kernel(where_ref, own_hbm, other_hbm, wout_hbm, hidden_hbm, der_hbm, *refs):
     feats_hbm, out_refs, refs = refs[:4], refs[4:13], refs[13:]
-    grads_ref, wout_ref, der_ref, hidden_ref, feats_ref, sems = refs
+    grads_ref, loss_ref, wout_ref, der_ref, hidden_ref, feats_ref, sems = refs
     x_index, c_index = where_ref[0], where_ref[1]
-    rows = own_hbm.shape[1]
+    _, mp_count, own_rows, _ = grads_ref.shape
+    rows = mp_count * own_rows
     hid, emb = wout_ref.shape
+    tiles = emb // LANES
     z_count = feats_ref.shape[1] // LANES
     spans = parts_of(hid, 2)
     copies = []
     for block in range(4):
         rx, rc = block // 2, block % 2
         source = other_hbm if rc else own_hbm
-        copies.append((source.at[rx ^ x_index], grads_ref.at[block]))
+        source = source.at[rx ^ x_index]
+        for tile in range(tiles):
+            place = grads_ref.at[block, :, :, pl.ds(tile * LANES, LANES)]
+            copies.append((source.at[:, pl.ds(tile * own_rows, own_rows), :], place))
+        copies.append((source.at[:, pl.ds(tiles * own_rows, EXTRA), :], loss_ref.at[block]))
+    ready = len(copies) + 1
     copies.append((wout_hbm, wout_ref))
     copies.append((der_hbm.at[spans[0]], der_ref.at[spans[0]]))
     for block in range(4):
@@ -288,25 +309,26 @@
     column = lax.rem(where_ref[3] + target // OUT_COLS, z_count) * 2 + c_index
     column = x_index * (emb // 2) + column * OUT_COLS + target % OUT_COLS
     pick = jnp.where(source == column, 1.0, 0.0).astype(BF)
-    for copy in copies[:5]:
+    for copy in copies[:ready]:
         copy.wait()
-    grads = grads_ref[:, :, :emb].reshape(4 * rows, emb)
+    grads = grads_ref[...].reshape(4 * rows, emb)
     picked = jnp.dot(grads, pick, preferred_element_type=F32).astype(BF)
     loss = jnp.zeros((1, LANES), F32)
     for block in range(4):
-        loss += jnp.sum(grads_ref[block, :, emb:].astype(F32), axis=0, keepdims=True)
+        part = loss_ref[block].reshape(mp_count * EXTRA, LANES).astype(F32)
+        loss += jnp.sum(part, axis=0, keepdims=True)
     a, b, c = split3(jnp.sum(loss, axis=1, keepdims=True))
     for i, span in enumerate(spans):
         size = span.stop - span.start
         lane = lax.broadcasted_iota(jnp.int32, (size, LANES), 1)
         grad_hidden = lax.dot_general(wout_ref[span, :], grads, NT, preferred_element_type=F32)
-        copies[(5, 11)[i]].wait()
+        copies[ready + (0, 6)[i]].wait()
         grad_pre = (grad_hidden * der_ref[span, :].astype(F32)).astype(BF)
         if i == 0:
-            for copy in copies[6:10]:
+            for copy in copies[ready + 1 : ready + 5]:
                 copy.wait()
         total = jnp.dot(grad_pre, feats_ref[...], preferred_element_type=F32)
-        copies[(10, 12)[i]].wait()
+        copies[ready + (5, 7)[i]].wait()
         outer = jnp.dot(hidden_ref[span, :], picked, preferred_element_type=F32)
         for z in range(z_count):
             moved = outer if z == 0 else pltpu.roll(outer, LANES - z * OUT_COLS, 1)
@@ -351,6 +373,7 @@
     hid, emb = weight_out.shape
     mp_count = lax.axis_size(MP)
     own_rows = rows // mp_count
+    packs = own_rows * (emb // LANES)
     batch_total = rows * lax.axis_size(DP)
     where = [lax.axis_index(name) for name in ("x_lo", "core", MP, "z")]
     where = jnp.stack(where).astype(jnp.int32)
@@ -389,7 +412,7 @@
     pre_x = swap(pre_own, "x_lo")
     pre = (pre_own, swap(pre_own, "core"), pre_x, swap(pre_x, "core"))
     packed, logs = call(
-        weights_kernel, [((8, own_rows, 2 * emb + LANES), BF), ((8, LANES), F32)], LIM[4],
+        weights_kernel, [((z_count, 2 * packs + EXTRA, LANES), BF), ((8, LANES), F32)], LIM[4],
         where, logit_scale, video_rows, text_emb, *texts, cols, scalars=2, direct=True,
         scratch=[pltpu.VMEM((8, LANES), F32)],
     )
@@ -397,12 +420,12 @@
     back = exchange(packed, "z")
     (sent,) = call(
         functools.partial(proj_kernel, sharers=4 * mp_count),
-        [((2 * mp_count, own_rows, emb + LANES), BF)], LIM[5],
+        [((2 * mp_count, packs + EXTRA, LANES), BF)], LIM[5],
         where, logit_scale, back, unit, inv_norm, text_emb.reshape(mp_count, own_rows, emb), logs,
         scalars=2, after=(feats_q[1], feats_q[3], pre[1], pre[3]),
     )
     gelus = call(gelu_kernel, [((hid, 4 * rows), BF)] * 2, LIM[6], *pre, after=(sent,))
-    grads = exchange(sent, SPREAD).reshape(2, rows, emb + LANES)
+    grads = exchange(sent, SPREAD).reshape(2, mp_count, packs + EXTRA, LANES)
     (grads,) = gate(gelus[0], grads, after=(gelus[1],))
     other = swap(grads, "core")
     first = parts_of(hid, 2)[0].stop
@@ -411,9 +434,10 @@
         grads_kernel, [((size, LANES), BF) for size in sizes], LIM[7],
         where, grads, other, weight_out, *gelus, *feats_q, scalars=1, raw=True,
         scratch=[
-            pltpu.VMEM((4, rows, emb + LANES), BF), pltpu.VMEM((hid, emb), BF),
+            pltpu.VMEM((4, mp_count, own_rows, emb), BF), pltpu.VMEM((4, mp_count, EXTRA, LANES), BF),
+            pltpu.VMEM((hid, emb), BF),
             pltpu.VMEM((hid, 4 * rows), BF), pltpu.VMEM((hid, 4 * rows), BF),
-            pltpu.VMEM((4 * rows, z_count * LANES), BF), pltpu.SemaphoreType.DMA((13,)),
+            pltpu.VMEM((4 * rows, z_count * LANES), BF), pltpu.SemaphoreType.DMA((29,)),
         ],
     )
     near = call(

time: 157 us -> 155 us (0.987)
    unnamed x32 -> x34, local copies, waits for them, and re-layouts: 6.79 us -> 6.71 us
where the time goes in v7:
time: 155 us; the launch traced here: 154 us
  waiting for transfers between devices  59.9 us (39%)
  starting transfers between devices  50.1 us (32%)
  Pallas kernels  35.2 us (23%)
  local copies, waits for them, and re-layouts  6.71 us (4%)
    pallas_call x10, Pallas kernels, call(): pl.pallas_call(body, grid=(1,), out_shape=[jax.ShapeDtypeStruct(s, d) for...  35.2 us
    all_to_all x5, starting transfers between devices, exchange(): return lax.all_to_all(value, axis, 0, 0)  30.5 us
    all_to_all x5, waiting for transfers between devices, exchange(): return lax.all_to_all(value, axis, 0, 0)  24.5 us
    ppermute x8, waiting for transfers between devices, ahead(): return lax.ppermute(value, 'z', [(i, (i + step) % 8) for i in range(8)])  21.2 us
    ppermute x10, waiting for transfers between devices, swap(): return lax.ppermute(value, axis, [(0, 1), (1, 0)])  14.2 us
    ppermute x10, starting transfers between devices, swap(): return lax.ppermute(value, axis, [(0, 1), (1, 0)])  9.93 us
    ppermute x8, starting transfers between devices, ahead(): return lax.ppermute(value, 'z', [(i, (i + step) % 8) for i in range(8)])  9.66 us
    unnamed x34, local copies, waits for them, and re-layouts  6.71 us
  transfers between devices with their start and end apart: 23, of which 12 were waited for; matrix products, arithmetic and copies ran while one was open for 0% of the time, Pallas kernels for 9%

profile of v7, /device:TPU:1, one launch (start us, length us, event | category | flops | bytes accessed | tf_op | source)
XLA Modules:
  0.0 154.1 jit_solution(15518778700158594142)
XLA Ops:
  0.6 6.4 %shard_map.76 = (bf16[256,512]{1,0:T(8,128)(2,1)}, bf16[800,256]{1,0:T(8,128)(2,1)}, bf16[256,512]{1,0:T(8,128)(2,1)}) custom-call(bf16[256,512]{1,0:T(8,128)(2,1)} %refs_0_.1, bf16[256,3200]{1,0:T(8,128)(2,1)} %refs_1_.6, bf16[800,3200]{1,0:T(8,128)(2,1)} %bitcast.12, bf16[800,512]{1,0:T(8,128)(2,1)} %refs_3_.3), custom_call_target="tpu_custom_call" | custom-call | flops 1024 | bytes 1024 | tf_op jit(solution)/shard_map/pallas_call | solution.py:83
  7.1 2.1 %collective-permute-start = (bf16[256,512]{1,0:T(8,128)(2,1)}, bf16[256,512]{1,0:T(8,128)(2,1)S(1)}, u32[]{:S(2)}, u32[]{:S(2)}) collective-permute-start(bf16[256,512]{1,0:T(8,128)(2,1)} %get-tuple-element.33.refs_3_), channel_id=1, source_target_pairs={{0,128},{128,0},{1,129},{129,1},{2,130},{130,2},{3,131},{131,3},{4... | collective-permute-start | bytes 786440 | tf_op jit(solution)/shard_map/ppermute | solution.py:43
  9.2 6.4 %all-to-all-start = ((bf16[8,32,512]{2,1,0:T(8,128)(2,1)}), bf16[8,32,512]{2,1,0:T(8,128)(2,1)S(1)}, u32[]{:S(2)}, u32[]{:S(2)}) async-start(bf16[8,32,512]{2,1,0:T(8,128)(2,1)} %bitcast.13), calls=%async_computation | async-start | bytes 524288 | tf_op jit(solution)/shard_map/all_to_all | solution.py:47
  15.6 0.7 pad_add_fusion.refs_0_
  16.2 4.5 %shard_map.77 = (bf16[512,1024]{1,0:T(8,128)(2,1)}, bf16[512,1024]{1,0:T(8,128)(2,1)}) custom-call(s32[4]{0:T(128)} %pad_add_fusion.refs_0_, bf16[256,3200]{1,0:T(8,128)(2,1)} %refs_1_.6), custom_call_target="tpu_custom_call" | custom-call | flops 1024 | bytes 1024 | tf_op jit(solution)/shard_map/pallas_call | solution.py:83
  20.8 2.4 %all-to-all-done.refs_0_ = bf16[8,32,512]{2,1,0:T(8,128)(2,1)S(1)} async-done(((bf16[8,32,512]{2,1,0:T(8,128)(2,1)}), bf16[8,32,512]{2,1,0:T(8,128)(2,1)S(1)}, u32[]{:S(2)}, u32[]{:S(2)}) %all-to-all-start) | async-done | bytes 262176 | tf_op jit(solution)/shard_map/all_to_all | solution.py:47
  23.2 0.0 collective-permute-done.refs_2_.refs_5_
  23.2 0.7 copy-done.14
  23.9 0.1 copy-done.1
  24.0 1.8 %shard_map.78 = (f32[32,512]{1,0:T(8,128)}, f32[32,128]{1,0:T(8,128)}, bf16[8,32,512]{2,1,0:T(8,128)(2,1)}) custom-call(bf16[8,32,512]{2,1,0:T(8,128)(2,1)} %copy-done.14, bf16[512,1024]{1,0:T(8,128)(2,1)} %get-tuple-element.32.refs_1_.refs_6_, bf16[256,512]{1,0:T(8,128)(2,1)} %copy-done.1), custom_call_target="tpu_custom_call" | custom-call | flops 1024 | bytes 1024 | tf_op jit(solution)/shard_map/pallas_call | solution.py:83
  25.9 0.1 collective-permute-start.7
  26.0 8.3 %all-to-all-start.1 = ((bf16[8,32,512]{2,1,0:T(8,128)(2,1)}), bf16[8,32,512]{2,1,0:T(8,128)(2,1)S(1)}, u32[]{:S(2)}, u32[]{:S(2)}) async-start(bf16[8,32,512]{2,1,0:T(8,128)(2,1)} %get-tuple-element.38), calls=%async_computation.1 | async-start | bytes 524288 | tf_op jit(solution)/shard_map/all_to_all | solution.py:47
  34.3 2.9 %collective-permute-start.4 = (bf16[256,512]{1,0:T(8,128)(2,1)S(1)}, bf16[256,512]{1,0:T(8,128)(2,1)S(1)}, u32[]{:S(2)}, u32[]{:S(2)}) collective-permute-start(bf16[256,512]{1,0:T(8,128)(2,1)S(1)} %copy-done), channel_id=1, source_target_pairs={{0,8},{8,0},{1,9},{9,1},{2,10},{10,2},{3,11},{11,3},{4,12},{12,4},... | collective-permute-start | bytes 786440 | tf_op jit(solution)/shard_map/ppermute | solution.py:43
  37.3 0.1 collective-permute-start.5
  38.0 0.4 collective-permute-done.4.refs_4_
  38.4 0.4 collective-permute-done.5.refs_6_
  38.8 4.9 %all-to-all-done.1.refs_2_ = bf16[8,32,512]{2,1,0:T(8,128)(2,1)S(1)} async-done(((bf16[8,32,512]{2,1,0:T(8,128)(2,1)}), bf16[8,32,512]{2,1,0:T(8,128)(2,1)S(1)}, u32[]{:S(2)}, u32[]{:S(2)}) %all-to-all-start.1) | async-done | bytes 262176 | tf_op jit(solution)/shard_map/all_to_all | solution.py:47
  43.7 1.7 %shard_map.80 = f32[32,8,128]{2,1,0:T(8,128)} custom-call(s32[4]{0:T(128)S(1)} %copy-done.6, f32[1]{0:T(128)S(6)} %copy.14.refs_1_, bf16[8,32,512]{2,1,0:T(8,128)(2,1)S(1)} %all-to-all-done.1.refs_2_, bf16[256,512]{1,0:T(8,128)(2,1)S(1)} %copy-done, bf16[256,512]{1,0:T(8,128)(2,1)S(1)} %collective-permute-done.4.refs_4_, bf16[256,512]{1,0:T(8,128)(2,1)S(1)} %copy-done.2, ...), custom_call_target="tpu_custom_call" | custom-call | flops 1024 | bytes 1024 | tf_op jit(solution)/shard_map/pallas_call | solution.py:83
  45.4 8.5 %all-to-all-start.2 = ((f32[32,8,128]{2,1,0:T(8,128)}), f32[32,8,128]{2,1,0:T(8,128)S(1)}, u32[]{:S(2)}, u32[]{:S(2)}) async-start(f32[32,8,128]{2,1,0:T(8,128)} %shard_map.80), calls=%async_computation.2 | async-start | bytes 262144 | tf_op jit(solution)/shard_map/all_to_all | solution.py:47
  53.9 0.3 collective-permute-start.6
  54.2 0.0 collective-permute-done.7.refs_8_
  54.2 0.3 collective-permute-start.8
  54.5 7.1 %all-to-all-done.2.refs_7_ = f32[32,8,128]{2,1,0:T(8,128)S(1)} async-done(((f32[32,8,128]{2,1,0:T(8,128)}), f32[32,8,128]{2,1,0:T(8,128)S(1)}, u32[]{:S(2)}, u32[]{:S(2)}) %all-to-all-start.2) | async-done | bytes 131104 | tf_op jit(solution)/shard_map/all_to_all | solution.py:47
  61.6 2.8 %shard_map.81 = (bf16[8,272,128]{2,1,0:T(8,128)(2,1)}, f32[8,128]{1,0:T(8,128)S(1)}) custom-call(s32[4]{0:T(128)S(1)} %copy-done.6, f32[1]{0:T(128)S(6)} %copy.14.refs_1_, bf16[8,32,512]{2,1,0:T(8,128)(2,1)S(1)} %all-to-all-done.1.refs_2_, bf16[256,512]{1,0:T(8,128)(2,1)S(1)} %copy-done, bf16[256,512]{1,0:T(8,128)(2,1)S(1)} %collective-permute-done.4.refs_4_, ...), custom_call_target="tpu_custom_call" | custom-call | flops 1024 | bytes 1024 | tf_op jit(solution)/shard_map/pallas_call | solution.py:83
  64.4 0.6 copy-done.7
  65.0 3.5 %all-to-all-start.3 = ((bf16[8,272,128]{2,1,0:T(8,128)(2,1)}), bf16[8,272,128]{2,1,0:T(8,128)(2,1)S(1)}, u32[]{:S(2)}, u32[]{:S(2)}) async-start(bf16[8,272,128]{2,1,0:T(8,128)(2,1)} %get-tuple-element.39), calls=%async_computation.3 | async-start | bytes 1114112 | tf_op jit(solution)/shard_map/all_to_all | solution.py:47
  68.5 0.4 collective-permute-start.2
  68.9 0.5 collective-permute-start.1
  69.4 10.2 %collective-permute-done.2.refs_2_ = bf16[800,256]{1,0:T(8,128)(2,1)S(1)} collective-permute-done((bf16[800,256]{1,0:T(8,128)(2,1)}, bf16[800,256]{1,0:T(8,128)(2,1)S(1)}, u32[]{:S(2)}, u32[]{:S(2)}) %collective-permute-start.2) | collective-permute-done | bytes 409632 | tf_op jit(solution)/shard_map/ppermute | solution.py:43
  79.6 1.1 collective-permute-start.3
  80.7 0.0 collective-permute-done.1.refs_9_.refs_1_
  80.7 0.0 collective-permute-done.6.refs_7_
  80.7 1.3 collective-permute-done.3.refs_10_.refs_3_
  82.1 5.1 %all-to-all-done.3.refs_2_ = bf16[8,272,128]{2,1,0:T(8,128)(2,1)S(1)} async-done(((bf16[8,272,128]{2,1,0:T(8,128)(2,1)}), bf16[8,272,128]{2,1,0:T(8,128)(2,1)S(1)}, u32[]{:S(2)}, u32[]{:S(2)}) %all-to-all-start.3) | async-done | bytes 557088 | tf_op jit(solution)/shard_map/all_to_all | solution.py:47
  87.2 0.8 copy-done.11
  88.0 3.0 %shard_map.82.refs_4_ = bf16[16,144,128]{2,1,0:T(8,128)(2,1)} custom-call(s32[4]{0:T(128)} %pad_add_fusion.refs_0_, f32[1]{0:T(128)S(6)} %copy.14.refs_1_, bf16[8,272,128]{2,1,0:T(8,128)(2,1)} %copy-done.11, f32[32,512]{1,0:T(8,128)} %get-tuple-element.40.refs_3_, f32[32,128]{1,0:T(8,128)} %get-tuple-element.34.refs_0_.refs_4_, ...), custom_call_target="tpu_custom_call" | custom-call | flops 1024 | bytes 1024 | tf_op jit(solution)/shard_map/pallas_call | solution.py:83
  90.9 3.8 %all-to-all-start.4 = ((bf16[16,144,128]{2,1,0:T(8,128)(2,1)}), bf16[16,144,128]{2,1,0:T(8,128)(2,1)S(1)}, u32[]{:S(2)}, u32[]{:S(2)}) async-start(bf16[16,144,128]{2,1,0:T(8,128)(2,1)} %shard_map.82.refs_4_), calls=%async_computation.4 | async-start | bytes 1179648 | tf_op jit(solution)/shard_map/all_to_all | solution.py:47
  94.7 5.3 %shard_map.83 = (bf16[800,1024]{1,0:T(8,128)(2,1)}, bf16[800,1024]{1,0:T(8,128)(2,1)}) custom-call(bf16[800,256]{1,0:T(8,128)(2,1)} %get-tuple-element.37.refs_0_, bf16[800,256]{1,0:T(8,128)(2,1)} %copy-done.12, bf16[800,256]{1,0:T(8,128)(2,1)} %copy-done.16, bf16[800,256]{1,0:T(8,128)(2,1)} %copy-done.13, bf16[16,144,128]{2,1,0:T(8,128)(2,1)} %shard_map.82.refs_4_), custom_call_target="tpu_custom_call" | custom-call | flops 1024 | bytes 1024 | tf_op jit(solution)/shard_map/pallas_call | solution.py:83
  100.0 5.0 %all-to-all-done.4 = bf16[16,144,128]{2,1,0:T(8,128)(2,1)S(1)} async-done(((bf16[16,144,128]{2,1,0:T(8,128)(2,1)}), bf16[16,144,128]{2,1,0:T(8,128)(2,1)S(1)}, u32[]{:S(2)}, u32[]{:S(2)}) %all-to-all-start.4) | async-done | bytes 589856 | tf_op jit(solution)/shard_map/all_to_all | solution.py:47
  105.0 0.9 copy-done.8
  105.9 2.1 %collective-permute-start.9 = (bf16[2,8,144,128]{3,2,1,0:T(8,128)(2,1)}, bf16[2,8,144,128]{3,2,1,0:T(8,128)(2,1)S(1)}, u32[]{:S(2)}, u32[]{:S(2)}) collective-permute-start(bf16[2,8,144,128]{3,2,1,0:T(8,128)(2,1)} %shard_map.84.refs_1_), channel_id=1, source_target_pairs={{0,8},{8,0},{1,9},{9,1},{2,10},{10,2},{3,11},{11,3},{4,12},{12,4},... | collective-permute-start | bytes 1769480 | tf_op jit(solution)/shard_map/ppermute | solution.py:43
  107.9 1.8 %collective-permute-done.9.refs_2_ = bf16[2,8,144,128]{3,2,1,0:T(8,128)(2,1)S(1)} collective-permute-done((bf16[2,8,144,128]{3,2,1,0:T(8,128)(2,1)}, bf16[2,8,144,128]{3,2,1,0:T(8,128)(2,1)S(1)}, u32[]{:S(2)}, u32[]{:S(2)}) %collective-permute-start.9) | collective-permute-done | bytes 589856 | tf_op jit(solution)/shard_map/ppermute | solution.py:43
  109.8 0.9 copy-done.15
  110.7 8.6 %shard_map.85 = (bf16[800,128]{1,0:T(8,128)(2,1)}, bf16[800,128]{1,0:T(8,128)(2,1)}, bf16[800,128]{1,0:T(8,128)(2,1)}, bf16[800,128]{1,0:T(8,128)(2,1)}, bf16[40...) custom-call(s32[4]{0:T(128)} %pad_add_fusion.refs_0_, ...), custom_call_target="tpu_custom_call" | custom-call | flops 1024 | bytes 1024 | tf_op jit(solution)/shard_map/pallas_call | solution.py:83
  119.3 0.1 collective-permute-start.14
  119.4 0.1 collective-permute-start.10
  119.5 2.7 %collective-permute-start.11 = (bf16[400,128]{1,0:T(8,128)(2,1)}, bf16[400,128]{1,0:T(8,128)(2,1)S(1)}, u32[]{:S(2)}, u32[]{:S(2)}) collective-permute-start(bf16[400,128]{1,0:T(8,128)(2,1)} %get-tuple-element.49), channel_id=1, source_target_pairs={{0,112},{16,0},{32,16},{48,32},{64,48},{80,64},{96,80},{112,96},{1... | collective-permute-start | bytes 307208 | tf_op jit(solution)/shard_map/ppermute | solution.py:368
  122.2 2.3 %collective-permute-start.15 = (bf16[800,128]{1,0:T(8,128)(2,1)}, bf16[800,128]{1,0:T(8,128)(2,1)S(1)}, u32[]{:S(2)}, u32[]{:S(2)}) collective-permute-start(bf16[800,128]{1,0:T(8,128)(2,1)} %get-tuple-element.53), channel_id=1, source_target_pairs={{0,96},{16,112},{32,0},{48,16},{64,32},{80,48},{96,64},{112,80},{1... | collective-permute-start | bytes 614408 | tf_op jit(solution)/shard_map/ppermute | solution.py:368
  124.4 0.0 collective-permute-start.16
  124.4 8.6 %collective-permute-done.10.refs_2_ = bf16[400,128]{1,0:T(8,128)(2,1)S(1)} collective-permute-done((bf16[400,128]{1,0:T(8,128)(2,1)}, bf16[400,128]{1,0:T(8,128)(2,1)S(1)}, u32[]{:S(2)}, u32[]{:S(2)}) %collective-permute-start.10) | collective-permute-done | bytes 102432 | tf_op jit(solution)/shard_map/ppermute | solution.py:368
  133.1 0.0 collective-permute-start.17
  133.1 0.9 copy-done.3
  134.0 0.9 copy-done.4
  134.9 0.1 shard_map.86
  135.0 0.5 collective-permute-start.12
  135.5 0.0 collective-permute-done.14.refs_3_
  135.5 4.1 %collective-permute-start.13 = (bf16[800,128]{1,0:T(8,128)(2,1)S(1)}, bf16[800,128]{1,0:T(8,128)(2,1)S(1)}, u32[]{:S(2)}, u32[]{:S(2)}) collective-permute-start(bf16[800,128]{1,0:T(8,128)(2,1)S(1)} %get-tuple-element.51), channel_id=1, source_target_pairs={{0,80},{16,96},{32,112},{48,0},{64,16},{80,32},{96,48},{112,64},{1... | collective-permute-start | bytes 614408 | tf_op jit(solution)/shard_map/ppermute | solution.py:368
  139.6 0.0 collective-permute-done.15.refs_4_
  139.6 0.0 collective-permute-done.16.refs_5_
  139.6 0.0 collective-permute-done.17.refs_6_
  139.6 12.6 %collective-permute-done.12.refs_1_ = bf16[800,128]{1,0:T(8,128)(2,1)S(1)} collective-permute-done((bf16[800,128]{1,0:T(8,128)(2,1)S(1)}, bf16[800,128]{1,0:T(8,128)(2,1)S(1)}, u32[]{:S(2)}, u32[]{:S(2)}) %collective-permute-start.12) | collective-permute-done | bytes 204832 | tf_op jit(solution)/shard_map/ppermute | solution.py:368
  152.1 0.0 collective-permute-done.13.refs_2_
  152.1 0.9 copy-done.5
  153.1 1.0 shard_map.87
  (29 shorter events, 0.1 us)
Async XLA Ops:
  7.1 16.1 %collective-permute-start = (bf16[256,512]{1,0:T(8,128)(2,1)}, bf16[256,512]{1,0:T(8,128)(2,1)S(1)}, u32[]{:S(2)}, u32[]{:S(2)}) collective-permute-start(bf16[256,512]{1,0:T(8,128)(2,1)} %get-tuple-element.33.refs_3_), channel_id=1, source_target_pairs={{0,128},{128,0},{1,129},{129,1},{2,130},{130,2},{3,131},{131,3},{4... | collective-permute-start | bytes 786440 | tf_op jit(solution)/shard_map/ppermute | solution.py:43
  9.2 14.0 %all-to-all-start = ((bf16[8,32,512]{2,1,0:T(8,128)(2,1)}), bf16[8,32,512]{2,1,0:T(8,128)(2,1)S(1)}, u32[]{:S(2)}, u32[]{:S(2)}) async-start(bf16[8,32,512]{2,1,0:T(8,128)(2,1)} %bitcast.13), calls=%async_computation | async-start | bytes 524288 | tf_op jit(solution)/shard_map/all_to_all | solution.py:47
  23.2 0.7 copy-start.14
  23.2 0.8 copy-start.1
  24.0 10.3 %copy-start = (bf16[256,512]{1,0:T(8,128)(2,1)S(1)}, bf16[256,512]{1,0:T(8,128)(2,1)}, u32[]{:S(2)}) copy-start(bf16[256,512]{1,0:T(8,128)(2,1)} %get-tuple-element.33.refs_3_) | copy-start | bytes 786436
  24.0 19.7 %copy-start.6 = (s32[4]{0:T(128)S(1)}, s32[4]{0:T(128)}, u32[]{:S(2)}) copy-start(s32[4]{0:T(128)} %pad_add_fusion.refs_0_) | copy-start | bytes 52
  25.9 11.4 %copy-start.2 = (bf16[256,512]{1,0:T(8,128)(2,1)S(1)}, bf16[256,512]{1,0:T(8,128)(2,1)}, u32[]{:S(2)}) copy-start(bf16[256,512]{1,0:T(8,128)(2,1)} %copy-done.1) | copy-start | bytes 786436
  25.9 28.0 %copy-start.9 = (bf16[512,1024]{1,0:T(8,128)(2,1)S(1)}, bf16[512,1024]{1,0:T(8,128)(2,1)}, u32[]{:S(2)}) copy-start(bf16[512,1024]{1,0:T(8,128)(2,1)} %get-tuple-element.32.refs_1_.refs_6_) | copy-start | bytes 3145732
  25.9 28.4 %collective-permute-start.7 = (bf16[512,1024]{1,0:T(8,128)(2,1)}, bf16[512,1024]{1,0:T(8,128)(2,1)}, u32[]{:S(2)}, u32[]{:S(2)}) collective-permute-start(bf16[512,1024]{1,0:T(8,128)(2,1)} %get-tuple-element.42), channel_id=1, source_target_pairs={{0,128},{128,0},{1,129},{129,1},{2,130},{130,2},{3,131},{131,3},{4... | collective-permute-start | bytes 3145736 | tf_op jit(solution)/shard_map/ppermute | solution.py:43
  26.0 17.7 %all-to-all-start.1 = ((bf16[8,32,512]{2,1,0:T(8,128)(2,1)}), bf16[8,32,512]{2,1,0:T(8,128)(2,1)S(1)}, u32[]{:S(2)}, u32[]{:S(2)}) async-start(bf16[8,32,512]{2,1,0:T(8,128)(2,1)} %get-tuple-element.38), calls=%async_computation.1 | async-start | bytes 524288 | tf_op jit(solution)/shard_map/all_to_all | solution.py:47
  34.3 4.1 %collective-permute-start.4 = (bf16[256,512]{1,0:T(8,128)(2,1)S(1)}, bf16[256,512]{1,0:T(8,128)(2,1)S(1)}, u32[]{:S(2)}, u32[]{:S(2)}) collective-permute-start(bf16[256,512]{1,0:T(8,128)(2,1)S(1)} %copy-done), channel_id=1, source_target_pairs={{0,8},{8,0},{1,9},{9,1},{2,10},{10,2},{3,11},{11,3},{4,12},{12,4},... | collective-permute-start | bytes 786440 | tf_op jit(solution)/shard_map/ppermute | solution.py:43
  37.3 1.5 collective-permute-start.5
  45.4 16.2 %all-to-all-start.2 = ((f32[32,8,128]{2,1,0:T(8,128)}), f32[32,8,128]{2,1,0:T(8,128)S(1)}, u32[]{:S(2)}, u32[]{:S(2)}) async-start(f32[32,8,128]{2,1,0:T(8,128)} %shard_map.80), calls=%async_computation.2 | async-start | bytes 262144 | tf_op jit(solution)/shard_map/all_to_all | solution.py:47
  53.9 26.8 %collective-permute-start.6 = (bf16[512,1024]{1,0:T(8,128)(2,1)S(1)}, bf16[512,1024]{1,0:T(8,128)(2,1)S(1)}, u32[]{:S(2)}, u32[]{:S(2)}) collective-permute-start(bf16[512,1024]{1,0:T(8,128)(2,1)S(1)} %copy-done.9), channel_id=1, source_target_pairs={{0,8},{8,0},{1,9},{9,1},{2,10},{10,2},{3,11},{11,3},{4,12},{12,4},... | collective-permute-start | bytes 3145736 | tf_op jit(solution)/shard_map/ppermute | solution.py:43
  54.2 32.9 %collective-permute-start.8 = (bf16[512,1024]{1,0:T(8,128)(2,1)}, bf16[512,1024]{1,0:T(8,128)(2,1)}, u32[]{:S(2)}, u32[]{:S(2)}) collective-permute-start(bf16[512,1024]{1,0:T(8,128)(2,1)} %collective-permute-done.7.refs_8_), channel_id=1, source_target_pairs={{0,8},{8,0},{1,9},{9,1},{2,10},{10,2},{3,11},{11,3},{4,12},{12,4},... | collective-permute-start | bytes 3145736 | tf_op jit(solution)/shard_map/ppermute | solution.py:43
  64.4 0.6 copy-start.7
  65.0 22.2 %all-to-all-start.3 = ((bf16[8,272,128]{2,1,0:T(8,128)(2,1)}), bf16[8,272,128]{2,1,0:T(8,128)(2,1)S(1)}, u32[]{:S(2)}, u32[]{:S(2)}) async-start(bf16[8,272,128]{2,1,0:T(8,128)(2,1)} %get-tuple-element.39), calls=%async_computation.3 | async-start | bytes 1114112 | tf_op jit(solution)/shard_map/all_to_all | solution.py:47
  68.5 11.1 %collective-permute-start.2 = (bf16[800,256]{1,0:T(8,128)(2,1)}, bf16[800,256]{1,0:T(8,128)(2,1)S(1)}, u32[]{:S(2)}, u32[]{:S(2)}) collective-permute-start(bf16[800,256]{1,0:T(8,128)(2,1)} %get-tuple-element.37.refs_0_), channel_id=1, source_target_pairs={{0,128},{128,0},{1,129},{129,1},{2,130},{130,2},{3,131},{131,3},{4... | collective-permute-start | bytes 1228808 | tf_op jit(solution)/shard_map/ppermute | solution.py:43
  68.9 11.8 %collective-permute-start.1 = (bf16[800,256]{1,0:T(8,128)(2,1)}, bf16[800,256]{1,0:T(8,128)(2,1)S(1)}, u32[]{:S(2)}, u32[]{:S(2)}) collective-permute-start(bf16[800,256]{1,0:T(8,128)(2,1)} %get-tuple-element.37.refs_0_), channel_id=1, source_target_pairs={{0,8},{8,0},{1,9},{9,1},{2,10},{10,2},{3,11},{11,3},{4,12},{12,4},... | collective-permute-start | bytes 1228808 | tf_op jit(solution)/shard_map/ppermute | solution.py:43
  79.6 1.1 copy-start.16
  79.6 2.4 %collective-permute-start.3 = (bf16[800,256]{1,0:T(8,128)(2,1)S(1)}, bf16[800,256]{1,0:T(8,128)(2,1)S(1)}, u32[]{:S(2)}, u32[]{:S(2)}) collective-permute-start(bf16[800,256]{1,0:T(8,128)(2,1)S(1)} %collective-permute-done.2.refs_2_), channel_id=1, source_target_pairs={{0,8},{8,0},{1,9},{9,1},{2,10},{10,2},{3,11},{11,3},{4,12},{12,4},... | collective-permute-start | bytes 1228808 | tf_op jit(solution)/shard_map/ppermute | solution.py:43
  80.7 6.5 %copy-start.12 = (bf16[800,256]{1,0:T(8,128)(2,1)}, bf16[800,256]{1,0:T(8,128)(2,1)S(1)}, u32[]{:S(2)}) copy-start(bf16[800,256]{1,0:T(8,128)(2,1)S(1)} %collective-permute-done.1.refs_9_.refs_1_) | copy-start | bytes 1228804
  80.7 6.5 %copy-start.10 = (bf16[512,1024]{1,0:T(8,128)(2,1)}, bf16[512,1024]{1,0:T(8,128)(2,1)S(1)}, u32[]{:S(2)}) copy-start(bf16[512,1024]{1,0:T(8,128)(2,1)S(1)} %collective-permute-done.6.refs_7_) | copy-start | bytes 3145732
  82.1 5.1 %copy-start.13 = (bf16[800,256]{1,0:T(8,128)(2,1)}, bf16[800,256]{1,0:T(8,128)(2,1)S(1)}, u32[]{:S(2)}) copy-start(bf16[800,256]{1,0:T(8,128)(2,1)S(1)} %collective-permute-done.3.refs_10_.refs_3_) | copy-start | bytes 1228804
  87.1 0.8 copy-start.11
  90.9 14.1 %all-to-all-start.4 = ((bf16[16,144,128]{2,1,0:T(8,128)(2,1)}), bf16[16,144,128]{2,1,0:T(8,128)(2,1)S(1)}, u32[]{:S(2)}, u32[]{:S(2)}) async-start(bf16[16,144,128]{2,1,0:T(8,128)(2,1)} %shard_map.82.refs_4_), calls=%async_computation.4 | async-start | bytes 1179648 | tf_op jit(solution)/shard_map/all_to_all | solution.py:47
  105.0 0.9 copy-start.8
  105.9 3.9 %collective-permute-start.9 = (bf16[2,8,144,128]{3,2,1,0:T(8,128)(2,1)}, bf16[2,8,144,128]{3,2,1,0:T(8,128)(2,1)S(1)}, u32[]{:S(2)}, u32[]{:S(2)}) collective-permute-start(bf16[2,8,144,128]{3,2,1,0:T(8,128)(2,1)} %shard_map.84.refs_1_), channel_id=1, source_target_pairs={{0,8},{8,0},{1,9},{9,1},{2,10},{10,2},{3,11},{11,3},{4,12},{12,4},... | collective-permute-start | bytes 1769480 | tf_op jit(solution)/shard_map/ppermute | solution.py:43
  109.8 0.9 copy-start.15
  119.3 16.2 %collective-permute-start.14 = (bf16[800,128]{1,0:T(8,128)(2,1)}, bf16[800,128]{1,0:T(8,128)(2,1)S(1)}, u32[]{:S(2)}, u32[]{:S(2)}) collective-permute-start(bf16[800,128]{1,0:T(8,128)(2,1)} %get-tuple-element.52), channel_id=1, source_target_pairs={{0,32},{16,48},{32,64},{48,80},{64,96},{80,112},{96,0},{112,16},{1... | collective-permute-start | bytes 614408 | tf_op jit(solution)/shard_map/ppermute | solution.py:368
  119.4 13.7 %collective-permute-start.10 = (bf16[400,128]{1,0:T(8,128)(2,1)}, bf16[400,128]{1,0:T(8,128)(2,1)S(1)}, u32[]{:S(2)}, u32[]{:S(2)}) collective-permute-start(bf16[400,128]{1,0:T(8,128)(2,1)} %get-tuple-element.48), channel_id=1, source_target_pairs={{0,16},{16,32},{32,48},{48,64},{64,80},{80,96},{96,112},{112,0},{1... | collective-permute-start | bytes 307208 | tf_op jit(solution)/shard_map/ppermute | solution.py:368
  119.5 13.6 %collective-permute-start.11 = (bf16[400,128]{1,0:T(8,128)(2,1)}, bf16[400,128]{1,0:T(8,128)(2,1)S(1)}, u32[]{:S(2)}, u32[]{:S(2)}) collective-permute-start(bf16[400,128]{1,0:T(8,128)(2,1)} %get-tuple-element.49), channel_id=1, source_target_pairs={{0,112},{16,0},{32,16},{48,32},{64,48},{80,64},{96,80},{112,96},{1... | collective-permute-start | bytes 307208 | tf_op jit(solution)/shard_map/ppermute | solution.py:368
  122.2 17.4 %collective-permute-start.15 = (bf16[800,128]{1,0:T(8,128)(2,1)}, bf16[800,128]{1,0:T(8,128)(2,1)S(1)}, u32[]{:S(2)}, u32[]{:S(2)}) collective-permute-start(bf16[800,128]{1,0:T(8,128)(2,1)} %get-tuple-element.53), channel_id=1, source_target_pairs={{0,96},{16,112},{32,0},{48,16},{64,32},{80,48},{96,64},{112,80},{1... | collective-permute-start | bytes 614408 | tf_op jit(solution)/shard_map/ppermute | solution.py:368
  124.4 15.1 %collective-permute-start.16 = (bf16[800,128]{1,0:T(8,128)(2,1)}, bf16[800,128]{1,0:T(8,128)(2,1)S(1)}, u32[]{:S(2)}, u32[]{:S(2)}) collective-permute-start(bf16[800,128]{1,0:T(8,128)(2,1)} %get-tuple-element.54), channel_id=1, source_target_pairs={{0,16},{16,32},{32,48},{48,64},{64,80},{80,96},{96,112},{112,0},{1... | collective-permute-start | bytes 614408 | tf_op jit(solution)/shard_map/ppermute | solution.py:368
  133.1 6.5 %collective-permute-start.17 = (bf16[800,128]{1,0:T(8,128)(2,1)}, bf16[800,128]{1,0:T(8,128)(2,1)S(1)}, u32[]{:S(2)}, u32[]{:S(2)}) collective-permute-start(bf16[800,128]{1,0:T(8,128)(2,1)} %get-tuple-element.55), channel_id=1, source_target_pairs={{0,112},{16,0},{32,16},{48,32},{64,48},{80,64},{96,80},{112,96},{1... | collective-permute-start | bytes 614408 | tf_op jit(solution)/shard_map/ppermute | solution.py:368
  133.1 0.9 copy-start.3
  134.0 0.9 copy-start.4
  135.0 17.1 %collective-permute-start.12 = (bf16[800,128]{1,0:T(8,128)(2,1)S(1)}, bf16[800,128]{1,0:T(8,128)(2,1)S(1)}, u32[]{:S(2)}, u32[]{:S(2)}) collective-permute-start(bf16[800,128]{1,0:T(8,128)(2,1)S(1)} %get-tuple-element.50), channel_id=1, source_target_pairs={{0,48},{16,64},{32,80},{48,96},{64,112},{80,0},{96,16},{112,32},{1... | collective-permute-start | bytes 614408 | tf_op jit(solution)/shard_map/ppermute | solution.py:368
  135.5 16.7 %collective-permute-start.13 = (bf16[800,128]{1,0:T(8,128)(2,1)S(1)}, bf16[800,128]{1,0:T(8,128)(2,1)S(1)}, u32[]{:S(2)}, u32[]{:S(2)}) collective-permute-start(bf16[800,128]{1,0:T(8,128)(2,1)S(1)} %get-tuple-element.51), channel_id=1, source_target_pairs={{0,80},{16,96},{32,112},{48,0},{64,16},{80,32},{96,48},{112,64},{1... | collective-permute-start | bytes 614408 | tf_op jit(solution)/shard_map/ppermute | solution.py:368
  152.1 0.9 copy-start.5

commit v8 on v7

--- a/solution.py
+++ b/solution.py
@@ -199,11 +199,12 @@
 
 
 def weights_kernel(where_ref, scale_ref, video_ref, *refs):
-    text_refs, (got_ref, packed_ref, log_ref, inv_ref) = refs[:4], refs[4:]
+    text_refs, (got_ref, packed_ref, inv_ref) = refs[:4], refs[4:]
     count, own_rows, emb = video_ref.shape
     rows = count * own_rows
     col_sum = jnp.sum(got_ref[...], axis=0)
-    log_ref[...] = jnp.log(col_sum)
+    logs = jnp.sum(jnp.sum(jnp.log(col_sum), axis=0, keepdims=True), axis=1, keepdims=True)
+    logs = split3(logs)
     inv_ref[...] = 1.0 / col_sum
     first = jnp.zeros((rows, emb), F32)
     second = jnp.zeros((rows, emb), F32)
@@ -229,10 +230,13 @@
     lane = lax.broadcasted_iota(jnp.int32, (count, own_rows, LANES), 2)
     turned = jnp.where(lane == row, row_hi, jnp.where(lane == row + own_rows, row_lo, 0.0))
     turned = jnp.sum(turned, axis=1, keepdims=True)
-    packed_ref[:, 2 * tiles * own_rows :, :] = jnp.broadcast_to(turned, (count, EXTRA, LANES)).astype(BF)
-
-
-def proj_kernel(where_ref, scale_ref, back_ref, unit_ref, inv_ref, text_ref, log_ref, out_ref, *, sharers):
+    row, lane = row[:, :EXTRA], lane[:, :EXTRA]
+    extra = jnp.where(lane == 0, logs[0], jnp.where(lane == 1, logs[1], jnp.where(lane == 2, logs[2], 0.0)))
+    extra = jnp.where(row == 0, turned, extra)
+    packed_ref[:, 2 * tiles * own_rows :, :] = extra.astype(BF)
+
+
+def proj_kernel(where_ref, scale_ref, back_ref, unit_ref, inv_ref, text_ref, out_ref, *, sharers):
     scale_val = scale_ref[0]
     own_rows, emb = unit_ref.shape
     back = jnp.sum(back_ref[...].astype(F32), axis=0)
@@ -248,7 +252,8 @@
     unit = unit_ref[...]
     positive = scale_val * jnp.sum(unit.astype(BF).astype(F32) * text, axis=-1, keepdims=True)
     rows_piece = jnp.sum(jnp.log(row_sum) - 2.0 * positive, axis=0, keepdims=True)
-    cols_piece = jnp.sum(jnp.sum(log_ref[...], axis=0, keepdims=True), axis=1, keepdims=True)
+    logs = back[2 * tiles * own_rows + 1 : 2 * tiles * own_rows + 2]
+    cols_piece = jnp.sum(logs, axis=1, keepdims=True)
     a, b, c = split3(rows_piece + cols_piece / sharers)
     grad_emb = 0.5 * scale_val * weighted - scale_val * text
     grad_proj = inv_ref[:, :1] * (
@@ -411,17 +416,17 @@
     cols = exchange(cols, PLANE)
     pre_x = swap(pre_own, "x_lo")
     pre = (pre_own, swap(pre_own, "core"), pre_x, swap(pre_x, "core"))
-    packed, logs = call(
-        weights_kernel, [((z_count, 2 * packs + EXTRA, LANES), BF), ((8, LANES), F32)], LIM[4],
+    (packed,) = call(
+        weights_kernel, [((z_count, 2 * packs + EXTRA, LANES), BF)], LIM[4],
         where, logit_scale, video_rows, text_emb, *texts, cols, scalars=2, direct=True,
         scratch=[pltpu.VMEM((8, LANES), F32)],
     )
     feats_q = (feats, swap(feats, "core"), feats_x, swap(feats_x, "core"))
     back = exchange(packed, "z")
     (sent,) = call(
-        functools.partial(proj_kernel, sharers=4 * mp_count),
+        functools.partial(proj_kernel, sharers=4 * mp_count * z_count),
         [((2 * mp_count, packs + EXTRA, LANES), BF)], LIM[5],
-        where, logit_scale, back, unit, inv_norm, text_emb.reshape(mp_count, own_rows, emb), logs,
+        where, logit_scale, back, unit, inv_norm, text_emb.reshape(mp_count, own_rows, emb),
         scalars=2, after=(feats_q[1], feats_q[3], pre[1], pre[3]),
     )
     gelus = call(gelu_kernel, [((hid, 4 * rows), BF)] * 2, LIM[6], *pre, after=(sent,))

time: 155 us -> 155 us (level)
    unnamed x34 -> x32, local copies, waits for them, and re-layouts: 6.71 us -> 6.53 us
where the time goes in v8:
time: 155 us; the launch traced here: 154 us
  waiting for transfers between devices  60.1 us (39%)
  starting transfers between devices  50 us (32%)
  Pallas kernels  35.2 us (23%)
  local copies, waits for them, and re-layouts  6.53 us (4%)
    pallas_call x10, Pallas kernels, call(): pl.pallas_call(body, grid=(1,), out_shape=[jax.ShapeDtypeStruct(s, d) for...  35.2 us
    all_to_all x5, starting transfers between devices, exchange(): return lax.all_to_all(value, axis, 0, 0)  30.4 us
    all_to_all x5, waiting for transfers between devices, exchange(): return lax.all_to_all(value, axis, 0, 0)  24.6 us
    ppermute x8, waiting for transfers between devices, ahead(): return lax.ppermute(value, 'z', [(i, (i + step) % 8) for i in range(8)])  21.2 us
    ppermute x10, waiting for transfers between devices, swap(): return lax.ppermute(value, axis, [(0, 1), (1, 0)])  14.2 us
    ppermute x10, starting transfers between devices, swap(): return lax.ppermute(value, axis, [(0, 1), (1, 0)])  9.94 us
    ppermute x8, starting transfers between devices, ahead(): return lax.ppermute(value, 'z', [(i, (i + step) % 8) for i in range(8)])  9.66 us
    unnamed x32, local copies, waits for them, and re-layouts  6.53 us
  transfers between devices with their start and end apart: 23, of which 12 were waited for; matrix products, arithmetic and copies ran while one was open for 0% of the time, Pallas kernels for 9%

profile of v8, /device:TPU:1, one launch (start us, length us, event | category | flops | bytes accessed | tf_op | source)
XLA Modules:
  0.0 153.8 jit_solution(1278598702364828246)
XLA Ops:
  0.6 6.4 %shard_map.76 = (bf16[256,512]{1,0:T(8,128)(2,1)}, bf16[800,256]{1,0:T(8,128)(2,1)}, bf16[256,512]{1,0:T(8,128)(2,1)}) custom-call(bf16[256,512]{1,0:T(8,128)(2,1)} %refs_0_.1, bf16[256,3200]{1,0:T(8,128)(2,1)} %refs_1_.6, bf16[800,3200]{1,0:T(8,128)(2,1)} %bitcast.12, bf16[800,512]{1,0:T(8,128)(2,1)} %refs_3_.3), custom_call_target="tpu_custom_call" | custom-call | flops 1024 | bytes 1024 | tf_op jit(solution)/shard_map/pallas_call | solution.py:83
  7.1 2.1 %collective-permute-start = (bf16[256,512]{1,0:T(8,128)(2,1)}, bf16[256,512]{1,0:T(8,128)(2,1)S(1)}, u32[]{:S(2)}, u32[]{:S(2)}) collective-permute-start(bf16[256,512]{1,0:T(8,128)(2,1)} %get-tuple-element.31.refs_3_), channel_id=1, source_target_pairs={{0,128},{128,0},{1,129},{129,1},{2,130},{130,2},{3,131},{131,3},{4... | collective-permute-start | bytes 786440 | tf_op jit(solution)/shard_map/ppermute | solution.py:43
  9.2 6.4 %all-to-all-start = ((bf16[8,32,512]{2,1,0:T(8,128)(2,1)}), bf16[8,32,512]{2,1,0:T(8,128)(2,1)S(1)}, u32[]{:S(2)}, u32[]{:S(2)}) async-start(bf16[8,32,512]{2,1,0:T(8,128)(2,1)} %bitcast.13), calls=%async_computation | async-start | bytes 524288 | tf_op jit(solution)/shard_map/all_to_all | solution.py:47
  15.6 0.6 pad_add_fusion.refs_0_
  16.1 4.5 %shard_map.77 = (bf16[512,1024]{1,0:T(8,128)(2,1)}, bf16[512,1024]{1,0:T(8,128)(2,1)}) custom-call(s32[4]{0:T(128)} %pad_add_fusion.refs_0_, bf16[256,3200]{1,0:T(8,128)(2,1)} %refs_1_.6), custom_call_target="tpu_custom_call" | custom-call | flops 1024 | bytes 1024 | tf_op jit(solution)/shard_map/pallas_call | solution.py:83
  20.6 2.6 %all-to-all-done.refs_0_ = bf16[8,32,512]{2,1,0:T(8,128)(2,1)S(1)} async-done(((bf16[8,32,512]{2,1,0:T(8,128)(2,1)}), bf16[8,32,512]{2,1,0:T(8,128)(2,1)S(1)}, u32[]{:S(2)}, u32[]{:S(2)}) %all-to-all-start) | async-done | bytes 262176 | tf_op jit(solution)/shard_map/all_to_all | solution.py:47
  23.2 0.0 collective-permute-done.refs_2_.refs_5_
  23.2 0.7 copy-done.13
  23.9 0.1 copy-done.1
  24.0 1.8 %shard_map.78 = (f32[32,512]{1,0:T(8,128)}, f32[32,128]{1,0:T(8,128)}, bf16[8,32,512]{2,1,0:T(8,128)(2,1)}) custom-call(bf16[8,32,512]{2,1,0:T(8,128)(2,1)} %copy-done.13, bf16[512,1024]{1,0:T(8,128)(2,1)} %get-tuple-element.30.refs_1_.refs_6_, bf16[256,512]{1,0:T(8,128)(2,1)} %copy-done.1), custom_call_target="tpu_custom_call" | custom-call | flops 1024 | bytes 1024 | tf_op jit(solution)/shard_map/pallas_call | solution.py:83
  25.9 0.1 collective-permute-start.7
  26.0 8.2 %all-to-all-start.1 = ((bf16[8,32,512]{2,1,0:T(8,128)(2,1)}), bf16[8,32,512]{2,1,0:T(8,128)(2,1)S(1)}, u32[]{:S(2)}, u32[]{:S(2)}) async-start(bf16[8,32,512]{2,1,0:T(8,128)(2,1)} %get-tuple-element.36), calls=%async_computation.1 | async-start | bytes 524288 | tf_op jit(solution)/shard_map/all_to_all | solution.py:47
  34.2 2.9 %collective-permute-start.4 = (bf16[256,512]{1,0:T(8,128)(2,1)S(1)}, bf16[256,512]{1,0:T(8,128)(2,1)S(1)}, u32[]{:S(2)}, u32[]{:S(2)}) collective-permute-start(bf16[256,512]{1,0:T(8,128)(2,1)S(1)} %copy-done), channel_id=1, source_target_pairs={{0,8},{8,0},{1,9},{9,1},{2,10},{10,2},{3,11},{11,3},{4,12},{12,4},... | collective-permute-start | bytes 786440 | tf_op jit(solution)/shard_map/ppermute | solution.py:43
  37.1 0.1 collective-permute-start.5
  37.9 0.4 collective-permute-done.4.refs_4_
  38.3 0.4 collective-permute-done.5.refs_6_
  38.7 4.9 %all-to-all-done.1.refs_2_ = bf16[8,32,512]{2,1,0:T(8,128)(2,1)S(1)} async-done(((bf16[8,32,512]{2,1,0:T(8,128)(2,1)}), bf16[8,32,512]{2,1,0:T(8,128)(2,1)S(1)}, u32[]{:S(2)}, u32[]{:S(2)}) %all-to-all-start.1) | async-done | bytes 262176 | tf_op jit(solution)/shard_map/all_to_all | solution.py:47
  43.6 1.7 %shard_map.80 = f32[32,8,128]{2,1,0:T(8,128)} custom-call(s32[4]{0:T(128)S(1)} %copy-done.6, f32[1]{0:T(128)S(6)} %copy.14.refs_1_, bf16[8,32,512]{2,1,0:T(8,128)(2,1)S(1)} %all-to-all-done.1.refs_2_, bf16[256,512]{1,0:T(8,128)(2,1)S(1)} %copy-done, bf16[256,512]{1,0:T(8,128)(2,1)S(1)} %collective-permute-done.4.refs_4_, bf16[256,512]{1,0:T(8,128)(2,1)S(1)} %copy-done.2, ...), custom_call_target="tpu_custom_call" | custom-call | flops 1024 | bytes 1024 | tf_op jit(solution)/shard_map/pallas_call | solution.py:83
  45.3 8.5 %all-to-all-start.2 = ((f32[32,8,128]{2,1,0:T(8,128)}), f32[32,8,128]{2,1,0:T(8,128)S(1)}, u32[]{:S(2)}, u32[]{:S(2)}) async-start(f32[32,8,128]{2,1,0:T(8,128)} %shard_map.80), calls=%async_computation.2 | async-start | bytes 262144 | tf_op jit(solution)/shard_map/all_to_all | solution.py:47
  53.8 0.3 collective-permute-start.6
  54.1 0.0 collective-permute-done.7.refs_8_
  54.1 0.3 collective-permute-start.8
  54.4 7.1 %all-to-all-done.2.refs_7_ = f32[32,8,128]{2,1,0:T(8,128)S(1)} async-done(((f32[32,8,128]{2,1,0:T(8,128)}), f32[32,8,128]{2,1,0:T(8,128)S(1)}, u32[]{:S(2)}, u32[]{:S(2)}) %all-to-all-start.2) | async-done | bytes 131104 | tf_op jit(solution)/shard_map/all_to_all | solution.py:47
  61.5 2.8 %shard_map.81 = bf16[8,272,128]{2,1,0:T(8,128)(2,1)} custom-call(s32[4]{0:T(128)S(1)} %copy-done.6, f32[1]{0:T(128)S(6)} %copy.14.refs_1_, bf16[8,32,512]{2,1,0:T(8,128)(2,1)S(1)} %all-to-all-done.1.refs_2_, bf16[256,512]{1,0:T(8,128)(2,1)S(1)} %copy-done, bf16[256,512]{1,0:T(8,128)(2,1)S(1)} %collective-permute-done.4.refs_4_, ...), custom_call_target="tpu_custom_call" | custom-call | flops 1024 | bytes 1024 | tf_op jit(solution)/shard_map/pallas_call | solution.py:83
  64.2 3.5 %all-to-all-start.3 = ((bf16[8,272,128]{2,1,0:T(8,128)(2,1)}), bf16[8,272,128]{2,1,0:T(8,128)(2,1)S(1)}, u32[]{:S(2)}, u32[]{:S(2)}) async-start(bf16[8,272,128]{2,1,0:T(8,128)(2,1)} %shard_map.81), calls=%async_computation.3 | async-start | bytes 1114112 | tf_op jit(solution)/shard_map/all_to_all | solution.py:47
  67.8 0.4 collective-permute-start.2
  68.2 0.5 collective-permute-start.1
  68.7 10.2 %collective-permute-done.2.refs_2_ = bf16[800,256]{1,0:T(8,128)(2,1)S(1)} collective-permute-done((bf16[800,256]{1,0:T(8,128)(2,1)}, bf16[800,256]{1,0:T(8,128)(2,1)S(1)}, u32[]{:S(2)}, u32[]{:S(2)}) %collective-permute-start.2) | collective-permute-done | bytes 409632 | tf_op jit(solution)/shard_map/ppermute | solution.py:43
  78.9 1.1 collective-permute-start.3
  80.0 0.0 collective-permute-done.1.refs_8_.refs_1_
  80.0 1.3 collective-permute-done.3.refs_9_.refs_3_
  81.3 5.1 %all-to-all-done.3.refs_2_ = bf16[8,272,128]{2,1,0:T(8,128)(2,1)S(1)} async-done(((bf16[8,272,128]{2,1,0:T(8,128)(2,1)}), bf16[8,272,128]{2,1,0:T(8,128)(2,1)S(1)}, u32[]{:S(2)}, u32[]{:S(2)}) %all-to-all-start.3) | async-done | bytes 557088 | tf_op jit(solution)/shard_map/all_to_all | solution.py:47
  86.5 0.8 copy-done.10
  87.2 0.4 copy-done.9
  87.6 2.9 %shard_map.82.refs_4_ = bf16[16,144,128]{2,1,0:T(8,128)(2,1)} custom-call(s32[4]{0:T(128)} %pad_add_fusion.refs_0_, f32[1]{0:T(128)S(6)} %copy.14.refs_1_, bf16[8,272,128]{2,1,0:T(8,128)(2,1)} %copy-done.10, f32[32,512]{1,0:T(8,128)} %get-tuple-element.37.refs_3_, f32[32,128]{1,0:T(8,128)} %get-tuple-element.32.refs_0_.refs_4_, ...), custom_call_target="tpu_custom_call" | custom-call | flops 1024 | bytes 1024 | tf_op jit(solution)/shard_map/pallas_call | solution.py:83
  90.6 3.8 %all-to-all-start.4 = ((bf16[16,144,128]{2,1,0:T(8,128)(2,1)}), bf16[16,144,128]{2,1,0:T(8,128)(2,1)S(1)}, u32[]{:S(2)}, u32[]{:S(2)}) async-start(bf16[16,144,128]{2,1,0:T(8,128)(2,1)} %shard_map.82.refs_4_), calls=%async_computation.4 | async-start | bytes 1179648 | tf_op jit(solution)/shard_map/all_to_all | solution.py:47
  94.4 5.3 %shard_map.83 = (bf16[800,1024]{1,0:T(8,128)(2,1)}, bf16[800,1024]{1,0:T(8,128)(2,1)}) custom-call(bf16[800,256]{1,0:T(8,128)(2,1)} %get-tuple-element.35.refs_0_, bf16[800,256]{1,0:T(8,128)(2,1)} %copy-done.11, bf16[800,256]{1,0:T(8,128)(2,1)} %copy-done.15, bf16[800,256]{1,0:T(8,128)(2,1)} %copy-done.12, bf16[16,144,128]{2,1,0:T(8,128)(2,1)} %shard_map.82.refs_4_), custom_call_target="tpu_custom_call" | custom-call | flops 1024 | bytes 1024 | tf_op jit(solution)/shard_map/pallas_call | solution.py:83
  99.6 5.0 %all-to-all-done.4 = bf16[16,144,128]{2,1,0:T(8,128)(2,1)S(1)} async-done(((bf16[16,144,128]{2,1,0:T(8,128)(2,1)}), bf16[16,144,128]{2,1,0:T(8,128)(2,1)S(1)}, u32[]{:S(2)}, u32[]{:S(2)}) %all-to-all-start.4) | async-done | bytes 589856 | tf_op jit(solution)/shard_map/all_to_all | solution.py:47
  104.6 0.9 copy-done.7
  105.5 2.1 %collective-permute-start.9 = (bf16[2,8,144,128]{3,2,1,0:T(8,128)(2,1)}, bf16[2,8,144,128]{3,2,1,0:T(8,128)(2,1)S(1)}, u32[]{:S(2)}, u32[]{:S(2)}) collective-permute-start(bf16[2,8,144,128]{3,2,1,0:T(8,128)(2,1)} %shard_map.84.refs_1_), channel_id=1, source_target_pairs={{0,8},{8,0},{1,9},{9,1},{2,10},{10,2},{3,11},{11,3},{4,12},{12,4},... | collective-permute-start | bytes 1769480 | tf_op jit(solution)/shard_map/ppermute | solution.py:43
  107.6 1.8 %collective-permute-done.9.refs_2_ = bf16[2,8,144,128]{3,2,1,0:T(8,128)(2,1)S(1)} collective-permute-done((bf16[2,8,144,128]{3,2,1,0:T(8,128)(2,1)}, bf16[2,8,144,128]{3,2,1,0:T(8,128)(2,1)S(1)}, u32[]{:S(2)}, u32[]{:S(2)}) %collective-permute-start.9) | collective-permute-done | bytes 589856 | tf_op jit(solution)/shard_map/ppermute | solution.py:43
  109.5 0.9 copy-done.14
  110.3 8.6 %shard_map.85 = (bf16[800,128]{1,0:T(8,128)(2,1)}, bf16[800,128]{1,0:T(8,128)(2,1)}, bf16[800,128]{1,0:T(8,128)(2,1)}, bf16[800,128]{1,0:T(8,128)(2,1)}, bf16[40...) custom-call(s32[4]{0:T(128)} %pad_add_fusion.refs_0_, ...), custom_call_target="tpu_custom_call" | custom-call | flops 1024 | bytes 1024 | tf_op jit(solution)/shard_map/pallas_call | solution.py:83
  119.0 0.1 collective-permute-start.14
  119.1 0.1 collective-permute-start.10
  119.2 2.7 %collective-permute-start.11 = (bf16[400,128]{1,0:T(8,128)(2,1)}, bf16[400,128]{1,0:T(8,128)(2,1)S(1)}, u32[]{:S(2)}, u32[]{:S(2)}) collective-permute-start(bf16[400,128]{1,0:T(8,128)(2,1)} %get-tuple-element.45), channel_id=1, source_target_pairs={{0,112},{16,0},{32,16},{48,32},{64,48},{80,64},{96,80},{112,96},{1... | collective-permute-start | bytes 307208 | tf_op jit(solution)/shard_map/ppermute | solution.py:373
  121.8 2.3 %collective-permute-start.15 = (bf16[800,128]{1,0:T(8,128)(2,1)}, bf16[800,128]{1,0:T(8,128)(2,1)S(1)}, u32[]{:S(2)}, u32[]{:S(2)}) collective-permute-start(bf16[800,128]{1,0:T(8,128)(2,1)} %get-tuple-element.49), channel_id=1, source_target_pairs={{0,96},{16,112},{32,0},{48,16},{64,32},{80,48},{96,64},{112,80},{1... | collective-permute-start | bytes 614408 | tf_op jit(solution)/shard_map/ppermute | solution.py:373
  124.1 0.0 collective-permute-start.16
  124.1 8.6 %collective-permute-done.10.refs_2_ = bf16[400,128]{1,0:T(8,128)(2,1)S(1)} collective-permute-done((bf16[400,128]{1,0:T(8,128)(2,1)}, bf16[400,128]{1,0:T(8,128)(2,1)S(1)}, u32[]{:S(2)}, u32[]{:S(2)}) %collective-permute-start.10) | collective-permute-done | bytes 102432 | tf_op jit(solution)/shard_map/ppermute | solution.py:373
  132.7 0.0 collective-permute-start.17
  132.7 0.0 collective-permute-done.11.refs_3_
  132.7 0.9 copy-done.3
  133.7 0.9 copy-done.4
  134.6 0.1 shard_map.86
  134.7 0.5 collective-permute-start.12
  135.1 0.0 collective-permute-done.14.refs_3_
  135.1 4.1 %collective-permute-start.13 = (bf16[800,128]{1,0:T(8,128)(2,1)S(1)}, bf16[800,128]{1,0:T(8,128)(2,1)S(1)}, u32[]{:S(2)}, u32[]{:S(2)}) collective-permute-start(bf16[800,128]{1,0:T(8,128)(2,1)S(1)} %get-tuple-element.47), channel_id=1, source_target_pairs={{0,80},{16,96},{32,112},{48,0},{64,16},{80,32},{96,48},{112,64},{1... | collective-permute-start | bytes 614408 | tf_op jit(solution)/shard_map/ppermute | solution.py:373
  139.2 0.0 collective-permute-done.15.refs_4_
  139.2 0.0 collective-permute-done.16.refs_5_
  139.2 0.0 collective-permute-done.17.refs_6_
  139.2 12.6 %collective-permute-done.12.refs_1_ = bf16[800,128]{1,0:T(8,128)(2,1)S(1)} collective-permute-done((bf16[800,128]{1,0:T(8,128)(2,1)S(1)}, bf16[800,128]{1,0:T(8,128)(2,1)S(1)}, u32[]{:S(2)}, u32[]{:S(2)}) %collective-permute-start.12) | collective-permute-done | bytes 204832 | tf_op jit(solution)/shard_map/ppermute | solution.py:373
  151.8 0.0 collective-permute-done.13.refs_2_
  151.8 0.9 copy-done.5
  152.8 1.0 shard_map.87
  (27 shorter events, 0.0 us)
Async XLA Ops:
  7.1 16.1 %collective-permute-start = (bf16[256,512]{1,0:T(8,128)(2,1)}, bf16[256,512]{1,0:T(8,128)(2,1)S(1)}, u32[]{:S(2)}, u32[]{:S(2)}) collective-permute-start(bf16[256,512]{1,0:T(8,128)(2,1)} %get-tuple-element.31.refs_3_), channel_id=1, source_target_pairs={{0,128},{128,0},{1,129},{129,1},{2,130},{130,2},{3,131},{131,3},{4... | collective-permute-start | bytes 786440 | tf_op jit(solution)/shard_map/ppermute | solution.py:43
  9.2 14.0 %all-to-all-start = ((bf16[8,32,512]{2,1,0:T(8,128)(2,1)}), bf16[8,32,512]{2,1,0:T(8,128)(2,1)S(1)}, u32[]{:S(2)}, u32[]{:S(2)}) async-start(bf16[8,32,512]{2,1,0:T(8,128)(2,1)} %bitcast.13), calls=%async_computation | async-start | bytes 524288 | tf_op jit(solution)/shard_map/all_to_all | solution.py:47
  23.2 0.7 copy-start.13
  23.2 0.8 copy-start.1
  24.0 10.2 %copy-start = (bf16[256,512]{1,0:T(8,128)(2,1)S(1)}, bf16[256,512]{1,0:T(8,128)(2,1)}, u32[]{:S(2)}) copy-start(bf16[256,512]{1,0:T(8,128)(2,1)} %get-tuple-element.31.refs_3_) | copy-start | bytes 786436
  24.0 19.6 %copy-start.6 = (s32[4]{0:T(128)S(1)}, s32[4]{0:T(128)}, u32[]{:S(2)}) copy-start(s32[4]{0:T(128)} %pad_add_fusion.refs_0_) | copy-start | bytes 52
  25.9 11.3 %copy-start.2 = (bf16[256,512]{1,0:T(8,128)(2,1)S(1)}, bf16[256,512]{1,0:T(8,128)(2,1)}, u32[]{:S(2)}) copy-start(bf16[256,512]{1,0:T(8,128)(2,1)} %copy-done.1) | copy-start | bytes 786436
  25.9 28.2 %collective-permute-start.7 = (bf16[512,1024]{1,0:T(8,128)(2,1)}, bf16[512,1024]{1,0:T(8,128)(2,1)}, u32[]{:S(2)}, u32[]{:S(2)}) collective-permute-start(bf16[512,1024]{1,0:T(8,128)(2,1)} %get-tuple-element.38), channel_id=1, source_target_pairs={{0,128},{128,0},{1,129},{129,1},{2,130},{130,2},{3,131},{131,3},{4... | collective-permute-start | bytes 3145736 | tf_op jit(solution)/shard_map/ppermute | solution.py:43
  26.0 17.6 %all-to-all-start.1 = ((bf16[8,32,512]{2,1,0:T(8,128)(2,1)}), bf16[8,32,512]{2,1,0:T(8,128)(2,1)S(1)}, u32[]{:S(2)}, u32[]{:S(2)}) async-start(bf16[8,32,512]{2,1,0:T(8,128)(2,1)} %get-tuple-element.36), calls=%async_computation.1 | async-start | bytes 524288 | tf_op jit(solution)/shard_map/all_to_all | solution.py:47
  34.2 4.1 %collective-permute-start.4 = (bf16[256,512]{1,0:T(8,128)(2,1)S(1)}, bf16[256,512]{1,0:T(8,128)(2,1)S(1)}, u32[]{:S(2)}, u32[]{:S(2)}) collective-permute-start(bf16[256,512]{1,0:T(8,128)(2,1)S(1)} %copy-done), channel_id=1, source_target_pairs={{0,8},{8,0},{1,9},{9,1},{2,10},{10,2},{3,11},{11,3},{4,12},{12,4},... | collective-permute-start | bytes 786440 | tf_op jit(solution)/shard_map/ppermute | solution.py:43
  37.1 1.5 collective-permute-start.5
  45.3 16.2 %all-to-all-start.2 = ((f32[32,8,128]{2,1,0:T(8,128)}), f32[32,8,128]{2,1,0:T(8,128)S(1)}, u32[]{:S(2)}, u32[]{:S(2)}) async-start(f32[32,8,128]{2,1,0:T(8,128)} %shard_map.80), calls=%async_computation.2 | async-start | bytes 262144 | tf_op jit(solution)/shard_map/all_to_all | solution.py:47
  53.8 26.2 %collective-permute-start.6 = (bf16[512,1024]{1,0:T(8,128)(2,1)}, bf16[512,1024]{1,0:T(8,128)(2,1)S(1)}, u32[]{:S(2)}, u32[]{:S(2)}) collective-permute-start(bf16[512,1024]{1,0:T(8,128)(2,1)} %get-tuple-element.30.refs_1_.refs_6_), channel_id=1, source_target_pairs={{0,8},{8,0},{1,9},{9,1},{2,10},{10,2},{3,11},{11,3},{4,12},{12,4},... | collective-permute-start | bytes 3145736 | tf_op jit(solution)/shard_map/ppermute | solution.py:43
  54.1 32.3 %collective-permute-start.8 = (bf16[512,1024]{1,0:T(8,128)(2,1)}, bf16[512,1024]{1,0:T(8,128)(2,1)S(1)}, u32[]{:S(2)}, u32[]{:S(2)}) collective-permute-start(bf16[512,1024]{1,0:T(8,128)(2,1)} %collective-permute-done.7.refs_8_), channel_id=1, source_target_pairs={{0,8},{8,0},{1,9},{9,1},{2,10},{10,2},{3,11},{11,3},{4,12},{12,4},... | collective-permute-start | bytes 3145736 | tf_op jit(solution)/shard_map/ppermute | solution.py:43
  64.2 22.2 %all-to-all-start.3 = ((bf16[8,272,128]{2,1,0:T(8,128)(2,1)}), bf16[8,272,128]{2,1,0:T(8,128)(2,1)S(1)}, u32[]{:S(2)}, u32[]{:S(2)}) async-start(bf16[8,272,128]{2,1,0:T(8,128)(2,1)} %shard_map.81), calls=%async_computation.3 | async-start | bytes 1114112 | tf_op jit(solution)/shard_map/all_to_all | solution.py:47
  67.8 11.1 %collective-permute-start.2 = (bf16[800,256]{1,0:T(8,128)(2,1)}, bf16[800,256]{1,0:T(8,128)(2,1)S(1)}, u32[]{:S(2)}, u32[]{:S(2)}) collective-permute-start(bf16[800,256]{1,0:T(8,128)(2,1)} %get-tuple-element.35.refs_0_), channel_id=1, source_target_pairs={{0,128},{128,0},{1,129},{129,1},{2,130},{130,2},{3,131},{131,3},{4... | collective-permute-start | bytes 1228808 | tf_op jit(solution)/shard_map/ppermute | solution.py:43
  68.2 11.8 %collective-permute-start.1 = (bf16[800,256]{1,0:T(8,128)(2,1)}, bf16[800,256]{1,0:T(8,128)(2,1)S(1)}, u32[]{:S(2)}, u32[]{:S(2)}) collective-permute-start(bf16[800,256]{1,0:T(8,128)(2,1)} %get-tuple-element.35.refs_0_), channel_id=1, source_target_pairs={{0,8},{8,0},{1,9},{9,1},{2,10},{10,2},{3,11},{11,3},{4,12},{12,4},... | collective-permute-start | bytes 1228808 | tf_op jit(solution)/shard_map/ppermute | solution.py:43
  78.9 1.1 copy-start.15
  78.9 2.4 %collective-permute-start.3 = (bf16[800,256]{1,0:T(8,128)(2,1)S(1)}, bf16[800,256]{1,0:T(8,128)(2,1)S(1)}, u32[]{:S(2)}, u32[]{:S(2)}) collective-permute-start(bf16[800,256]{1,0:T(8,128)(2,1)S(1)} %collective-permute-done.2.refs_2_), channel_id=1, source_target_pairs={{0,8},{8,0},{1,9},{9,1},{2,10},{10,2},{3,11},{11,3},{4,12},{12,4},... | collective-permute-start | bytes 1228808 | tf_op jit(solution)/shard_map/ppermute | solution.py:43
  80.0 6.5 %copy-start.11 = (bf16[800,256]{1,0:T(8,128)(2,1)}, bf16[800,256]{1,0:T(8,128)(2,1)S(1)}, u32[]{:S(2)}) copy-start(bf16[800,256]{1,0:T(8,128)(2,1)S(1)} %collective-permute-done.1.refs_8_.refs_1_) | copy-start | bytes 1228804
  80.0 6.5 %copy-start.8 = (bf16[512,1024]{1,0:T(8,128)(2,1)}, bf16[512,1024]{1,0:T(8,128)(2,1)S(1)}, u32[]{:S(2)}) copy-start(bf16[512,1024]{1,0:T(8,128)(2,1)S(1)} %collective-permute-done.6.refs_6_.refs_7_) | copy-start | bytes 3145732
  81.3 5.1 %copy-start.12 = (bf16[800,256]{1,0:T(8,128)(2,1)}, bf16[800,256]{1,0:T(8,128)(2,1)S(1)}, u32[]{:S(2)}) copy-start(bf16[800,256]{1,0:T(8,128)(2,1)S(1)} %collective-permute-done.3.refs_9_.refs_3_) | copy-start | bytes 1228804
  86.4 0.8 copy-start.10
  86.4 1.2 copy-start.9
  90.6 14.1 %all-to-all-start.4 = ((bf16[16,144,128]{2,1,0:T(8,128)(2,1)}), bf16[16,144,128]{2,1,0:T(8,128)(2,1)S(1)}, u32[]{:S(2)}, u32[]{:S(2)}) async-start(bf16[16,144,128]{2,1,0:T(8,128)(2,1)} %shard_map.82.refs_4_), calls=%async_computation.4 | async-start | bytes 1179648 | tf_op jit(solution)/shard_map/all_to_all | solution.py:47
  104.6 0.9 copy-start.7
  105.5 3.9 %collective-permute-start.9 = (bf16[2,8,144,128]{3,2,1,0:T(8,128)(2,1)}, bf16[2,8,144,128]{3,2,1,0:T(8,128)(2,1)S(1)}, u32[]{:S(2)}, u32[]{:S(2)}) collective-permute-start(bf16[2,8,144,128]{3,2,1,0:T(8,128)(2,1)} %shard_map.84.refs_1_), channel_id=1, source_target_pairs={{0,8},{8,0},{1,9},{9,1},{2,10},{10,2},{3,11},{11,3},{4,12},{12,4},... | collective-permute-start | bytes 1769480 | tf_op jit(solution)/shard_map/ppermute | solution.py:43
  109.5 0.9 copy-start.14
  119.0 16.2 %collective-permute-start.14 = (bf16[800,128]{1,0:T(8,128)(2,1)}, bf16[800,128]{1,0:T(8,128)(2,1)S(1)}, u32[]{:S(2)}, u32[]{:S(2)}) collective-permute-start(bf16[800,128]{1,0:T(8,128)(2,1)} %get-tuple-element.48), channel_id=1, source_target_pairs={{0,32},{16,48},{32,64},{48,80},{64,96},{80,112},{96,0},{112,16},{1... | collective-permute-start | bytes 614408 | tf_op jit(solution)/shard_map/ppermute | solution.py:373
  119.1 13.6 %collective-permute-start.10 = (bf16[400,128]{1,0:T(8,128)(2,1)}, bf16[400,128]{1,0:T(8,128)(2,1)S(1)}, u32[]{:S(2)}, u32[]{:S(2)}) collective-permute-start(bf16[400,128]{1,0:T(8,128)(2,1)} %get-tuple-element.44), channel_id=1, source_target_pairs={{0,16},{16,32},{32,48},{48,64},{64,80},{80,96},{96,112},{112,0},{1... | collective-permute-start | bytes 307208 | tf_op jit(solution)/shard_map/ppermute | solution.py:373
  119.2 13.6 %collective-permute-start.11 = (bf16[400,128]{1,0:T(8,128)(2,1)}, bf16[400,128]{1,0:T(8,128)(2,1)S(1)}, u32[]{:S(2)}, u32[]{:S(2)}) collective-permute-start(bf16[400,128]{1,0:T(8,128)(2,1)} %get-tuple-element.45), channel_id=1, source_target_pairs={{0,112},{16,0},{32,16},{48,32},{64,48},{80,64},{96,80},{112,96},{1... | collective-permute-start | bytes 307208 | tf_op jit(solution)/shard_map/ppermute | solution.py:373
  121.8 17.4 %collective-permute-start.15 = (bf16[800,128]{1,0:T(8,128)(2,1)}, bf16[800,128]{1,0:T(8,128)(2,1)S(1)}, u32[]{:S(2)}, u32[]{:S(2)}) collective-permute-start(bf16[800,128]{1,0:T(8,128)(2,1)} %get-tuple-element.49), channel_id=1, source_target_pairs={{0,96},{16,112},{32,0},{48,16},{64,32},{80,48},{96,64},{112,80},{1... | collective-permute-start | bytes 614408 | tf_op jit(solution)/shard_map/ppermute | solution.py:373
  124.1 15.1 %collective-permute-start.16 = (bf16[800,128]{1,0:T(8,128)(2,1)}, bf16[800,128]{1,0:T(8,128)(2,1)S(1)}, u32[]{:S(2)}, u32[]{:S(2)}) collective-permute-start(bf16[800,128]{1,0:T(8,128)(2,1)} %get-tuple-element.50), channel_id=1, source_target_pairs={{0,16},{16,32},{32,48},{48,64},{64,80},{80,96},{96,112},{112,0},{1... | collective-permute-start | bytes 614408 | tf_op jit(solution)/shard_map/ppermute | solution.py:373
  132.7 6.5 %collective-permute-start.17 = (bf16[800,128]{1,0:T(8,128)(2,1)}, bf16[800,128]{1,0:T(8,128)(2,1)S(1)}, u32[]{:S(2)}, u32[]{:S(2)}) collective-permute-start(bf16[800,128]{1,0:T(8,128)(2,1)} %get-tuple-element.51), channel_id=1, source_target_pairs={{0,112},{16,0},{32,16},{48,32},{64,48},{80,64},{96,80},{112,96},{1... | collective-permute-start | bytes 614408 | tf_op jit(solution)/shard_map/ppermute | solution.py:373
  132.7 0.9 copy-start.3
  133.7 0.9 copy-start.4
  134.7 17.2 %collective-permute-start.12 = (bf16[800,128]{1,0:T(8,128)(2,1)S(1)}, bf16[800,128]{1,0:T(8,128)(2,1)S(1)}, u32[]{:S(2)}, u32[]{:S(2)}) collective-permute-start(bf16[800,128]{1,0:T(8,128)(2,1)S(1)} %get-tuple-element.46), channel_id=1, source_target_pairs={{0,48},{16,64},{32,80},{48,96},{64,112},{80,0},{96,16},{112,32},{1... | collective-permute-start | bytes 614408 | tf_op jit(solution)/shard_map/ppermute | solution.py:373
  135.1 16.7 %collective-permute-start.13 = (bf16[800,128]{1,0:T(8,128)(2,1)S(1)}, bf16[800,128]{1,0:T(8,128)(2,1)S(1)}, u32[]{:S(2)}, u32[]{:S(2)}) collective-permute-start(bf16[800,128]{1,0:T(8,128)(2,1)S(1)} %get-tuple-element.47), channel_id=1, source_target_pairs={{0,80},{16,96},{32,112},{48,0},{64,16},{80,32},{96,48},{112,64},{1... | collective-permute-start | bytes 614408 | tf_op jit(solution)/shard_map/ppermute | solution.py:373
  151.8 0.9 copy-start.5
